TPU v7x, 32 devices: a whole 2x2x4 slice. The times are simulated.
32 devices in a mesh: seq: 16 (over z, y, x), head: 2 (over core).
Axes of the slice: x: 2, y: 2, z: 4, core: 2. Of those that a mesh axis runs over, the one named last changes fastest.
Arguments:
- queries: bfloat16 [4096, 5120], P('seq', 'head'), may hold values from -12 to 12
- keys: bfloat16 [4096, 5120], P('seq', 'head'), may hold values from -4.5 to 4.5
- values: bfloat16 [4096, 5120], P('seq', 'head'), may hold values from -6 to 6
- class_map: int32 [40, 32, 8, 2], P('head', 'seq'), may hold values from 0 to 2, as said below
- out_weight: bfloat16 [5120, 5120], P('seq', 'head'), may hold values from -0.5 to 0.5
Outputs:
- mixed: bfloat16 [4096, 5120], P(('seq', 'head'))
Inputs may be any that keep to these rules, and one draw needn't show every extreme that they name: `class_map`: entry [h, b, r, j] classes, for head h, the pair of query block b and key block j of the token shard r places before block b's shard, counted cyclically (0 skipped, 1 linear, 2 exact softmax). Every query block's own key block (r = 0, j = b mod 2) is 2.
All inputs are finite; a program needn't handle non-finite values.
Results may differ from a plain program's by a relative error of at most 0.0061.
Values may be sent and summed in bfloat16 or wider, within the bound.
No kernel may reach another device: no remote copies, remote signals or barrier semaphores. Data moves between devices by JAX's collectives and lax.ppermute only.
A program may use at most 256 MiB of HBM per device.

v0:
```python
import math

import jax
import jax.numpy as jnp
from jax import lax
from jax.sharding import PartitionSpec as P

HD = 128
CYCLE = 8


def passed_along(value, axis, steps):
    count = lax.axis_size(axis)
    pairs = [(source, (source + steps) % count) for source in range(count)]
    return lax.ppermute(value, axis, pairs)


def feature_map(numbers):
    return (jax.nn.elu(numbers.astype(jnp.float32)) + 1.0).astype(jnp.bfloat16)


def token_classes(block_row, tok_rows, key_rows):
    heads_here, query_blocks, key_blocks = block_row.shape
    query_width = tok_rows // query_blocks
    key_width = key_rows // key_blocks
    widened = jnp.broadcast_to(
        block_row[:, :, None, :, None],
        (heads_here, query_blocks, query_width, key_blocks, key_width),
    )
    return widened.reshape(heads_here, tok_rows, key_rows)


def local(queries, keys, values, class_map, out_weight):
    tok_rows = queries.shape[0]
    heads_here = queries.shape[1] // HD
    stacked = jnp.stack([keys, values])
    arrivals = [stacked]
    current = stacked
    for cycle_step in range(1, CYCLE):
        current = passed_along(current, "seq", 1)
        arrivals.append(current)
    window = jnp.concatenate(arrivals, axis=1)
    key_rows = window.shape[1]
    query_heads = queries.reshape(tok_rows, heads_here, HD)
    key_heads = window[0].reshape(key_rows, heads_here, HD)
    value_heads = window[1].reshape(key_rows, heads_here, HD)
    block_count = class_map.shape[1]
    classes = token_classes(class_map.reshape(heads_here, block_count, -1), tok_rows, key_rows)
    scores = jnp.einsum(
        "thd,uhd->htu", query_heads, key_heads, preferred_element_type=jnp.float32
    ) * (1.0 / math.sqrt(HD))
    masked = jnp.where(classes == 2, scores, -jnp.inf)
    row_max = jnp.max(masked, axis=2, keepdims=True)
    weights_exact = jnp.exp(masked - row_max)
    exact_total = jnp.sum(weights_exact, axis=2, keepdims=True)
    exact_out = (
        jnp.einsum(
            "htu,uhd->htd",
            weights_exact.astype(jnp.bfloat16),
            value_heads,
            preferred_element_type=jnp.float32,
        )
        / exact_total
    )
    affinity = jnp.einsum(
        "thd,uhd->htu",
        feature_map(query_heads),
        feature_map(key_heads),
        preferred_element_type=jnp.float32,
    )
    affinity = jnp.where(classes == 1, affinity, 0.0)
    linear_total = jnp.maximum(jnp.sum(affinity, axis=2, keepdims=True), 1.0)
    linear_out = (
        jnp.einsum(
            "htu,uhd->htd",
            affinity.astype(jnp.bfloat16),
            value_heads,
            preferred_element_type=jnp.float32,
        )
        / linear_total
    )
    attended = (
        (exact_out + linear_out)
        .transpose(1, 0, 2)
        .reshape(tok_rows, heads_here * HD)
        .astype(jnp.bfloat16)
    )
    contract_last = (((1,), (1,)), ((), ()))
    partial_rows = lax.dot_general(
        attended,
        lax.all_gather(out_weight, "seq", axis=0, tiled=True),
        contract_last,
        preferred_element_type=jnp.float32,
    )
    mixed = lax.psum_scatter(
        partial_rows.astype(jnp.bfloat16), "head", scatter_dimension=0, tiled=True
    )
    return mixed


def solution(mesh):
    placed = (
        P("seq", "head"),
        P("seq", "head"),
        P("seq", "head"),
        P("head", "seq", None, None),
        P("seq", "head"),
    )
    return jax.shard_map(
        local, mesh=mesh, in_specs=placed, out_specs=P(("seq", "head"), None), check_vma=False
    )
```

profile of v0, /device:TPU:0, one launch (start us, length us, event | category | flops | bytes accessed | tf_op | source)
XLA Modules:
  0.0 875.1 jit_solution(4996188301740760790)
XLA Ops:
  6.5 0.0 copy-start.9
  6.5 0.0 all-gather.2.cloned.1.call-start
  6.5 0.7 all-gather.2.cloned.1.call-update
  7.3 0.0 reduce-scatter.2.cloned.1.call-start
  7.3 1.6 copy.13
  8.9 1.6 copy.14
  10.5 1.9 pad_maximum_fusion
  12.4 2.9 collective-permute-start
  15.4 100.5 %collective-permute-done = bf16[2,256,2560]{1,2,0:T(8,128)(2,1)S(1)} collective-permute-done((bf16[2,256,2560]{1,2,0:T(8,128)(2,1)S(1)}, bf16[2,256,2560]{1,2,0:T(8,128)(2,1)S(1)}, u32[]{:S(2)}, u32[]{:S(2)}) %collective-permute-start) | collective-permute-done | bytes 2621472 | tf_op jit(solution)/shard_map/ppermute | solution.py:15
  115.8 1.5 copy-done
  117.3 0.0 collective-permute-start.1
  117.3 118.3 %collective-permute-done.1 = bf16[2,256,2560]{1,2,0:T(8,128)(2,1)S(1)} collective-permute-done((bf16[2,256,2560]{1,2,0:T(8,128)(2,1)S(1)}, bf16[2,256,2560]{1,2,0:T(8,128)(2,1)S(1)}, u32[]{:S(2)}, u32[]{:S(2)}) %collective-permute-start.1) | collective-permute-done | bytes 2621472 | tf_op jit(solution)/shard_map/ppermute | solution.py:15
  235.7 0.0 copy-start.1
  235.7 1.5 copy-done.1
  237.2 0.0 collective-permute-start.2
  237.2 115.6 %collective-permute-done.2 = bf16[2,256,2560]{1,2,0:T(8,128)(2,1)S(1)} collective-permute-done((bf16[2,256,2560]{1,2,0:T(8,128)(2,1)S(1)}, bf16[2,256,2560]{1,2,0:T(8,128)(2,1)S(1)}, u32[]{:S(2)}, u32[]{:S(2)}) %collective-permute-start.2) | collective-permute-done | bytes 2621472 | tf_op jit(solution)/shard_map/ppermute | solution.py:15
  352.8 0.0 copy-start.2
  352.8 1.6 copy-done.2
  354.4 0.0 collective-permute-start.3
  354.4 116.9 %collective-permute-done.3 = bf16[2,256,2560]{1,2,0:T(8,128)(2,1)S(1)} collective-permute-done((bf16[2,256,2560]{1,2,0:T(8,128)(2,1)S(1)}, bf16[2,256,2560]{1,2,0:T(8,128)(2,1)S(1)}, u32[]{:S(2)}, u32[]{:S(2)}) %collective-permute-start.3) | collective-permute-done | bytes 2621472 | tf_op jit(solution)/shard_map/ppermute | solution.py:15
  471.3 0.0 copy-start.4
  471.3 1.5 copy-done.4
  472.8 0.0 collective-permute-start.4
  472.8 76.5 %collective-permute-done.4 = bf16[2,256,2560]{1,2,0:T(8,128)(2,1)S(1)} collective-permute-done((bf16[2,256,2560]{1,2,0:T(8,128)(2,1)S(1)}, bf16[2,256,2560]{1,2,0:T(8,128)(2,1)S(1)}, u32[]{:S(2)}, u32[]{:S(2)}) %collective-permute-start.4) | collective-permute-done | bytes 2621472 | tf_op jit(solution)/shard_map/ppermute | solution.py:15
  549.3 0.0 copy-start.6
  549.3 1.5 copy-done.6
  550.8 0.0 collective-permute-start.5
  550.8 57.7 %collective-permute-done.5 = bf16[2,256,2560]{1,2,0:T(8,128)(2,1)} collective-permute-done((bf16[2,256,2560]{1,2,0:T(8,128)(2,1)S(1)}, bf16[2,256,2560]{1,2,0:T(8,128)(2,1)}, u32[]{:S(2)}, u32[]{:S(2)}) %collective-permute-start.5) | collective-permute-done | bytes 2621472 | tf_op jit(solution)/shard_map/ppermute | solution.py:15
  608.5 0.0 collective-permute-start.6
  608.5 0.0 copy-done.9
  608.6 0.1 copy.12
  608.7 4.6 broadcast_in_dim.23
  613.2 28.2 %eq.29 = pred[20,256,2048]{2,1,0:T(32,128)(4,1)} reshape(pred[20,2,128,16,128]{4,3,2,1,0:T(8,128)(4,1)} %broadcast_in_dim.23) | data formatting | bytes 20971520 | tf_op jit(solution)/shard_map/eq | solution.py:52
  641.4 15.7 %copy.18 = pred[20,256,2048]{1,2,0:T(32,128)(4,1)} copy(pred[20,256,2048]{2,1,0:T(32,128)(4,1)} %eq.29) | data formatting | bytes 20971520 | tf_op jit(solution)/shard_map/eq | solution.py:52
  657.2 0.0 copy-done.8
  657.2 0.6 copy.15
  657.8 0.1 copy.20
  657.9 4.6 broadcast_in_dim.25
  662.5 28.2 %eq.33 = pred[20,256,2048]{2,1,0:T(32,128)(4,1)} reshape(pred[20,2,128,16,128]{4,3,2,1,0:T(8,128)(4,1)} %broadcast_in_dim.25) | data formatting | bytes 20971520 | tf_op jit(solution)/shard_map/eq | solution.py:71
  690.7 0.0 copy-start.3
  690.7 3.6 constant_dynamic-update-slice_fusion.6
  694.3 3.9 constant_dynamic-update-slice_fusion.5
  698.2 0.0 copy-done.3
  698.2 1.7 constant_dynamic-update-slice_fusion.4
  699.9 0.0 copy-done.5
  699.9 1.7 constant_dynamic-update-slice_fusion.3
  701.6 0.0 copy-done.7
  701.6 1.7 constant_dynamic-update-slice_fusion.2
  703.3 3.4 constant_dynamic-update-slice_fusion.1
  706.8 0.0 collective-permute-done.6
  706.8 3.5 constant_dynamic-update-slice_fusion
  710.3 18.1 %fusion.27 = (bf16[1,2048,2560]{1,2,0:T(8,128)(2,1)}, bf16[1,2048,2560]{1,2,0:T(8,128)(2,1)}) fusion(bf16[2,2048,2560]{1,2,0:T(8,128)(2,1)} %constant_dynamic-update-slice_fusion), kind=kLoop, calls=%fused_computation.47 | loop fusion | bytes 41943040 | tf_op jit(solution)/shard_map/slice | solution.py:45
  728.4 33.9 %select_reduce_fusion = (f32[20,256]{1,0:T(8,128)S(1)}, bf16[20,256,2048]{2,1,0:T(8,128)(2,1)}) fusion(pred[20,256,2048]{2,1,0:T(32,128)(4,1)} %eq.33, bf16[2048,20,128]{0,2,1:T(8,128)(2,1)} %bitcast.44, bf16[256,20,128]{0,2,1:T(8,128)(2,1)S(1)} %bitcast.50), kind=kOutput, calls=%fused_computation.6 | convolution fusion | flops 2751196160 | bytes 43274240 | tf_op jit(solution)/shard_map/thd,uhd->htu/dot_general | solution.py:65
  762.2 0.0 slice-done
  762.2 0.0 slice-done.1
  762.2 0.0 slice-done.2
  762.3 21.7 %fusion.2 = (f32[20,256]{1,0:T(8,128)S(1)}, f32[20,2048,256]{2,1,0:T(8,128)}) fusion(pred[20,256,2048]{1,2,0:T(32,128)(4,1)S(1)} %bitcast.43, bf16[2048,20,128]{0,2,1:T(8,128)(2,1)} %bitcast.45, bf16[256,20,128]{0,2,1:T(8,128)(2,1)S(1)} %bitcast.51), kind=kOutput, calls=%fused_computation.8 | convolution fusion | flops 2715806720 | bytes 64245760 | tf_op jit(solution)/shard_map/thd,uhd->htu/dot_general | solution.py:49
  783.9 14.4 %fusion = f32[20,256]{1,0:T(8,128)S(1)} fusion(pred[20,256,2048]{1,2,0:T(32,128)(4,1)S(1)} %bitcast.43, f32[20,2048,256]{2,1,0:T(8,128)} %get-tuple-element.12, f32[20,256]{1,0:T(8,128)S(1)} %get-tuple-element.11), kind=kLoop, calls=%fused_computation.4 | loop fusion | flops 41937920 | bytes 52469760 | tf_op jit(solution)/shard_map/reduce_sum | solution.py:55
  798.3 21.1 %fusion.8 = f32[20,256,128]{1,2,0:T(8,128)} fusion(bf16[2048,20,128]{0,2,1:T(8,128)(2,1)} %bitcast.46, pred[20,256,2048]{1,2,0:T(32,128)(4,1)S(1)} %bitcast.43, f32[20,2048,256]{2,1,0:T(8,128)} %get-tuple-element.12, f32[20,256]{1,0:T(8,128)S(1)} %get-tuple-element.11), kind=kOutput, calls=%fused_computation.14 | convolution fusion | flops 2726297600 | bytes 65556480 | tf_op jit(solution)/shard_map/htu,uhd->htd/dot_general | solution.py:57
  819.4 16.5 %fusion.18 = bf16[256,20,128]{0,2,1:T(8,128)(2,1)S(1)} fusion(f32[20,256,128]{1,2,0:T(8,128)} %fusion.8, bf16[2048,20,128]{0,2,1:T(8,128)(2,1)} %bitcast.47, pred[20,256,2048]{2,1,0:T(32,128)(4,1)} %eq.33, bf16[20,256,2048]{2,1,0:T(8,128)(2,1)} %get-tuple-element.14, f32[256,20]{0,1:T(8,128)S(1)} %maximum_bitcast_fusion, f32[256,20]{0,1:T(8,128)S(1)} %bitcast.52), kind=kOutput, calls=%fused_computation.27 | convolution fusion | flops 2697461760 | bytes 45916160 | tf_op jit(solution)/shard_map/htu,uhd->htd/dot_general | solution.py:74
  836.0 0.0 all-gather.2.cloned.1.call-done
  836.0 14.2 %convolution_convert_fusion = bf16[256,5120]{1,0:T(8,128)(2,1)} fusion(bf16[256,2560]{0,1:T(8,128)(2,1)S(1)} %bitcast.53, bf16[5120,2560]{1,0:T(8,128)(2,1)} %all-gather.2.cloned.1.call-done), kind=kOutput, calls=%fused_computation.20 | convolution fusion | flops 6712197120 | bytes 30146560 | tf_op jit(solution)/shard_map/dot_general | solution.py:89
  850.2 0.0 reduce-scatter.2.cloned.1.call-update
  850.2 18.0 %reduce-scatter.2.cloned.1.call-done = bf16[128,5120]{1,0:T(8,128)(2,1)} async-done(((bf16[256,5120]{1,0:T(8,128)(2,1)}), bf16[128,5120]{1,0:T(8,128)(2,1)}) %reduce-scatter.2.cloned.1.call-update) | async-done | bytes 1310736 | tf_op jit(solution)/shard_map/reduce_scatter | solution.py:95
  (12 shorter events, 0.1 us)
Async XLA Ops:
  6.5 602.0 %copy-start.9 = (s32[20,2,8,2]{0,3,2,1:T(2,128)S(1)}, s32[20,2,8,2]{0,3,2,1:T(2,128)}, u32[]{:S(2)}) copy-start(s32[20,2,8,2]{0,3,2,1:T(2,128)} %param.8) | copy-start | bytes 7684
  6.5 829.4 %all-gather.2.cloned.1.call-start = ((), (), s32[]{:S(2)}) async-start(), calls=%async_computation.1 | async-start | bytes 27852800 | tf_op jit(solution)/shard_map/all_gather | solution.py:91
  7.3 861.0 %reduce-scatter.2.cloned.1.call-start = ((), (), s32[]{:S(2)}) async-start(), calls=%async_computation.2 | async-start | bytes 3932160 | tf_op jit(solution)/shard_map/reduce_scatter | solution.py:95
  12.4 103.4 %collective-permute-start = (bf16[2,256,2560]{1,2,0:T(8,128)(2,1)S(1)}, bf16[2,256,2560]{1,2,0:T(8,128)(2,1)S(1)}, u32[]{:S(2)}, u32[]{:S(2)}) collective-permute-start(bf16[2,256,2560]{1,2,0:T(8,128)(2,1)S(1)} %get-tuple-element.7), channel_id=1, source_target_pairs={{0,2},{2,4},{4,6},{6,8},{8,10},{10,12},{12,14},{14,16},{16,18},{18... | collective-permute-start | bytes 7864328 | tf_op jit(solution)/shard_map/ppermute | solution.py:15
  115.8 1.5 copy-start
  117.3 118.3 %collective-permute-start.1 = (bf16[2,256,2560]{1,2,0:T(8,128)(2,1)S(1)}, bf16[2,256,2560]{1,2,0:T(8,128)(2,1)S(1)}, u32[]{:S(2)}, u32[]{:S(2)}) collective-permute-start(bf16[2,256,2560]{1,2,0:T(8,128)(2,1)S(1)} %collective-permute-done), channel_id=1, source_target_pairs={{0,2},{2,4},{4,6},{6,8},{8,10},{10,12},{12,14},{14,16},{16,18},{18... | collective-permute-start | bytes 7864328 | tf_op jit(solution)/shard_map/ppermute | solution.py:15
  235.7 1.5 copy-start.1
  237.2 115.6 %collective-permute-start.2 = (bf16[2,256,2560]{1,2,0:T(8,128)(2,1)S(1)}, bf16[2,256,2560]{1,2,0:T(8,128)(2,1)S(1)}, u32[]{:S(2)}, u32[]{:S(2)}) collective-permute-start(bf16[2,256,2560]{1,2,0:T(8,128)(2,1)S(1)} %collective-permute-done.1), channel_id=1, source_target_pairs={{0,2},{2,4},{4,6},{6,8},{8,10},{10,12},{12,14},{14,16},{16,18},{18... | collective-permute-start | bytes 7864328 | tf_op jit(solution)/shard_map/ppermute | solution.py:15
  352.8 1.6 copy-start.2
  354.4 116.9 %collective-permute-start.3 = (bf16[2,256,2560]{1,2,0:T(8,128)(2,1)S(1)}, bf16[2,256,2560]{1,2,0:T(8,128)(2,1)S(1)}, u32[]{:S(2)}, u32[]{:S(2)}) collective-permute-start(bf16[2,256,2560]{1,2,0:T(8,128)(2,1)S(1)} %collective-permute-done.2), channel_id=1, source_target_pairs={{0,2},{2,4},{4,6},{6,8},{8,10},{10,12},{12,14},{14,16},{16,18},{18... | collective-permute-start | bytes 7864328 | tf_op jit(solution)/shard_map/ppermute | solution.py:15
  471.3 1.5 copy-start.4
  472.8 76.5 %collective-permute-start.4 = (bf16[2,256,2560]{1,2,0:T(8,128)(2,1)S(1)}, bf16[2,256,2560]{1,2,0:T(8,128)(2,1)S(1)}, u32[]{:S(2)}, u32[]{:S(2)}) collective-permute-start(bf16[2,256,2560]{1,2,0:T(8,128)(2,1)S(1)} %collective-permute-done.3), channel_id=1, source_target_pairs={{0,2},{2,4},{4,6},{6,8},{8,10},{10,12},{12,14},{14,16},{16,18},{18... | collective-permute-start | bytes 7864328 | tf_op jit(solution)/shard_map/ppermute | solution.py:15
  549.3 1.5 copy-start.6
  550.8 57.7 %collective-permute-start.5 = (bf16[2,256,2560]{1,2,0:T(8,128)(2,1)S(1)}, bf16[2,256,2560]{1,2,0:T(8,128)(2,1)}, u32[]{:S(2)}, u32[]{:S(2)}) collective-permute-start(bf16[2,256,2560]{1,2,0:T(8,128)(2,1)S(1)} %collective-permute-done.4), channel_id=1, source_target_pairs={{0,2},{2,4},{4,6},{6,8},{8,10},{10,12},{12,14},{14,16},{16,18},{18... | collective-permute-start | bytes 7864328 | tf_op jit(solution)/shard_map/ppermute | solution.py:15
  608.5 98.3 %collective-permute-start.6 = (bf16[2,256,2560]{1,2,0:T(8,128)(2,1)}, bf16[2,256,2560]{1,2,0:T(8,128)(2,1)}, u32[]{:S(2)}, u32[]{:S(2)}) collective-permute-start(bf16[2,256,2560]{1,2,0:T(8,128)(2,1)} %collective-permute-done.5), channel_id=1, source_target_pairs={{0,2},{2,4},{4,6},{6,8},{8,10},{10,12},{12,14},{14,16},{16,18},{18... | collective-permute-start | bytes 7864328 | tf_op jit(solution)/shard_map/ppermute | solution.py:15
  641.4 15.7 %copy-start.8 = (bf16[256,2560]{1,0:T(8,128)(2,1)S(1)}, bf16[256,2560]{1,0:T(8,128)(2,1)}, u32[]{:S(2)}) copy-start(bf16[256,2560]{1,0:T(8,128)(2,1)} %param.5) | copy-start | bytes 3932164
  690.7 7.5 copy-start.3
  690.7 9.2 %copy-start.5 = (bf16[2,256,2560]{1,2,0:T(8,128)(2,1)S(1)}, bf16[2,256,2560]{1,2,0:T(8,128)(2,1)}, u32[]{:S(2)}) copy-start(bf16[2,256,2560]{1,2,0:T(8,128)(2,1)} %copy-done.4) | copy-start | bytes 7864324
  690.7 10.9 %copy-start.7 = (bf16[2,256,2560]{1,2,0:T(8,128)(2,1)S(1)}, bf16[2,256,2560]{1,2,0:T(8,128)(2,1)}, u32[]{:S(2)}) copy-start(bf16[2,256,2560]{1,2,0:T(8,128)(2,1)} %copy-done.6) | copy-start | bytes 7864324
  710.3 51.9 %slice-start = ((s8[10485760]{0:T(1024)(128)(4,1)}), s8[4194304]{0:T(1024)(128)(4,1)S(1)}, s32[]{:S(2)}) async-start(s8[10485760]{0:T(1024)(128)(4,1)} %bitcast.42), calls=%async_computation.3 | async-start | bytes 8388608
  710.3 51.9 %slice-start.1 = ((s8[10485760]{0:T(1024)(128)(4,1)}), s8[4194304]{0:T(1024)(128)(4,1)S(1)}, s32[]{:S(2)}) async-start(s8[10485760]{0:T(1024)(128)(4,1)} %bitcast.42), calls=%async_computation.4 | async-start | bytes 8388608
  728.4 33.9 %slice-start.2 = ((s8[10485760]{0:T(1024)(128)(4,1)}), s8[2097152]{0:T(1024)(128)(4,1)S(1)}, s32[]{:S(2)}) async-start(s8[10485760]{0:T(1024)(128)(4,1)} %bitcast.42), calls=%async_computation.5 | async-start | bytes 4194304
Sparse Core Ops, SparseCore 0:
  10.1 465.3 all-gather.1
  850.4 17.8 reduce-scatter.1
where the time goes:
time: 877 us; the launch traced here: 875 us
  waiting for transfers between devices  604 us (69%)
  local copies, waits for them, and re-layouts  131 us (15%)
  matrix products  107 us (12%)
  other arithmetic  16.3 us (2%)
  between operations  13.5 us (2%)
    ppermute x7, waiting for transfers between devices, passed_along(): return lax.ppermute(value, axis, pairs)  586 us
    eq x4, local copies, waits for them, and re-layouts, local(): masked = jnp.where(classes == 2, scores, -jnp.inf)  44.1 us
    dot_general x1, matrix products, local(): jnp.einsum('thd,uhd->htu', feature_map(query_heads), feature_map(key_head...  33.9 us
    eq x3, local copies, waits for them, and re-layouts, local(): affinity = jnp.where(classes == 1, affinity, 0.0)  28.4 us
    unnamed x35, local copies, waits for them, and re-layouts  27.5 us
    dot_general x1, matrix products, local(): jnp.einsum('thd,uhd->htu', query_heads, key_heads, preferred_element_type...  21.7 us
    dot_general x1, matrix products, local(): jnp.einsum('htu,uhd->htd', weights_exact.astype(jnp.bfloat16), value_head...  21.1 us
    slice x1, local copies, waits for them, and re-layouts, local(): key_heads = window[0].reshape(key_rows, heads_here, HD)  18.1 us
  transfers between devices with their start and end apart: 9, of which 7 were waited for; matrix products, arithmetic and copies ran while one was open for 27% of the time, Pallas kernels for 0%

commit v1 on v0

v1 whole, which is shorter than its diff:
```python
import functools
import math

import jax
import jax.numpy as jnp
from jax import lax
from jax.experimental import pallas as pl
from jax.experimental.pallas import tpu as pltpu
from jax.sharding import PartitionSpec as P

HD = 128
CYCLE = 8
BLOCK = 128
LINE = 4
PLANE = 4
CHUNKS = (2, 3)
MASKED = -1e30


def feature_map(numbers):
    x = numbers.astype(jnp.float32)
    return jnp.where(x > 0, x + 1.0, jnp.exp(jnp.minimum(x, 0.0))).astype(jnp.bfloat16)


def passed_along(value, axis, steps):
    count = lax.axis_size(axis)
    pairs = [(source, (source + steps) % count) for source in range(count)]
    return lax.ppermute(value, axis, pairs)


def token_classes(block_row, tok_rows, key_rows):
    heads_here, query_blocks, key_blocks = block_row.shape
    query_width = tok_rows // query_blocks
    key_width = key_rows // key_blocks
    widened = jnp.broadcast_to(
        block_row[:, :, None, :, None],
        (heads_here, query_blocks, query_width, key_blocks, key_width),
    )
    return widened.reshape(heads_here, tok_rows, key_rows)


def ring_plan(queries, keys, values, class_map, out_weight):
    tok_rows = queries.shape[0]
    heads_here = queries.shape[1] // HD
    current = jnp.stack([keys, values])
    arrivals = [current]
    for _ in range(1, CYCLE):
        current = passed_along(current, "seq", 1)
        arrivals.append(current)
    window = jnp.concatenate(arrivals, axis=1)
    key_rows = window.shape[1]
    query_heads = queries.reshape(tok_rows, heads_here, HD)
    key_heads = window[0].reshape(key_rows, heads_here, HD)
    value_heads = window[1].reshape(key_rows, heads_here, HD)
    block_count = class_map.shape[1]
    classes = token_classes(class_map.reshape(heads_here, block_count, -1), tok_rows, key_rows)
    scores = jnp.einsum(
        "thd,uhd->htu", query_heads, key_heads, preferred_element_type=jnp.float32
    ) * (1.0 / math.sqrt(HD))
    masked = jnp.where(classes == 2, scores, -jnp.inf)
    row_max = jnp.max(masked, axis=2, keepdims=True)
    probs = jnp.exp(masked - row_max)
    exact_total = jnp.sum(probs, axis=2, keepdims=True)
    apply_values = functools.partial(
        jnp.einsum, "htu,uhd->htd", preferred_element_type=jnp.float32
    )
    exact_out = apply_values(probs.astype(jnp.bfloat16), value_heads) / exact_total
    affinity = jnp.einsum(
        "thd,uhd->htu",
        feature_map(query_heads),
        feature_map(key_heads),
        preferred_element_type=jnp.float32,
    )
    affinity = jnp.where(classes == 1, affinity, 0.0)
    linear_total = jnp.maximum(jnp.sum(affinity, axis=2, keepdims=True), 1.0)
    linear_out = apply_values(affinity.astype(jnp.bfloat16), value_heads) / linear_total
    attended = (
        (exact_out + linear_out)
        .transpose(1, 0, 2)
        .reshape(tok_rows, heads_here * HD)
        .astype(jnp.bfloat16)
    )
    partial_rows = lax.dot_general(
        attended,
        lax.all_gather(out_weight, "seq", axis=0, tiled=True),
        (((1,), (1,)), ((), ())),
        preferred_element_type=jnp.float32,
    )
    return lax.psum_scatter(
        partial_rows.astype(jnp.bfloat16), "head", scatter_dimension=0, tiled=True
    )


def moves(target):
    pairs = []
    for z in range(LINE):
        for j in range(PLANE):
            to = target(z, j)
            if to is not None:
                pairs.append((z * PLANE + j, to[0] * PLANE + to[1]))
    return pairs


PLANES = [[z * PLANE + j for j in range(PLANE)] for z in range(LINE)]
PLANE_SWAP = [moves(lambda z, j, turn=turn: (z, j ^ turn)) for turn in range(PLANE)]
NEXT_PLANE = moves(lambda z, j: ((z + 1) % LINE, j))
SWAP_PAIR = moves(lambda z, j: (z ^ 1, j))
SWAP_MID = moves(lambda z, j: (3 - z, j) if z in (1, 2) else None)
TO_ENDS = moves(lambda z, j: ({1: 0, 2: 3}[z], j) if z in (1, 2) else None)

CONTRACT_LAST = (((1,), (1,)), ((), ()))
CONTRACT_ROWS = (((1,), (0,)), ((), ()))
CONTRACT_FIRST = (((0,), (0,)), ((), ()))
SMEM = pl.BlockSpec(memory_space=pltpu.SMEM)
VMEM = pl.BlockSpec(memory_space=pltpu.VMEM)


def send(value, pairs):
    return lax.ppermute(value, "seq", pairs)


def exchange(value):
    return lax.all_to_all(value, "seq", 0, 0, tiled=True, axis_index_groups=PLANES)


def after(value, *others):
    return lax.optimization_barrier((value,) + others)[0]


def dot(left, right, dims):
    return lax.dot_general(left, right, dims, preferred_element_type=jnp.float32)


def pack_kernel(chunks, group, q_ref, k_ref, v_ref, *outs):
    first = 0
    for count, out in zip(chunks, outs):
        for owner in range(PLANE):
            for h in range(count):
                at = (owner * group + first + h) * HD
                for i, ref in enumerate((q_ref, k_ref, v_ref)):
                    out[owner, h, i] = ref[:, at : at + HD]
        first += count


def pack(chunks, group, queries, keys, values):
    tok = queries.shape[0]
    outs = [jax.ShapeDtypeStruct((PLANE, n, 3, tok, HD), jnp.bfloat16) for n in chunks]
    return pl.pallas_call(
        functools.partial(pack_kernel, chunks, group),
        out_shape=outs,
        in_specs=[VMEM] * 3,
        out_specs=[VMEM] * len(outs),
        compiler_params=pltpu.CompilerParams(vmem_limit_bytes=24 * 1024 * 1024),
        cost_estimate=pl.CostEstimate(
            flops=0, bytes_accessed=4 * 3 * queries.size, transcendentals=0
        ),
    )(queries, keys, values)


def attention_kernel(
    tok, count, own, last, last2, bias_ref, lin_ref, out_ref, q_all, k_all, v_all, s_all
):
    blocks = tok // BLOCK
    window = CYCLE * tok
    skipped = 2 * PLANE + 1 - CYCLE
    scale = math.log2(math.e) / math.sqrt(HD)
    v_all[:, HD:] = jnp.ones((v_all.shape[0], HD), jnp.bfloat16)

    def one_head(h, carry):
        def fill(get, places, first):
            def body(i, inner):
                k, v = get(i)
                at = pl.multiple_of((first + i) * tok, tok)
                k_all[pl.ds(at, tok), :] = k
                v_all[pl.ds(at, tok), :HD] = v
                f = feature_map(k)
                counted = jnp.concatenate([v, jnp.ones_like(v)], axis=1)
                for b in range(blocks):
                    block = slice(b * BLOCK, (b + 1) * BLOCK)
                    s_all[pl.ds(at + b * BLOCK, BLOCK), :] = dot(
                        f[block], counted[block], CONTRACT_FIRST
                    ).astype(jnp.bfloat16)
                return inner

            lax.fori_loop(0, places, body, 0)

        fill(lambda i: (last2[i, h, 0], last2[i, h, 1]), PLANE - skipped, 0)
        fill(lambda i: (last[i, h, 0], last[i, h, 1]), PLANE, PLANE - skipped)
        fill(lambda i: (own[i, h, 1], own[i, h, 2]), PLANE, 2 * PLANE - skipped)

        def one_shard(i, inner):
            rows = pl.ds(pl.multiple_of(i * tok, tok), window)
            q = own[i, h, 0]
            scores = dot(q, k_all[rows, :], CONTRACT_LAST)
            scores = scores.reshape(blocks, BLOCK, window) * scale + bias_ref[h, i][:, None, :]
            scores = scores.reshape(tok, window)
            probs = jnp.exp2(scores - jnp.max(scores, axis=1, keepdims=True))
            exact = dot(probs.astype(jnp.bfloat16), v_all[rows, :], CONTRACT_ROWS)
            f = jnp.concatenate([feature_map(q)] * (window // BLOCK), axis=1)
            f = (f.reshape(blocks, BLOCK, window) * lin_ref[h, i][:, None, :]).reshape(tok, window)
            linear = dot(f, s_all[rows, :], CONTRACT_ROWS)
            out_ref[i, h] = (
                exact[:, :HD] / exact[:, HD:] + linear[:, :HD] / jnp.maximum(linear[:, HD:], 1.0)
            ).astype(jnp.bfloat16)
            return inner

        lax.fori_loop(0, PLANE, one_shard, 0)
        return carry

    lax.fori_loop(0, count, one_head, 0)


def attention(own, last, last2, bias, lin):
    _, count, _, tok, _ = own.shape
    rows = (2 * PLANE + last2.shape[0]) * tok
    pairs = count * tok * PLANE * CYCLE * tok
    return pl.pallas_call(
        functools.partial(attention_kernel, tok, count),
        out_shape=jax.ShapeDtypeStruct((PLANE, count, tok, HD), jnp.bfloat16),
        in_specs=[VMEM] * 5,
        out_specs=VMEM,
        scratch_shapes=[
            pltpu.VMEM((16, HD), jnp.bfloat16),
            pltpu.VMEM((rows, HD), jnp.bfloat16),
            pltpu.VMEM((rows, 2 * HD), jnp.bfloat16),
            pltpu.VMEM((rows, 2 * HD), jnp.bfloat16),
        ],
        compiler_params=pltpu.CompilerParams(vmem_limit_bytes=48 * 1024 * 1024),
        cost_estimate=pl.CostEstimate(
            flops=8 * pairs * HD, bytes_accessed=8 * count * rows * HD, transcendentals=pairs
        ),
    )(own, last, last2, bias, lin)


def project_kernel(tok, group, spans, summed, place, *refs):
    j, core = place[1], place[2]
    sources = refs[: PLANE * len(spans)]
    refs = refs[PLANE * len(spans) :]
    pieces = []
    for two in summed:
        pieces.append(refs[: 1 + two])
        refs = refs[1 + two :]
    mine, theirs, left, weight = refs
    for g, (first, count) in enumerate(spans):
        for turn in range(PLANE):
            owner = jnp.bitwise_xor(j, turn)
            for h in range(count):
                lanes = pl.ds(pl.multiple_of((owner * group + first + h) * HD, HD), HD)
                for i in range(PLANE):
                    left[i * tok : (i + 1) * tok, lanes] = sources[PLANE * g + turn][i, h]

    for p, piece in enumerate(pieces):
        if len(piece) == 2:
            weight[...] = piece[0][...] + piece[1][...]
            source = weight
        else:
            source = piece[0]

        def one_shard(i, carry, p=p, source=source):
            rows = pl.ds(pl.multiple_of(i * tok, tok), tok)
            product = dot(left[rows, :], source[...], CONTRACT_LAST).astype(jnp.bfloat16)
            low, high = product[: tok // 2], product[tok // 2 :]
            mine[i, p] = jnp.where(core == 0, low, high)
            theirs[i, p] = jnp.where(core == 0, high, low)
            return carry

        lax.fori_loop(0, PLANE, one_shard, 0)


def project(place, group, spans, gathered, pieces):
    tok = gathered[0].shape[2]
    rows, depth = pieces[0][0].shape
    operands = [*gathered] + [a for piece in pieces for a in piece]
    shape = jax.ShapeDtypeStruct((PLANE, len(pieces), tok // 2, rows), jnp.bfloat16)
    return pl.pallas_call(
        functools.partial(project_kernel, tok, group, spans, tuple(len(p) - 1 for p in pieces)),
        out_shape=[shape] * 2,
        in_specs=[SMEM] + [VMEM] * len(operands),
        out_specs=[VMEM] * 2,
        scratch_shapes=[
            pltpu.VMEM((PLANE * tok, depth), jnp.bfloat16),
            pltpu.VMEM((rows, depth), jnp.bfloat16),
        ],
        compiler_params=pltpu.CompilerParams(vmem_limit_bytes=48 * 1024 * 1024),
        cost_estimate=pl.CostEstimate(
            flops=2 * PLANE * tok * rows * len(pieces) * depth,
            bytes_accessed=2 * depth * (PLANE * tok + len(pieces) * rows),
            transcendentals=0,
        ),
    )(place, *operands)


def two_level_plan(queries, keys, values, class_map, out_weight):
    tok = queries.shape[0]
    heads = queries.shape[1] // HD
    group = heads // PLANE
    chunks = CHUNKS if sum(CHUNKS) == group else (1,) * group
    steps = len(chunks)
    firsts = [sum(chunks[:t]) for t in range(steps)]
    spans = tuple(zip(firsts, chunks))
    here = lax.axis_index("seq")
    core = lax.axis_index("head")
    z, j = here // PLANE, here % PLANE
    place = jnp.stack([z, j, core]).astype(jnp.int32)
    skipped = 2 * PLANE + 1 - CYCLE

    packed = pack(chunks, group, queries, keys, values)

    weight_pair = send(after(out_weight, packed[0]), SWAP_PAIR)
    weight_mid = [send(after(out_weight, packed[0]), SWAP_MID), None]

    own, last, last2 = [], [], []
    for t in range(steps):
        message = packed[t] if t == 0 else after(packed[t], own[t - 1])
        own.append(exchange(message))
        if t == 1:
            weight_mid[1] = send(after(weight_pair, last[0]), SWAP_MID)
        current = own[t][:, :, 1:]
        if t:
            current = after(current, last[t - 1])
        last.append(send(current, NEXT_PLANE))
        last2.append(send(last[t][skipped:], NEXT_PLANE))
    weight_end = [send(after(weight_mid[0], last[-1]), TO_ENDS)]
    weight_end.append(send(after(weight_mid[1], weight_end[0]), TO_ENDS))

    parts = class_map.reshape((PLANE, group) + class_map.shape[1:])
    class_parts = []
    for turn in range(PLANE):
        part = lax.dynamic_index_in_dim(parts, jnp.bitwise_xor(j, turn), 0, keepdims=False)
        class_parts.append(send(part, PLANE_SWAP[turn]) if turn else part)
    class_parts = [
        jnp.where(j % 2 == 1, class_parts[i ^ 1], class_parts[i]) for i in range(PLANE)
    ]
    class_parts = [jnp.where(j >= 2, class_parts[i ^ 2], class_parts[i]) for i in range(PLANE)]
    classes = jnp.stack(class_parts, axis=1)[:, :, :, ::-1, :]
    classes = classes.reshape(classes.shape[:3] + (-1, 1))
    wide = jnp.broadcast_to(classes, classes.shape[:4] + (BLOCK,)).reshape(classes.shape[:3] + (-1,))
    bias = jnp.where(wide == 2, 0.0, MASKED).astype(jnp.float32)
    lin = jnp.where(wide == 1, 1.0, 0.0).astype(jnp.bfloat16)

    gathered = []
    for t in range(steps):
        some = slice(firsts[t], firsts[t] + chunks[t])
        att = attention(own[t], last[t], last2[t], bias[some], lin[some])
        gathered += [att] + [send(att, PLANE_SWAP[turn]) for turn in range(1, PLANE)]

    far = jnp.where(z < 2, 2, 1)
    plans = [
        (
            [(out_weight,), (weight_pair,), (weight_mid[0], weight_end[0])],
            [z, jnp.bitwise_xor(z, 1), far],
        ),
        ([(weight_mid[1], weight_end[1])], [jnp.bitwise_xor(far, 1)]),
    ]
    rows = out_weight.shape[0]
    out = jnp.zeros((tok // 2, LINE * PLANE * rows), jnp.bfloat16)
    before = None
    for pieces, lines in plans:
        if before is not None:
            pieces = [tuple(after(a, before) for a in piece) for piece in pieces]
        mine, theirs = project(place, group, spans, gathered, pieces)
        before = mine
        other = lax.ppermute(theirs, "head", [(0, 1), (1, 0)])
        both = (mine.astype(jnp.float32) + other.astype(jnp.float32)).astype(jnp.bfloat16)
        arrived = exchange(both)
        wide = jnp.concatenate([arrived[i] for i in range(PLANE)], axis=2)
        for p, line in enumerate(lines):
            out = lax.dynamic_update_slice_in_dim(out, wide[p], line * PLANE * rows, 1)
    return out


def solution(mesh):
    placed = (
        P("seq", "head"),
        P("seq", "head"),
        P("seq", "head"),
        P("head", "seq", None, None),
        P("seq", "head"),
    )

    def local(queries, *rest):
        heads_here = queries.shape[1] // HD
        two_level = (
            mesh.shape["seq"] == LINE * PLANE
            and mesh.shape["head"] == 2
            and heads_here % LINE == 0
        )
        return (two_level_plan if two_level else ring_plan)(queries, *rest)

    return jax.shard_map(
        local, mesh=mesh, in_specs=placed, out_specs=P(("seq", "head"), None), check_vma=False
    )
```

time: 877 us -> 316 us (0.36)
  waiting for transfers between devices: 604 us -> 149 us
  matrix products: 107 us -> 0 us
  local copies, waits for them, and re-layouts: 131 us -> 36.9 us
  Pallas kernels: 0 us -> 65.3 us
  starting transfers between devices: 2.99 us -> 35.9 us
  blocking collectives: 0 us -> 24.8 us
  between operations: 13.5 us -> 0.35 us
  other arithmetic: 16.3 us -> 3.3 us
    ppermute x7 -> x20, waiting for transfers between devices: 586 us -> 122 us  [the longest x18 117 us: send(): return lax.ppermute(value, 'seq', pairs)]
    dot_general x5 -> x0, matrix products: 107 us -> none  [the longest x1 33.9 us: local(): jnp.einsum('thd,uhd->htu', feature_map(query_heads), feature_map(key_head...]
    eq x7 -> x0, local copies, waits for them, and re-layouts: 72.4 us -> none  [the longest x4 44.1 us: local(): masked = jnp.where(classes == 2, scores, -jnp.inf)]
    pallas_call x0 -> x5, Pallas kernels: none -> 65.3 us  [the longest x2 40.8 us: attention(): pl.pallas_call(functools.partial(attention_kernel, tok, count), out_shape...]
    all_to_all x0 -> x3, waiting for transfers between devices: none -> 26.6 us  [exchange(): lax.all_to_all(value, 'seq', 0, 0, tiled=True, axis_index_groups=PLANES)]
    all_to_all x0 -> x1, blocking collectives: none -> 24.8 us  [exchange(): lax.all_to_all(value, 'seq', 0, 0, tiled=True, axis_index_groups=PLANES)]
    ppermute x7 -> x20, starting transfers between devices: 2.95 us -> 24.4 us  [the longest x18 24.4 us: send(): return lax.ppermute(value, 'seq', pairs)]
    reduce_scatter x1 -> x0, waiting for transfers between devices: 18 us -> none  [local(): lax.psum_scatter(partial_rows.astype(jnp.bfloat16), 'head', scatter_dimen...]
  transfers between devices with their start and end apart: 9 -> 23, of which waited for: 7 -> 12; matrix products, arithmetic and copies ran while one was open for 27% -> 9% of each run, Pallas kernels for 0% -> 21%
where the time goes in v1:
time: 316 us; the launch traced here: 315 us
  waiting for transfers between devices  149 us (47%)
  Pallas kernels  65.3 us (21%)
  local copies, waits for them, and re-layouts  36.9 us (12%)
  starting transfers between devices  35.9 us (11%)
  blocking collectives  24.8 us (8%)
  other arithmetic  3.3 us (1%)
    ppermute x18, waiting for transfers between devices, send(): return lax.ppermute(value, 'seq', pairs)  117 us
    pallas_call x2, Pallas kernels, attention(): pl.pallas_call(functools.partial(attention_kernel, tok, count), out_shape...  40.8 us
    all_to_all x3, waiting for transfers between devices, exchange(): lax.all_to_all(value, 'seq', 0, 0, tiled=True, axis_index_groups=PLANES)  26.6 us
    all_to_all x1, blocking collectives, exchange(): lax.all_to_all(value, 'seq', 0, 0, tiled=True, axis_index_groups=PLANES)  24.8 us
    ppermute x18, starting transfers between devices, send(): return lax.ppermute(value, 'seq', pairs)  24.4 us
    pallas_call x2, Pallas kernels, project(): pl.pallas_call(functools.partial(project_kernel, tok, group, spans, tuple...  23.9 us
    all_to_all x3, starting transfers between devices, exchange(): lax.all_to_all(value, 'seq', 0, 0, tiled=True, axis_index_groups=PLANES)  11.5 us
    unnamed x31, local copies, waits for them, and re-layouts  10.4 us
  transfers between devices with their start and end apart: 23, of which 12 were waited for; matrix products, arithmetic and copies ran while one was open for 9% of the time, Pallas kernels for 21%

profile of v1, /device:TPU:0, one launch (start us, length us, event | category | flops | bytes accessed | tf_op | source)
XLA Modules:
  0.0 315.3 jit_solution(12662999559183737684)
XLA Ops:
  0.0 1.3 copy-done.2
  1.3 1.3 copy-done.3
  2.6 1.3 copy-done.4
  4.0 0.7 shard_map.55
  4.6 24.8 %all_to_all.20.own = bf16[4,2,3,256,128]{4,3,2,1,0:T(8,128)(2,1)} all-to-all(bf16[4,2,3,256,128]{4,3,2,1,0:T(8,128)(2,1)S(1)} %get-tuple-element.19), channel_id=1, replica_groups={{0,2,4,6},{8,10,12,14},{16,18,20,22},{24,26,28,30},{1,3,5,7},{9,11,13,1..., dimensions={0} | all-to-all | bytes 3145728 | tf_op jit(solution)/shard_map/all_to_all | solution.py:123
  29.5 3.6 %all-to-all-start.1 = ((bf16[4,3,3,256,128]{4,3,2,1,0:T(8,128)(2,1)}), bf16[4,3,3,256,128]{4,3,2,1,0:T(8,128)(2,1)S(1)}, u32[]{:S(2)}, u32[]{:S(2)}) async-start(bf16[4,3,3,256,128]{4,3,2,1,0:T(8,128)(2,1)} %copy-done.1), calls=%async_computation.1 | async-start | bytes 4718592 | tf_op jit(solution)/shard_map/all_to_all | solution.py:123
  33.1 2.3 slice.112
  35.4 1.6 collective-permute-start
  37.0 22.5 %all-to-all-done.1.own = bf16[4,3,3,256,128]{4,3,2,1,0:T(8,128)(2,1)S(1)} async-done(((bf16[4,3,3,256,128]{4,3,2,1,0:T(8,128)(2,1)}), bf16[4,3,3,256,128]{4,3,2,1,0:T(8,128)(2,1)S(1)}, u32[]{:S(2)}, u32[]{:S(2)}) %all-to-all-start.1) | async-done | bytes 2359328 | tf_op jit(solution)/shard_map/all_to_all | solution.py:123
  59.6 1.2 collective-permute-done.last
  61.3 1.8 collective-permute-start.14
  63.1 3.3 %collective-permute-start.13 = (bf16[320,2560]{1,0:T(8,128)(2,1)}, bf16[320,2560]{1,0:T(8,128)(2,1)}, u32[]{:S(2)}, u32[]{:S(2)}) collective-permute-start(bf16[320,2560]{1,0:T(8,128)(2,1)} %refs_8_.1), channel_id=1, source_target_pairs={{0,8},{2,10},{4,12},{6,14},{8,0},{10,2},{12,4},{14,6},{16,24},{18,... | collective-permute-start | bytes 4915208 | tf_op jit(solution)/shard_map/ppermute | solution.py:119
  66.4 1.0 slice.113
  67.4 32.6 %collective-permute-done.8.last = bf16[4,3,2,256,128]{4,3,2,1,0:T(8,128)(2,1)S(1)} collective-permute-done((bf16[4,3,2,256,128]{4,3,2,1,0:T(8,128)(2,1)S(1)}, bf16[4,3,2,256,128]{4,3,2,1,0:T(8,128)(2,1)S(1)}, u32[]{:S(2)}, u32[]{:S(2)}) %collective-permute-start.8) | collective-permute-done | bytes 1572896 | tf_op jit(solution)/shard_map/ppermute | solution.py:119
  100.0 1.1 slice.117
  101.1 1.2 copy-done.5
  102.4 2.6 collective-permute-start.2
  105.6 29.5 %collective-permute-done.13.refs_9_ = bf16[320,2560]{1,0:T(8,128)(2,1)} collective-permute-done((bf16[320,2560]{1,0:T(8,128)(2,1)}, bf16[320,2560]{1,0:T(8,128)(2,1)}, u32[]{:S(2)}, u32[]{:S(2)}) %collective-permute-start.13) | collective-permute-done | bytes 1638432 | tf_op jit(solution)/shard_map/ppermute | solution.py:119
  135.2 1.7 collective-permute-start.4
  136.8 1.8 collective-permute-start.17
  138.7 1.3 collective-permute-start.15
  140.3 0.6 slice.115
  141.1 0.8 broadcast_in_dim.32
  141.9 1.7 slice.97.bias_ref
  144.1 0.7 slice.100.lin_ref
  144.9 0.7 broadcast_in_dim.29
  145.7 1.0 slice.89.bias_ref
  146.7 0.8 copy.23
  147.5 0.7 copy.24
  148.2 1.4 broadcast_in_dim.31
  149.6 1.5 slice.92.lin_ref
  151.1 1.2 collective-permute-done.1.last2
  152.2 1.4 copy-done
  153.6 0.8 copy-done.12
  154.5 17.1 %shard_map.56.refs_0_ = bf16[4,2,256,128]{3,2,1,0:T(8,128)(2,1)} custom-call(bf16[4,2,3,256,128]{4,3,2,1,0:T(8,128)(2,1)S(1)} %copy-done, bf16[4,2,2,256,128]{4,3,2,1,0:T(8,128)(2,1)S(1)} %collective-permute-done.last, bf16[3,2,2,256,128]{4,3,2,1,0:T(8,128)(2,1)} %collective-permute-done.1.last2, f32[2,4,2,2048]{3,2,1,0:T(2,128)S(1)} %slice.89.bias_ref, ...), custom_call_target="tpu_custom_call" | custom-call | flops 4294967296 | bytes 5767168 | tf_op jit(solution)/shard_map/pallas_call | solution.py:217
  171.6 1.7 collective-permute-start.5
  173.2 1.2 collective-permute-done.9.last2
  174.4 23.7 %shard_map.57.refs_4_ = bf16[4,3,256,128]{3,2,1,0:T(8,128)(2,1)S(1)} custom-call(bf16[4,3,3,256,128]{4,3,2,1,0:T(8,128)(2,1)S(1)} %all-to-all-done.1.own, bf16[4,3,2,256,128]{4,3,2,1,0:T(8,128)(2,1)S(1)} %copy-done.6, bf16[3,3,2,256,128]{4,3,2,1,0:T(8,128)(2,1)} %collective-permute-done.9.last2, f32[3,4,2,2048]{3,2,1,0:T(2,128)S(1)} %copy-done.10, ...), custom_call_target="tpu_custom_call" | custom-call | flops 6442450944 | bytes 8650752 | tf_op jit(solution)/shard_map/pallas_call | solution.py:217
  198.1 1.0 collective-permute-start.10
  199.1 1.5 collective-permute-start.11
  200.6 0.8 copy-done.7
  201.4 1.1 collective-permute-start.12
  202.5 1.0 collective-permute-start.6
  203.5 6.0 %collective-permute-done.15.refs_11_ = bf16[320,2560]{1,0:T(8,128)(2,1)} collective-permute-done((bf16[320,2560]{1,0:T(8,128)(2,1)}, bf16[320,2560]{1,0:T(8,128)(2,1)}, u32[]{:S(2)}, u32[]{:S(2)}) %collective-permute-start.15) | collective-permute-done | bytes 1638432 | tf_op jit(solution)/shard_map/ppermute | solution.py:119
  209.4 1.9 collective-permute-start.7
  211.4 42.7 %collective-permute-done.6.refs_2_ = bf16[4,2,256,128]{3,2,1,0:T(8,128)(2,1)} collective-permute-done((bf16[4,2,256,128]{3,2,1,0:T(8,128)(2,1)}, bf16[4,2,256,128]{3,2,1,0:T(8,128)(2,1)}, u32[]{:S(2)}, u32[]{:S(2)}) %collective-permute-start.6) | collective-permute-done | bytes 524320 | tf_op jit(solution)/shard_map/ppermute | solution.py:119
  254.1 1.3 collective-permute-start.18
  255.4 1.0 copy-done.8
  256.5 16.2 %shard_map.58 = (bf16[4,3,128,320]{3,2,1,0:T(8,128)(2,1)}, bf16[4,3,128,320]{3,2,1,0:T(8,128)(2,1)}) custom-call(s32[3]{0:T(128)S(1)} %pad_add_fusion.1.place, bf16[4,2,256,128]{3,2,1,0:T(8,128)(2,1)} %shard_map.56.refs_0_, bf16[4,2,256,128]{3,2,1,0:T(8,128)(2,1)S(1)} %copy-done.8, bf16[4,2,256,128]{3,2,1,0:T(8,128)(2,1)} %collective-permute-done.6.refs_2_, ...), custom_call_target="tpu_custom_call" | custom-call | flops 5033164800 | bytes 10158080 | tf_op jit(solution)/shard_map/pallas_call | solution.py:275
  272.7 2.3 copy.29
  275.0 2.9 collective-permute-done.16
  277.9 2.3 copy.30
  280.3 3.0 add_convert_fusion
  283.2 2.3 copy.31
  285.5 4.4 %all-to-all-start.2 = ((bf16[4,3,128,320]{2,3,1,0:T(8,128)(2,1)}), bf16[4,3,128,320]{2,3,1,0:T(8,128)(2,1)}, u32[]{:S(2)}, u32[]{:S(2)}) async-start(bf16[4,3,128,320]{2,3,1,0:T(8,128)(2,1)} %copy.31), calls=%async_computation.2 | async-start | bytes 1966080 | tf_op jit(solution)/shard_map/all_to_all | solution.py:123
  290.0 2.8 collective-permute-done.18.refs_9_
  292.7 1.0 copy-done.9
  293.8 7.7 %shard_map.59 = (bf16[4,1,128,320]{3,2,1,0:T(8,128)(2,1)S(1)}, bf16[4,1,128,320]{3,2,1,0:T(8,128)(2,1)}) custom-call(s32[3]{0:T(128)S(1)} %pad_add_fusion.1.place, bf16[4,2,256,128]{3,2,1,0:T(8,128)(2,1)} %shard_map.56.refs_0_, bf16[4,2,256,128]{3,2,1,0:T(8,128)(2,1)S(1)} %copy-done.9, bf16[4,2,256,128]{3,2,1,0:T(8,128)(2,1)} %collective-permute-done.6.refs_2_, ...), custom_call_target="tpu_custom_call" | custom-call | flops 1677721600 | bytes 6881280 | tf_op jit(solution)/shard_map/pallas_call | solution.py:275
  301.5 1.9 collective-permute-done.19
  303.5 0.9 copy.35
  304.4 3.5 %all-to-all-start.3 = ((bf16[4,1,128,320]{2,3,1,0:T(8,128)(2,1)}), bf16[4,1,128,320]{2,3,1,0:T(8,128)(2,1)S(1)}, u32[]{:S(2)}, u32[]{:S(2)}) async-start(bf16[4,1,128,320]{2,3,1,0:T(8,128)(2,1)} %copy.35), calls=%async_computation.3 | async-start | bytes 655360 | tf_op jit(solution)/shard_map/all_to_all | solution.py:123
  307.9 1.4 slice_bitcast_fusion.6
  310.2 4.1 %all-to-all-done.3 = bf16[4,1,128,320]{2,3,1,0:T(8,128)(2,1)S(1)} async-done(((bf16[4,1,128,320]{2,3,1,0:T(8,128)(2,1)}), bf16[4,1,128,320]{2,3,1,0:T(8,128)(2,1)S(1)}, u32[]{:S(2)}, u32[]{:S(2)}) %all-to-all-start.3) | async-done | bytes 327712 | tf_op jit(solution)/shard_map/all_to_all | solution.py:123
  314.6 0.8 constant_dynamic-update-slice_fusion
  (69 shorter events, 3.8 us)
Async XLA Ops:
  0.0 1.3 copy-start.2
  1.3 1.3 copy-start.3
  2.6 1.3 copy-start.4
  4.6 24.8 %copy-start.1 = (bf16[4,3,3,256,128]{4,3,2,1,0:T(8,128)(2,1)}, bf16[4,3,3,256,128]{4,3,2,1,0:T(8,128)(2,1)S(1)}, u32[]{:S(2)}) copy-start(bf16[4,3,3,256,128]{4,3,2,1,0:T(8,128)(2,1)S(1)} %get-tuple-element.21) | copy-start | bytes 7077892
  29.5 30.0 %all-to-all-start.1 = ((bf16[4,3,3,256,128]{4,3,2,1,0:T(8,128)(2,1)}), bf16[4,3,3,256,128]{4,3,2,1,0:T(8,128)(2,1)S(1)}, u32[]{:S(2)}, u32[]{:S(2)}) async-start(bf16[4,3,3,256,128]{4,3,2,1,0:T(8,128)(2,1)} %copy-done.1), calls=%async_computation.1 | async-start | bytes 4718592 | tf_op jit(solution)/shard_map/all_to_all | solution.py:123
  35.4 25.4 %collective-permute-start = (bf16[4,2,2,256,128]{4,3,2,1,0:T(8,128)(2,1)}, bf16[4,2,2,256,128]{4,3,2,1,0:T(8,128)(2,1)S(1)}, u32[]{:S(2)}, u32[]{:S(2)}) collective-permute-start(bf16[4,2,2,256,128]{4,3,2,1,0:T(8,128)(2,1)} %slice.112), channel_id=1, source_target_pairs={{0,8},{2,10},{4,12},{6,14},{8,16},{10,18},{12,20},{14,22},{16,24},... | collective-permute-start | bytes 3145736 | tf_op jit(solution)/shard_map/ppermute | solution.py:119
  60.8 39.2 %collective-permute-start.8 = (bf16[4,3,2,256,128]{4,3,2,1,0:T(8,128)(2,1)S(1)}, bf16[4,3,2,256,128]{4,3,2,1,0:T(8,128)(2,1)S(1)}, u32[]{:S(2)}, u32[]{:S(2)}) collective-permute-start(bf16[4,3,2,256,128]{4,3,2,1,0:T(8,128)(2,1)S(1)} %slice.116), channel_id=1, source_target_pairs={{0,8},{2,10},{4,12},{6,14},{8,16},{10,18},{12,20},{14,22},{16,24},... | collective-permute-start | bytes 4718600 | tf_op jit(solution)/shard_map/ppermute | solution.py:119
  61.3 43.8 %collective-permute-start.14 = (bf16[320,2560]{1,0:T(8,128)(2,1)}, bf16[320,2560]{1,0:T(8,128)(2,1)}, u32[]{:S(2)}, u32[]{:S(2)}) collective-permute-start(bf16[320,2560]{1,0:T(8,128)(2,1)} %refs_8_.1), channel_id=1, source_target_pairs={{8,16},{10,18},{12,20},{14,22},{16,8},{18,10},{20,12},{22,14},{9,1... | collective-permute-start | bytes 4915208 | tf_op jit(solution)/shard_map/ppermute | solution.py:119
  63.1 72.0 %collective-permute-start.13 = (bf16[320,2560]{1,0:T(8,128)(2,1)}, bf16[320,2560]{1,0:T(8,128)(2,1)}, u32[]{:S(2)}, u32[]{:S(2)}) collective-permute-start(bf16[320,2560]{1,0:T(8,128)(2,1)} %refs_8_.1), channel_id=1, source_target_pairs={{0,8},{2,10},{4,12},{6,14},{8,0},{10,2},{12,4},{14,6},{16,24},{18,... | collective-permute-start | bytes 4915208 | tf_op jit(solution)/shard_map/ppermute | solution.py:119
  67.4 34.9 %copy-start.14 = (s32[20,2,8,2]{0,3,2,1:T(2,128)S(1)}, s32[20,2,8,2]{0,3,2,1:T(2,128)}, u32[]{:S(2)}) copy-start(s32[20,2,8,2]{0,3,2,1:T(2,128)} %param.8) | copy-start | bytes 7684
  67.4 84.9 %collective-permute-start.1 = (bf16[3,2,2,256,128]{4,3,2,1,0:T(8,128)(2,1)}, bf16[3,2,2,256,128]{4,3,2,1,0:T(8,128)(2,1)}, u32[]{:S(2)}, u32[]{:S(2)}) collective-permute-start(bf16[3,2,2,256,128]{4,3,2,1,0:T(8,128)(2,1)} %slice.113), channel_id=1, source_target_pairs={{0,8},{2,10},{4,12},{6,14},{8,16},{10,18},{12,20},{14,22},{16,24},... | collective-permute-start | bytes 2359304 | tf_op jit(solution)/shard_map/ppermute | solution.py:119
  101.1 1.2 copy-start.5
  102.3 72.1 %collective-permute-start.9 = (bf16[3,3,2,256,128]{4,3,2,1,0:T(8,128)(2,1)}, bf16[3,3,2,256,128]{4,3,2,1,0:T(8,128)(2,1)}, u32[]{:S(2)}, u32[]{:S(2)}) collective-permute-start(bf16[3,3,2,256,128]{4,3,2,1,0:T(8,128)(2,1)} %slice.117), channel_id=1, source_target_pairs={{0,8},{2,10},{4,12},{6,14},{8,16},{10,18},{12,20},{14,22},{16,24},... | collective-permute-start | bytes 3538952 | tf_op jit(solution)/shard_map/ppermute | solution.py:119
  102.4 34.4 %collective-permute-start.2 = (s32[5,2,8,2]{2,3,1,0:T(2,128)S(1)}, s32[5,2,8,2]{2,3,1,0:T(2,128)S(1)}, u32[]{:S(2)}, u32[]{:S(2)}) collective-permute-start(s32[5,2,8,2]{2,3,1,0:T(2,128)S(1)} %get-tuple-element.52), channel_id=1, source_target_pairs={{0,6},{2,4},{4,2},{6,0},{8,14},{10,12},{12,10},{14,8},{16,22},{18,... | collective-permute-start | bytes 1928 | tf_op jit(solution)/shard_map/ppermute | solution.py:119
  105.1 33.6 %collective-permute-start.3 = (s32[5,2,8,2]{2,3,1,0:T(2,128)S(1)}, s32[5,2,8,2]{2,3,1,0:T(2,128)S(1)}, u32[]{:S(2)}, u32[]{:S(2)}) collective-permute-start(s32[5,2,8,2]{2,3,1,0:T(2,128)S(1)} %get-tuple-element.51), channel_id=1, source_target_pairs={{0,4},{2,6},{4,0},{6,2},{8,12},{10,14},{12,8},{14,10},{16,20},{18,... | collective-permute-start | bytes 1928 | tf_op jit(solution)/shard_map/ppermute | solution.py:119
  135.2 4.8 %collective-permute-start.4 = (s32[5,2,8,2]{2,3,1,0:T(2,128)S(1)}, s32[5,2,8,2]{2,3,1,0:T(2,128)S(1)}, u32[]{:S(2)}, u32[]{:S(2)}) collective-permute-start(s32[5,2,8,2]{2,3,1,0:T(2,128)S(1)} %get-tuple-element.50), channel_id=1, source_target_pairs={{0,2},{2,0},{4,6},{6,4},{8,10},{10,8},{12,14},{14,12},{16,18},{18,... | collective-permute-start | bytes 1928 | tf_op jit(solution)/shard_map/ppermute | solution.py:119
  136.8 65.7 %collective-permute-start.17 = (bf16[320,2560]{1,0:T(8,128)(2,1)}, bf16[320,2560]{1,0:T(8,128)(2,1)}, u32[]{:S(2)}, u32[]{:S(2)}) collective-permute-start(bf16[320,2560]{1,0:T(8,128)(2,1)} %collective-permute-done.13.refs_9_), channel_id=1, source_target_pairs={{8,16},{10,18},{12,20},{14,22},{16,8},{18,10},{20,12},{22,14},{9,1... | collective-permute-start | bytes 4915208 | tf_op jit(solution)/shard_map/ppermute | solution.py:119
  138.7 70.8 %collective-permute-start.15 = (bf16[320,2560]{1,0:T(8,128)(2,1)}, bf16[320,2560]{1,0:T(8,128)(2,1)}, u32[]{:S(2)}, u32[]{:S(2)}) collective-permute-start(bf16[320,2560]{1,0:T(8,128)(2,1)} %collective-permute-done.14.refs_10_), channel_id=1, source_target_pairs={{8,0},{10,2},{12,4},{14,6},{16,24},{18,26},{20,28},{22,30},{9,1},{... | collective-permute-start | bytes 4915208 | tf_op jit(solution)/shard_map/ppermute | solution.py:119
  152.2 1.4 copy-start
  153.6 0.8 copy-start.12
  154.5 19.9 %copy-start.6 = (bf16[4,3,2,256,128]{4,3,2,1,0:T(8,128)(2,1)S(1)}, bf16[4,3,2,256,128]{4,3,2,1,0:T(8,128)(2,1)}, u32[]{:S(2)}) copy-start(bf16[4,3,2,256,128]{4,3,2,1,0:T(8,128)(2,1)} %copy-done.5) | copy-start | bytes 4718596
  154.5 19.9 %copy-start.10 = (f32[3,4,2,2048]{3,2,1,0:T(2,128)S(1)}, f32[3,4,2,2048]{3,2,1,0:T(2,128)}, u32[]{:S(2)}) copy-start(f32[3,4,2,2048]{3,2,1,0:T(2,128)} %slice.97.bias_ref) | copy-start | bytes 589828
  154.5 19.9 %copy-start.11 = (bf16[3,4,2,2048]{3,2,1,0:T(2,128)(2,1)S(1)}, bf16[3,4,2,2048]{3,2,1,0:T(2,128)(2,1)}, u32[]{:S(2)}) copy-start(bf16[3,4,2,2048]{3,2,1,0:T(2,128)(2,1)} %slice.100.lin_ref) | copy-start | bytes 294916
  171.6 29.1 %collective-permute-start.5 = (bf16[4,2,256,128]{3,2,1,0:T(8,128)(2,1)}, bf16[4,2,256,128]{3,2,1,0:T(8,128)(2,1)S(1)}, u32[]{:S(2)}, u32[]{:S(2)}) collective-permute-start(bf16[4,2,256,128]{3,2,1,0:T(8,128)(2,1)} %shard_map.56.refs_0_), channel_id=1, source_target_pairs={{0,2},{2,0},{4,6},{6,4},{8,10},{10,8},{12,14},{14,12},{16,18},{18,... | collective-permute-start | bytes 1572872 | tf_op jit(solution)/shard_map/ppermute | solution.py:119
  198.1 57.2 %collective-permute-start.10 = (bf16[4,3,256,128]{3,2,1,0:T(8,128)(2,1)S(1)}, bf16[4,3,256,128]{3,2,1,0:T(8,128)(2,1)S(1)}, u32[]{:S(2)}, u32[]{:S(2)}) collective-permute-start(bf16[4,3,256,128]{3,2,1,0:T(8,128)(2,1)S(1)} %shard_map.57.refs_4_), channel_id=1, source_target_pairs={{0,2},{2,0},{4,6},{6,4},{8,10},{10,8},{12,14},{14,12},{16,18},{18,... | collective-permute-start | bytes 2359304 | tf_op jit(solution)/shard_map/ppermute | solution.py:119
  199.1 56.3 %collective-permute-start.11 = (bf16[4,3,256,128]{3,2,1,0:T(8,128)(2,1)S(1)}, bf16[4,3,256,128]{3,2,1,0:T(8,128)(2,1)S(1)}, u32[]{:S(2)}, u32[]{:S(2)}) collective-permute-start(bf16[4,3,256,128]{3,2,1,0:T(8,128)(2,1)S(1)} %shard_map.57.refs_4_), channel_id=1, source_target_pairs={{0,4},{2,6},{4,0},{6,2},{8,12},{10,14},{12,8},{14,10},{16,20},{18,... | collective-permute-start | bytes 2359304 | tf_op jit(solution)/shard_map/ppermute | solution.py:119
  200.6 0.8 copy-start.7
  201.4 54.0 %collective-permute-start.12 = (bf16[4,3,256,128]{3,2,1,0:T(8,128)(2,1)S(1)}, bf16[4,3,256,128]{3,2,1,0:T(8,128)(2,1)S(1)}, u32[]{:S(2)}, u32[]{:S(2)}) collective-permute-start(bf16[4,3,256,128]{3,2,1,0:T(8,128)(2,1)S(1)} %shard_map.57.refs_4_), channel_id=1, source_target_pairs={{0,6},{2,4},{4,2},{6,0},{8,14},{10,12},{12,10},{14,8},{16,22},{18,... | collective-permute-start | bytes 2359304 | tf_op jit(solution)/shard_map/ppermute | solution.py:119
  202.5 51.6 %collective-permute-start.6 = (bf16[4,2,256,128]{3,2,1,0:T(8,128)(2,1)}, bf16[4,2,256,128]{3,2,1,0:T(8,128)(2,1)}, u32[]{:S(2)}, u32[]{:S(2)}) collective-permute-start(bf16[4,2,256,128]{3,2,1,0:T(8,128)(2,1)} %shard_map.56.refs_0_), channel_id=1, source_target_pairs={{0,4},{2,6},{4,0},{6,2},{8,12},{10,14},{12,8},{14,10},{16,20},{18,... | collective-permute-start | bytes 1572872 | tf_op jit(solution)/shard_map/ppermute | solution.py:119
  209.4 45.9 %collective-permute-start.7 = (bf16[4,2,256,128]{3,2,1,0:T(8,128)(2,1)}, bf16[4,2,256,128]{3,2,1,0:T(8,128)(2,1)}, u32[]{:S(2)}, u32[]{:S(2)}) collective-permute-start(bf16[4,2,256,128]{3,2,1,0:T(8,128)(2,1)} %shard_map.56.refs_0_), channel_id=1, source_target_pairs={{0,6},{2,4},{4,2},{6,0},{8,14},{10,12},{12,10},{14,8},{16,22},{18,... | collective-permute-start | bytes 1572872 | tf_op jit(solution)/shard_map/ppermute | solution.py:119
  254.1 38.7 %collective-permute-start.18 = (bf16[320,2560]{1,0:T(8,128)(2,1)}, bf16[320,2560]{1,0:T(8,128)(2,1)}, u32[]{:S(2)}, u32[]{:S(2)}) collective-permute-start(bf16[320,2560]{1,0:T(8,128)(2,1)} %collective-permute-done.17.refs_8_), channel_id=1, source_target_pairs={{8,0},{10,2},{12,4},{14,6},{16,24},{18,26},{20,28},{22,30},{9,1},{... | collective-permute-start | bytes 4915208 | tf_op jit(solution)/shard_map/ppermute | solution.py:119
  255.4 1.0 copy-start.8
  275.0 2.9 collective-permute-start.16
  285.5 18.9 %all-to-all-start.2 = ((bf16[4,3,128,320]{2,3,1,0:T(8,128)(2,1)}), bf16[4,3,128,320]{2,3,1,0:T(8,128)(2,1)}, u32[]{:S(2)}, u32[]{:S(2)}) async-start(bf16[4,3,128,320]{2,3,1,0:T(8,128)(2,1)} %copy.31), calls=%async_computation.2 | async-start | bytes 1966080 | tf_op jit(solution)/shard_map/all_to_all | solution.py:123
  292.7 1.0 copy-start.9
  301.5 1.9 collective-permute-start.19
  304.4 9.9 %all-to-all-start.3 = ((bf16[4,1,128,320]{2,3,1,0:T(8,128)(2,1)}), bf16[4,1,128,320]{2,3,1,0:T(8,128)(2,1)S(1)}, u32[]{:S(2)}, u32[]{:S(2)}) async-start(bf16[4,1,128,320]{2,3,1,0:T(8,128)(2,1)} %copy.35), calls=%async_computation.3 | async-start | bytes 655360 | tf_op jit(solution)/shard_map/all_to_all | solution.py:123
  310.2 4.4 %copy-start.13 = (bf16[128,5120]{1,0:T(8,128)(2,1)}, bf16[128,5120]{1,0:T(8,128)(2,1)S(1)}, u32[]{:S(2)}) copy-start(bf16[128,5120]{1,0:T(8,128)(2,1)S(1)} %constant_dynamic-update-slice_fusion.1) | copy-start | bytes 3932164

commit v2 on v1

v2 whole, which is shorter than its diff:
```python
import functools
import math

import jax
import jax.numpy as jnp
from jax import lax
from jax.experimental import pallas as pl
from jax.experimental.pallas import tpu as pltpu
from jax.sharding import PartitionSpec as P

HD = 128
CYCLE = 8
BLOCK = 128
LINE = 4
PLANE = 4
MASKED = -1e30
HEAVY = pl.CostEstimate(flops=10**10, bytes_accessed=2**24, transcendentals=0)
LIGHT = pl.CostEstimate(flops=1, bytes_accessed=1, transcendentals=0)


def feature_map(numbers):
    x = numbers.astype(jnp.float32)
    return jnp.where(x > 0, x + 1.0, jnp.exp(jnp.minimum(x, 0.0))).astype(jnp.bfloat16)


def passed_along(value, axis, steps):
    count = lax.axis_size(axis)
    pairs = [(source, (source + steps) % count) for source in range(count)]
    return lax.ppermute(value, axis, pairs)


def token_classes(block_row, tok_rows, key_rows):
    heads_here, query_blocks, key_blocks = block_row.shape
    query_width = tok_rows // query_blocks
    key_width = key_rows // key_blocks
    widened = jnp.broadcast_to(
        block_row[:, :, None, :, None],
        (heads_here, query_blocks, query_width, key_blocks, key_width),
    )
    return widened.reshape(heads_here, tok_rows, key_rows)


def ring_plan(queries, keys, values, class_map, out_weight):
    tok_rows = queries.shape[0]
    heads_here = queries.shape[1] // HD
    current = jnp.stack([keys, values])
    arrivals = [current]
    for _ in range(1, CYCLE):
        current = passed_along(current, "seq", 1)
        arrivals.append(current)
    window = jnp.concatenate(arrivals, axis=1)
    key_rows = window.shape[1]
    query_heads = queries.reshape(tok_rows, heads_here, HD)
    key_heads = window[0].reshape(key_rows, heads_here, HD)
    value_heads = window[1].reshape(key_rows, heads_here, HD)
    block_count = class_map.shape[1]
    classes = token_classes(class_map.reshape(heads_here, block_count, -1), tok_rows, key_rows)
    scores = jnp.einsum(
        "thd,uhd->htu", query_heads, key_heads, preferred_element_type=jnp.float32
    ) * (1.0 / math.sqrt(HD))
    masked = jnp.where(classes == 2, scores, -jnp.inf)
    row_max = jnp.max(masked, axis=2, keepdims=True)
    probs = jnp.exp(masked - row_max)
    exact_total = jnp.sum(probs, axis=2, keepdims=True)
    apply_values = functools.partial(
        jnp.einsum, "htu,uhd->htd", preferred_element_type=jnp.float32
    )
    exact_out = apply_values(probs.astype(jnp.bfloat16), value_heads) / exact_total
    affinity = jnp.einsum(
        "thd,uhd->htu",
        feature_map(query_heads),
        feature_map(key_heads),
        preferred_element_type=jnp.float32,
    )
    affinity = jnp.where(classes == 1, affinity, 0.0)
    linear_total = jnp.maximum(jnp.sum(affinity, axis=2, keepdims=True), 1.0)
    linear_out = apply_values(affinity.astype(jnp.bfloat16), value_heads) / linear_total
    attended = (
        (exact_out + linear_out)
        .transpose(1, 0, 2)
        .reshape(tok_rows, heads_here * HD)
        .astype(jnp.bfloat16)
    )
    partial_rows = lax.dot_general(
        attended,
        lax.all_gather(out_weight, "seq", axis=0, tiled=True),
        (((1,), (1,)), ((), ())),
        preferred_element_type=jnp.float32,
    )
    return lax.psum_scatter(
        partial_rows.astype(jnp.bfloat16), "head", scatter_dimension=0, tiled=True
    )


def moves(target):
    pairs = []
    for z in range(LINE):
        for j in range(PLANE):
            to = target(z, j)
            if to is not None:
                pairs.append((z * PLANE + j, to[0] * PLANE + to[1]))
    return pairs


PLANES = [[z * PLANE + j for j in range(PLANE)] for z in range(LINE)]
PLANE_SWAP = [moves(lambda z, j, turn=turn: (z, j ^ turn)) for turn in range(PLANE)]
NEXT_PLANE = moves(lambda z, j: ((z + 1) % LINE, j))
SWAP_PAIR = moves(lambda z, j: (z ^ 1, j))
SWAP_MID = moves(lambda z, j: (3 - z, j) if z in (1, 2) else None)
TO_ENDS = moves(lambda z, j: ({1: 0, 2: 3}[z], j) if z in (1, 2) else None)

CONTRACT_LAST = (((1,), (1,)), ((), ()))
CONTRACT_ROWS = (((1,), (0,)), ((), ()))
CONTRACT_FIRST = (((0,), (0,)), ((), ()))
SMEM = pl.BlockSpec(memory_space=pltpu.SMEM)
VMEM = pl.BlockSpec(memory_space=pltpu.VMEM)


def send(value, pairs):
    return lax.ppermute(value, "seq", pairs)


def exchange(value):
    return lax.all_to_all(value, "seq", 0, 0, tiled=True, axis_index_groups=PLANES)


def after(value, *others):
    return lax.optimization_barrier((value,) + others)[0]


def dot(left, right, dims):
    return lax.dot_general(left, right, dims, preferred_element_type=jnp.float32)


def together(*values):
    return lax.optimization_barrier(values)


def pack_kernel(group, count, *refs):
    out = refs[count]
    for owner in range(PLANE):
        for h in range(group):
            at = (owner * group + h) * HD
            for i in range(count):
                out[owner, h, i] = refs[i][:, at : at + HD]


def pack(group, *arrays):
    tok = arrays[0].shape[0]
    shape = (PLANE, group, len(arrays), tok, HD)
    return pl.pallas_call(
        functools.partial(pack_kernel, group, len(arrays)),
        out_shape=jax.ShapeDtypeStruct(shape, jnp.bfloat16),
        in_specs=[VMEM] * len(arrays),
        out_specs=VMEM,
        compiler_params=pltpu.CompilerParams(vmem_limit_bytes=24 * 1024 * 1024),
        cost_estimate=pl.CostEstimate(
            flops=0, bytes_accessed=4 * len(arrays) * arrays[0].size, transcendentals=0
        ),
    )(*arrays)


def attention_kernel(tok, q_ref, own, last, last2, bias_ref, lin_ref, out_ref, k_all, v_all, s_all):
    blocks = tok // BLOCK
    window = CYCLE * tok
    skipped = 2 * PLANE + 1 - CYCLE
    scale = math.log2(math.e) / math.sqrt(HD)

    @pl.when(pl.program_id(0) == 0)
    def _():
        v_all[:, HD:] = jnp.ones((v_all.shape[0], HD), jnp.bfloat16)

    def fill(ref, places, first):
        def body(i, carry):
            k, v = ref[i, 0, 0], ref[i, 0, 1]
            at = pl.multiple_of((first + i) * tok, tok)
            k_all[pl.ds(at, tok), :] = k
            v_all[pl.ds(at, tok), :HD] = v
            f = feature_map(k)
            counted = jnp.concatenate([v, jnp.ones_like(v)], axis=1)
            for b in range(blocks):
                block = slice(b * BLOCK, (b + 1) * BLOCK)
                s_all[pl.ds(at + b * BLOCK, BLOCK), :] = dot(
                    f[block], counted[block], CONTRACT_FIRST
                ).astype(jnp.bfloat16)
            return carry

        lax.fori_loop(0, places, body, 0)

    fill(last2, PLANE - skipped, 0)
    fill(last, PLANE, PLANE - skipped)
    fill(own, PLANE, 2 * PLANE - skipped)

    def one_shard(i, carry):
        rows = pl.ds(pl.multiple_of(i * tok, tok), window)
        q = q_ref[i, 0, 0]
        scores = dot(q, k_all[rows, :], CONTRACT_LAST)
        scores = scores.reshape(blocks, BLOCK, window) * scale + bias_ref[0, i][:, None, :]
        scores = scores.reshape(tok, window)
        probs = jnp.exp2(scores - jnp.max(scores, axis=1, keepdims=True))
        exact = dot(probs.astype(jnp.bfloat16), v_all[rows, :], CONTRACT_ROWS)
        f = jnp.concatenate([feature_map(q)] * (window // BLOCK), axis=1)
        f = (f.reshape(blocks, BLOCK, window) * lin_ref[0, i][:, None, :]).reshape(tok, window)
        linear = dot(f, s_all[rows, :], CONTRACT_ROWS)
        out_ref[i, 0] = (
            exact[:, :HD] / exact[:, HD:] + linear[:, :HD] / jnp.maximum(linear[:, HD:], 1.0)
        ).astype(jnp.bfloat16)
        return carry

    lax.fori_loop(0, PLANE, one_shard, 0)


def attention(first, count, q, own, last, last2, bias, lin):
    tok = q.shape[3]
    rows = (2 * PLANE + last2.shape[0]) * tok
    pairs = count * tok * PLANE * CYCLE * tok

    def heads(array, start):
        shape = array.shape[:1] + (1,) + array.shape[2:]
        zeros = (0,) * (array.ndim - 2)
        return pl.BlockSpec(shape, lambda h: (0, start + h) + zeros)

    def masks(array):
        return pl.BlockSpec((1,) + array.shape[1:], lambda h: (first + h, 0, 0, 0))

    return pl.pallas_call(
        functools.partial(attention_kernel, tok),
        grid=(count,),
        out_shape=jax.ShapeDtypeStruct((PLANE, count, tok, HD), jnp.bfloat16),
        in_specs=[heads(q, first), heads(own, first), heads(last, first), heads(last2, 0)]
        + [masks(bias), masks(lin)],
        out_specs=pl.BlockSpec((PLANE, 1, tok, HD), lambda h: (0, h, 0, 0)),
        scratch_shapes=[
            pltpu.VMEM((rows, HD), jnp.bfloat16),
            pltpu.VMEM((rows, 2 * HD), jnp.bfloat16),
            pltpu.VMEM((rows, 2 * HD), jnp.bfloat16),
        ],
        compiler_params=pltpu.CompilerParams(vmem_limit_bytes=48 * 1024 * 1024),
        cost_estimate=pl.CostEstimate(
            flops=8 * pairs * HD, bytes_accessed=8 * count * rows * HD, transcendentals=pairs
        ),
    )(q, own, last, last2, bias, lin)


def project_kernel(tok, group, spans, summed, begun, ends, place, *refs):
    j, core = place[1], place[2]
    sources = refs[: PLANE * len(spans)]
    refs = refs[PLANE * len(spans) :]
    pieces = []
    for two in summed:
        pieces.append(refs[: 1 + two])
        refs = refs[1 + two :]
    so_far = refs[0] if begun else None
    *outs, left, weight = refs[1 if begun else 0 :]
    blocks = []
    base = 0
    for g, (first, count) in enumerate(spans):
        width = count * HD
        for turn in range(PLANE):
            owner = jnp.bitwise_xor(j, turn)
            for h in range(count):
                lanes = pl.ds(pl.multiple_of(base + owner * width + h * HD, HD), HD)
                for i in range(PLANE):
                    left[i * tok : (i + 1) * tok, lanes] = sources[PLANE * g + turn][i, h]
        for owner in range(PLANE):
            there = (owner * group + first) * HD
            blocks.append((base + owner * width, there, width))
        base += PLANE * width

    for p, piece in enumerate(pieces):
        if len(piece) == 2:
            weight[...] = piece[0][...] + piece[1][...]
            source = weight
        else:
            source = piece[0]

        def one_shard(i, carry, p=p, source=source):
            rows = pl.ds(pl.multiple_of(i * tok, tok), tok)
            product = so_far[i, p] if begun else None
            for here, there, width in blocks:
                term = dot(
                    source[:, there : there + width], left[rows, here : here + width], CONTRACT_LAST
                )
                product = term if product is None else product + term
            if not ends:
                outs[0][i, p] = product
                return carry
            product = product.astype(jnp.bfloat16)
            low, high = product[:, : tok // 2], product[:, tok // 2 :]
            outs[0][i, p] = jnp.where(core == 0, low, high)
            outs[1][i, p] = jnp.where(core == 0, high, low)
            return carry

        lax.fori_loop(0, PLANE, one_shard, 0)


def project(place, group, spans, gathered, pieces, so_far=None, ends=True, cost=LIGHT):
    tok = gathered[0].shape[2]
    rows, depth = pieces[0][0].shape
    operands = [*gathered] + [a for piece in pieces for a in piece]
    if so_far is not None:
        operands.append(so_far)
    if ends:
        outs = [jax.ShapeDtypeStruct((PLANE, len(pieces), rows, tok // 2), jnp.bfloat16)] * 2
    else:
        outs = [jax.ShapeDtypeStruct((PLANE, len(pieces), rows, tok), jnp.float32)]
    some = sum(count for _, count in spans) * PLANE * HD
    return pl.pallas_call(
        functools.partial(
            project_kernel,
            tok,
            group,
            spans,
            tuple(len(p) - 1 for p in pieces),
            so_far is not None,
            ends,
        ),
        out_shape=outs,
        in_specs=[SMEM] + [VMEM] * len(operands),
        out_specs=[VMEM] * len(outs),
        scratch_shapes=[
            pltpu.VMEM((PLANE * tok, some), jnp.bfloat16),
            pltpu.VMEM((rows, depth), jnp.bfloat16),
        ],
        compiler_params=pltpu.CompilerParams(vmem_limit_bytes=48 * 1024 * 1024),
        cost_estimate=cost,
    )(place, *operands)


def two_level_plan(queries, keys, values, class_map, out_weight):
    tok = queries.shape[0]
    heads = queries.shape[1] // HD
    group = heads // PLANE
    early = max(1, 3 * group // 5)
    spans = ((0, early), (early, group - early))
    here = lax.axis_index("seq")
    core = lax.axis_index("head")
    z, j = here // PLANE, here % PLANE
    place = jnp.stack([z, j, core]).astype(jnp.int32)
    skipped = 2 * PLANE + 1 - CYCLE

    packed = pack(group, keys, values)
    weight_pair = send(out_weight, SWAP_PAIR)
    weight_mid = send(out_weight, SWAP_MID)
    own, queries, weight_pair, weight_mid = together(
        exchange(packed), queries, weight_pair, weight_mid
    )

    q = exchange(pack(group, queries))
    last = send(own, NEXT_PLANE)
    parts = after(class_map, own).reshape((PLANE, group) + class_map.shape[1:])
    class_parts = []
    for turn in range(PLANE):
        part = lax.dynamic_index_in_dim(parts, jnp.bitwise_xor(j, turn), 0, keepdims=False)
        class_parts.append(send(part, PLANE_SWAP[turn]) if turn else part)
    class_parts = [
        jnp.where(j % 2 == 1, class_parts[i ^ 1], class_parts[i]) for i in range(PLANE)
    ]
    class_parts = [jnp.where(j >= 2, class_parts[i ^ 2], class_parts[i]) for i in range(PLANE)]
    classes = jnp.stack(class_parts, axis=1)[:, :, :, ::-1, :]
    classes = classes.reshape(classes.shape[:3] + (-1, 1))
    wide = jnp.broadcast_to(classes, classes.shape[:4] + (BLOCK,)).reshape(classes.shape[:3] + (-1,))
    bias = jnp.where(wide == 2, 0.0, MASKED).astype(jnp.float32)
    lin = jnp.where(wide == 1, 1.0, 0.0).astype(jnp.bfloat16)

    q, own, last, bias, lin, weight_pair, weight_mid = together(
        q, own, last, bias, lin, weight_pair, weight_mid
    )

    behind = last[skipped:]
    last2 = send(behind[:, :early], NEXT_PLANE)
    late2 = send(after(behind[:, early:], last2), NEXT_PLANE)
    att = attention(0, early, q, own, last, last2, bias, lin)
    q, own, last, late2, att, bias, lin, weight_pair, weight_mid = together(
        q, own, last, late2, att, bias, lin, weight_pair, weight_mid
    )

    weight_end = send(weight_mid, TO_ENDS)
    weight_mid2 = send(weight_pair, SWAP_MID)
    gathered = [att] + [send(att, PLANE_SWAP[turn]) for turn in range(1, PLANE)]
    late = attention(early, group - early, q, own, last, late2, bias, lin)
    late, weight_pair, weight_mid, weight_end, weight_mid2, *gathered = together(
        late, weight_pair, weight_mid, weight_end, weight_mid2, *gathered
    )

    weight_end2 = send(weight_mid2, TO_ENDS)
    gathered += [late] + [send(late, PLANE_SWAP[turn]) for turn in range(1, PLANE)]
    far = jnp.where(z < 2, 2, 1)
    rows = out_weight.shape[0]
    out = jnp.zeros((tok // 2, LINE * PLANE * rows), jnp.bfloat16)

    def summed(mine, theirs):
        other = lax.ppermute(theirs, "head", [(0, 1), (1, 0)])
        return (mine.astype(jnp.float32) + other.astype(jnp.float32)).astype(jnp.bfloat16)

    def place_rows(out, arrived, lines):
        for p, line in enumerate(lines):
            wide = arrived[:, p].reshape(PLANE * rows, tok // 2).T
            out = lax.dynamic_update_slice_in_dim(out, wide, line * PLANE * rows, 1)
        return out

    pieces = [(out_weight,), (weight_pair,), (weight_mid, weight_end)]
    (so_far,) = project(place, group, spans[:1], gathered[:PLANE], pieces, ends=False)
    mine, theirs = project(place, group, spans[1:], gathered[PLANE:], pieces, so_far)
    mine, theirs, weight_mid2, weight_end2, *gathered = together(
        mine, theirs, weight_mid2, weight_end2, *gathered
    )

    both, weight_mid2, weight_end2 = together(summed(mine, theirs), weight_mid2, weight_end2)
    arrived = exchange(both)
    mine2, theirs2 = project(
        place, group, spans, gathered, [(weight_mid2, weight_end2)], cost=HEAVY
    )
    both2, arrived = together(summed(mine2, theirs2), arrived)
    turns = [
        lax.dynamic_index_in_dim(both2, jnp.bitwise_xor(j, turn), 0, keepdims=False)
        for turn in range(PLANE)
    ]
    turns = turns[:1] + [send(turns[turn], PLANE_SWAP[turn]) for turn in range(1, PLANE)]
    turns = [jnp.where(j % 2 == 1, turns[i ^ 1], turns[i]) for i in range(PLANE)]
    turns = [jnp.where(j >= 2, turns[i ^ 2], turns[i]) for i in range(PLANE)]
    out = place_rows(out, arrived, [z, jnp.bitwise_xor(z, 1), far])
    return place_rows(out, jnp.stack(turns), [jnp.bitwise_xor(far, 1)])


def solution(mesh):
    placed = (
        P("seq", "head"),
        P("seq", "head"),
        P("seq", "head"),
        P("head", "seq", None, None),
        P("seq", "head"),
    )

    def local(queries, *rest):
        heads_here = queries.shape[1] // HD
        two_level = (
            mesh.shape["seq"] == LINE * PLANE
            and mesh.shape["head"] == 2
            and heads_here % LINE == 0
        )
        return (two_level_plan if two_level else ring_plan)(queries, *rest)

    return jax.shard_map(
        local, mesh=mesh, in_specs=placed, out_specs=P(("seq", "head"), None), check_vma=False
    )
```

time: 316 us -> 270 us (0.85)
  blocking collectives: 24.8 us -> 0 us
  waiting for transfers between devices: 149 us -> 128 us
  local copies, waits for them, and re-layouts: 36.9 us -> 27.2 us
  starting transfers between devices: 35.9 us -> 42.2 us
  Pallas kernels: 65.3 us -> 70.3 us
    all_to_all x3, waiting for transfers between devices: 26.6 us -> 1.75 us  [exchange(): lax.all_to_all(value, 'seq', 0, 0, tiled=True, axis_index_groups=PLANES)]
    all_to_all x1 -> x0, blocking collectives: 24.8 us -> none  [exchange(): lax.all_to_all(value, 'seq', 0, 0, tiled=True, axis_index_groups=PLANES)]
    slice x20 -> x3, local copies, waits for them, and re-layouts: 12.2 us -> 3.78 us  [the longest x1 1.36 us: two_level_plan(): last2 = send(behind[:, :early], NEXT_PLANE)]
    unnamed x31 -> x62, local copies, waits for them, and re-layouts: 10.4 us -> 17 us
    ppermute x18 -> x20, waiting for transfers between devices: 117 us -> 122 us  [send(): return lax.ppermute(value, 'seq', pairs)]
    ppermute x18 -> x20, starting transfers between devices: 24.4 us -> 28.1 us  [send(): return lax.ppermute(value, 'seq', pairs)]
    pallas_call x2 -> x3, Pallas kernels: 23.9 us -> 26.9 us  [project(): pl.pallas_call(functools.partial(project_kernel, tok, group, spans, tuple...]
    pallas_call x3 -> x4, Pallas kernels: 41.4 us -> 43.4 us  [the longest x2 40.2 us: attention(): pl.pallas_call(functools.partial(attention_kernel, tok), grid=(count,), o...]
  transfers between devices with their start and end apart: 23 -> 25, of which waited for: 12 -> 13; matrix products, arithmetic and copies ran while one was open for 9% -> 3% of each run, Pallas kernels for 21% -> 25%
where the time goes in v2:
time: 270 us; the launch traced here: 269 us
  waiting for transfers between devices  128 us (47%)
  Pallas kernels  70.3 us (26%)
  starting transfers between devices  42.2 us (16%)
  local copies, waits for them, and re-layouts  27.2 us (10%)
    ppermute x20, waiting for transfers between devices, send(): return lax.ppermute(value, 'seq', pairs)  122 us
    pallas_call x2, Pallas kernels, attention(): pl.pallas_call(functools.partial(attention_kernel, tok), grid=(count,), o...  40.2 us
    ppermute x20, starting transfers between devices, send(): return lax.ppermute(value, 'seq', pairs)  28.1 us
    pallas_call x3, Pallas kernels, project(): pl.pallas_call(functools.partial(project_kernel, tok, group, spans, tuple...  26.9 us
    unnamed x62, local copies, waits for them, and re-layouts  17 us
    all_to_all x3, starting transfers between devices, exchange(): lax.all_to_all(value, 'seq', 0, 0, tiled=True, axis_index_groups=PLANES)  13.9 us
  transfers between devices with their start and end apart: 25, of which 13 were waited for; matrix products, arithmetic and copies ran while one was open for 3% of the time, Pallas kernels for 25%

profile of v2, /device:TPU:0, one launch (start us, length us, event | category | flops | bytes accessed | tf_op | source)
XLA Modules:
  0.0 269.3 jit_solution(14792431332638942777)
XLA Ops:
  0.0 1.3 copy-done.1
  1.3 1.3 copy-done.2
  2.6 1.9 shard_map.55
  4.6 5.4 %all-to-all-start = ((bf16[4,5,2,256,128]{4,3,2,1,0:T(8,128)(2,1)}), bf16[4,5,2,256,128]{4,3,2,1,0:T(8,128)(2,1)}, u32[]{:S(2)}, u32[]{:S(2)}) async-start(bf16[4,5,2,256,128]{4,3,2,1,0:T(8,128)(2,1)} %shard_map.55), calls=%async_computation | async-start | bytes 5242880 | tf_op jit(solution)/shard_map/all_to_all | solution.py:124
  10.0 2.5 collective-permute-start
  12.5 1.8 collective-permute-start.1
  14.3 34.0 %collective-permute-done.refs_5_ = bf16[320,2560]{1,0:T(8,128)(2,1)S(1)} collective-permute-done((bf16[320,2560]{1,0:T(8,128)(2,1)S(1)}, bf16[320,2560]{1,0:T(8,128)(2,1)S(1)}, u32[]{:S(2)}, u32[]{:S(2)}) %collective-permute-start) | collective-permute-done | bytes 1638432 | tf_op jit(solution)/shard_map/ppermute | solution.py:120
  48.3 1.3 copy-done.26
  49.6 3.6 %collective-permute-start.2 = (bf16[4,5,2,256,128]{4,3,2,1,0:T(8,128)(2,1)}, bf16[4,5,2,256,128]{4,3,2,1,0:T(8,128)(2,1)}, u32[]{:S(2)}, u32[]{:S(2)}) collective-permute-start(bf16[4,5,2,256,128]{4,3,2,1,0:T(8,128)(2,1)} %all-to-all-done.own), channel_id=1, source_target_pairs={{0,8},{2,10},{4,12},{6,14},{8,16},{10,18},{12,20},{14,22},{16,24},... | collective-permute-start | bytes 7864328 | tf_op jit(solution)/shard_map/ppermute | solution.py:120
  53.2 1.3 shard_map.56
  54.5 3.9 %all-to-all-start.1 = ((bf16[4,5,1,256,128]{4,3,2,1,0:T(8,128)(2,1)}), bf16[4,5,1,256,128]{4,3,2,1,0:T(8,128)(2,1)S(1)}, u32[]{:S(2)}, u32[]{:S(2)}) async-start(bf16[4,5,1,256,128]{4,3,2,1,0:T(8,128)(2,1)} %shard_map.56), calls=%async_computation.1 | async-start | bytes 2621440 | tf_op jit(solution)/shard_map/all_to_all | solution.py:124
  58.5 3.0 %collective-permute-start.3 = (s32[5,2,8,2]{2,3,1,0:T(2,128)S(1)}, s32[5,2,8,2]{2,3,1,0:T(2,128)S(1)}, u32[]{:S(2)}, u32[]{:S(2)}) collective-permute-start(s32[5,2,8,2]{2,3,1,0:T(2,128)S(1)} %get-tuple-element.127), channel_id=1, source_target_pairs={{0,6},{2,4},{4,2},{6,0},{8,14},{10,12},{12,10},{14,8},{16,22},{18,... | collective-permute-start | bytes 1928 | tf_op jit(solution)/shard_map/ppermute | solution.py:120
  61.5 0.6 collective-permute-start.4
  62.2 12.8 %collective-permute-done.3 = s32[5,2,8,2]{2,3,1,0:T(2,128)S(1)} collective-permute-done((s32[5,2,8,2]{2,3,1,0:T(2,128)S(1)}, s32[5,2,8,2]{2,3,1,0:T(2,128)S(1)}, u32[]{:S(2)}, u32[]{:S(2)}) %collective-permute-start.3) | collective-permute-done | bytes 672 | tf_op jit(solution)/shard_map/ppermute | solution.py:120
  75.5 0.9 broadcast_in_dim.25
  76.4 1.1 select_n.175.bias_ref
  77.8 0.8 broadcast_in_dim.27
  78.7 1.0 convert_element_type.30.lin_ref
  79.6 30.1 %collective-permute-done.2.last = bf16[4,5,2,256,128]{4,3,2,1,0:T(8,128)(2,1)} collective-permute-done((bf16[4,5,2,256,128]{4,3,2,1,0:T(8,128)(2,1)}, bf16[4,5,2,256,128]{4,3,2,1,0:T(8,128)(2,1)}, u32[]{:S(2)}, u32[]{:S(2)}) %collective-permute-start.2) | collective-permute-done | bytes 2621472 | tf_op jit(solution)/shard_map/ppermute | solution.py:120
  109.8 1.4 slice.19
  111.1 1.5 collective-permute-start.6
  112.7 1.2 slice.18
  113.9 25.4 %collective-permute-done.6.last2 = bf16[3,3,2,256,128]{4,3,2,1,0:T(8,128)(2,1)S(1)} collective-permute-done((bf16[3,3,2,256,128]{4,3,2,1,0:T(8,128)(2,1)S(1)}, bf16[3,3,2,256,128]{4,3,2,1,0:T(8,128)(2,1)S(1)}, u32[]{:S(2)}, u32[]{:S(2)}) %collective-permute-start.6) | collective-permute-done | bytes 1179680 | tf_op jit(solution)/shard_map/ppermute | solution.py:120
  139.2 23.9 %shard_map.57.refs_0_ = bf16[4,3,256,128]{3,2,1,0:T(8,128)(2,1)S(1)} custom-call(bf16[4,5,1,256,128]{4,3,2,1,0:T(8,128)(2,1)S(1)} %all-to-all-done.1.q_ref, bf16[4,5,2,256,128]{4,3,2,1,0:T(8,128)(2,1)} %all-to-all-done.own, bf16[4,5,2,256,128]{4,3,2,1,0:T(8,128)(2,1)} %collective-permute-done.2.last, ...), custom_call_target="tpu_custom_call" | custom-call | flops 6442450944 | bytes 8650752 | tf_op jit(solution)/shard_map/pallas_call | solution.py:226
  163.1 1.3 collective-permute-start.8
  164.4 1.8 collective-permute-start.9
  166.3 1.0 collective-permute-start.10
  167.2 1.5 collective-permute-start.11
  168.7 1.0 collective-permute-start.12
  169.7 1.0 copy-done.23
  170.7 0.9 copy-done.25
  171.6 16.3 %shard_map.58.refs_0_.refs_4_ = bf16[4,2,256,128]{3,2,1,0:T(8,128)(2,1)S(1)} custom-call(bf16[4,5,1,256,128]{4,3,2,1,0:T(8,128)(2,1)S(1)} %all-to-all-done.1.q_ref, bf16[4,5,2,256,128]{4,3,2,1,0:T(8,128)(2,1)} %all-to-all-done.own, bf16[4,5,2,256,128]{4,3,2,1,0:T(8,128)(2,1)} %collective-permute-done.2.last, ...), custom_call_target="tpu_custom_call" | custom-call | flops 4294967296 | bytes 5767168 | tf_op jit(solution)/shard_map/pallas_call | solution.py:226
  188.0 0.9 copy-done.7
  188.9 11.5 %collective-permute-done.11.refs_2_ = bf16[4,3,256,128]{3,2,1,0:T(8,128)(2,1)S(1)} collective-permute-done((bf16[4,3,256,128]{3,2,1,0:T(8,128)(2,1)S(1)}, bf16[4,3,256,128]{3,2,1,0:T(8,128)(2,1)S(1)}, u32[]{:S(2)}, u32[]{:S(2)}) %collective-permute-start.11) | collective-permute-done | bytes 786464 | tf_op jit(solution)/shard_map/ppermute | solution.py:120
  200.4 0.9 copy-done.10
  201.3 0.9 copy-done.13
  202.2 1.3 collective-permute-start.16
  203.5 1.4 collective-permute-start.13
  204.9 0.7 collective-permute-start.14
  205.6 1.4 collective-permute-start.15
  207.1 1.1 copy-done.5
  208.3 1.1 copy-done.8
  209.4 1.1 copy-done.11
  210.5 1.1 copy-done.14
  211.7 11.1 %shard_map.59.refs_8_ = f32[4,3,320,256]{3,2,1,0:T(8,128)} custom-call(s32[3]{0:T(128)S(1)} %pad_add_fusion.1.place, bf16[4,3,256,128]{3,2,1,0:T(8,128)(2,1)S(1)} %copy-done.5, bf16[4,3,256,128]{3,2,1,0:T(8,128)(2,1)S(1)} %copy-done.8, bf16[4,3,256,128]{3,2,1,0:T(8,128)(2,1)S(1)} %copy-done.11, bf16[4,3,256,128]{3,2,1,0:T(8,128)(2,1)S(1)} %copy-done.14, ...), custom_call_target="tpu_custom_call" | custom-call | flops 1 | bytes 1 | tf_op jit(solution)/shard_map/pallas_call | solution.py:308
  222.8 2.2 collective-permute-done.14.refs_2_.refs_6_
  225.0 9.1 %shard_map.60 = (bf16[4,3,320,128]{3,2,1,0:T(8,128)(2,1)S(1)}, bf16[4,3,320,128]{3,2,1,0:T(8,128)(2,1)S(1)}) custom-call(s32[3]{0:T(128)S(1)} %pad_add_fusion.1.place, bf16[4,2,256,128]{3,2,1,0:T(8,128)(2,1)S(1)} %shard_map.58.refs_0_.refs_4_, bf16[4,2,256,128]{3,2,1,0:T(8,128)(2,1)S(1)} %collective-permute-done.13.refs_1_.refs_5_, ...), custom_call_target="tpu_custom_call" | custom-call | flops 1 | bytes 1 | tf_op jit(solution)/shard_map/pallas_call | solution.py:308
  234.2 0.8 copy-done.16
  235.0 3.9 %collective-permute-done.16.refs_9_ = bf16[320,2560]{1,0:T(8,128)(2,1)} collective-permute-done((bf16[320,2560]{1,0:T(8,128)(2,1)}, bf16[320,2560]{1,0:T(8,128)(2,1)}, u32[]{:S(2)}, u32[]{:S(2)}) %collective-permute-start.16) | collective-permute-done | bytes 1638432 | tf_op jit(solution)/shard_map/ppermute | solution.py:120
  238.9 2.6 collective-permute-done.17
  241.5 1.2 add_convert_fusion
  242.7 4.5 %all-to-all-start.2 = ((bf16[4,3,320,128]{3,2,1,0:T(8,128)(2,1)}), bf16[4,3,320,128]{3,2,1,0:T(8,128)(2,1)}, u32[]{:S(2)}, u32[]{:S(2)}) async-start(bf16[4,3,320,128]{3,2,1,0:T(8,128)(2,1)} %add_convert_fusion), calls=%async_computation.2 | async-start | bytes 1966080 | tf_op jit(solution)/shard_map/all_to_all | solution.py:124
  247.3 1.0 copy-done.17
  248.4 1.0 copy-done.19
  249.4 1.0 copy-done.21
  250.5 6.7 %shard_map.61 = (bf16[4,1,320,128]{3,2,1,0:T(8,128)(2,1)S(1)}, bf16[4,1,320,128]{3,2,1,0:T(8,128)(2,1)}) custom-call(s32[3]{0:T(128)S(1)} %pad_add_fusion.1.place, bf16[4,3,256,128]{3,2,1,0:T(8,128)(2,1)S(1)} %copy-done.6, bf16[4,3,256,128]{3,2,1,0:T(8,128)(2,1)S(1)} %copy-done.9, bf16[4,3,256,128]{3,2,1,0:T(8,128)(2,1)S(1)} %copy-done.12, ...), custom_call_target="tpu_custom_call" | custom-call | flops 10000000000 | bytes 16777216 | tf_op jit(solution)/shard_map/pallas_call | solution.py:308
  257.2 1.7 collective-permute-done.18
  259.0 1.7 all-to-all-done.2
  260.8 1.4 collective-permute-start.19
  262.2 1.6 collective-permute-start.20
  263.8 0.6 collective-permute-start.21
  264.4 1.2 fusion.1
  267.3 0.9 collective-permute-done.21
  268.5 0.8 constant_dynamic-update-slice_fusion
  (87 shorter events, 3.4 us)
Async XLA Ops:
  0.0 1.3 copy-start.1
  1.3 1.3 copy-start.2
  4.6 5.4 %copy-start = (bf16[320,2560]{1,0:T(8,128)(2,1)S(1)}, bf16[320,2560]{1,0:T(8,128)(2,1)}, u32[]{:S(2)}) copy-start(bf16[320,2560]{1,0:T(8,128)(2,1)} %refs_4_.3) | copy-start | bytes 4915204
  4.6 48.6 %copy-start.3 = (bf16[256,2560]{1,0:T(8,128)(2,1)S(1)}, bf16[256,2560]{1,0:T(8,128)(2,1)}, u32[]{:S(2)}) copy-start(bf16[256,2560]{1,0:T(8,128)(2,1)} %refs_0_.2) | copy-start | bytes 3932164
  4.6 45.0 %all-to-all-start = ((bf16[4,5,2,256,128]{4,3,2,1,0:T(8,128)(2,1)}), bf16[4,5,2,256,128]{4,3,2,1,0:T(8,128)(2,1)}, u32[]{:S(2)}, u32[]{:S(2)}) async-start(bf16[4,5,2,256,128]{4,3,2,1,0:T(8,128)(2,1)} %shard_map.55), calls=%async_computation | async-start | bytes 5242880 | tf_op jit(solution)/shard_map/all_to_all | solution.py:124
  10.0 38.3 %collective-permute-start = (bf16[320,2560]{1,0:T(8,128)(2,1)S(1)}, bf16[320,2560]{1,0:T(8,128)(2,1)S(1)}, u32[]{:S(2)}, u32[]{:S(2)}) collective-permute-start(bf16[320,2560]{1,0:T(8,128)(2,1)S(1)} %copy-done), channel_id=1, source_target_pairs={{0,8},{2,10},{4,12},{6,14},{8,0},{10,2},{12,4},{14,6},{16,24},{18,... | collective-permute-start | bytes 4915208 | tf_op jit(solution)/shard_map/ppermute | solution.py:120
  12.5 37.1 %collective-permute-start.1 = (bf16[320,2560]{1,0:T(8,128)(2,1)S(1)}, bf16[320,2560]{1,0:T(8,128)(2,1)}, u32[]{:S(2)}, u32[]{:S(2)}) collective-permute-start(bf16[320,2560]{1,0:T(8,128)(2,1)S(1)} %copy-done), channel_id=1, source_target_pairs={{8,16},{10,18},{12,20},{14,22},{16,8},{18,10},{20,12},{22,14},{9,1... | collective-permute-start | bytes 4915208 | tf_op jit(solution)/shard_map/ppermute | solution.py:120
  48.3 1.3 copy-start.26
  49.6 60.2 %collective-permute-start.2 = (bf16[4,5,2,256,128]{4,3,2,1,0:T(8,128)(2,1)}, bf16[4,5,2,256,128]{4,3,2,1,0:T(8,128)(2,1)}, u32[]{:S(2)}, u32[]{:S(2)}) collective-permute-start(bf16[4,5,2,256,128]{4,3,2,1,0:T(8,128)(2,1)} %all-to-all-done.own), channel_id=1, source_target_pairs={{0,8},{2,10},{4,12},{6,14},{8,16},{10,18},{12,20},{14,22},{16,24},... | collective-permute-start | bytes 7864328 | tf_op jit(solution)/shard_map/ppermute | solution.py:120
  54.5 3.9 %copy-start.30 = (s32[20,2,8,2]{0,3,2,1:T(2,128)S(1)}, s32[20,2,8,2]{0,3,2,1:T(2,128)}, u32[]{:S(2)}) copy-start(s32[20,2,8,2]{0,3,2,1:T(2,128)} %param.8) | copy-start | bytes 7684
  54.5 25.2 %all-to-all-start.1 = ((bf16[4,5,1,256,128]{4,3,2,1,0:T(8,128)(2,1)}), bf16[4,5,1,256,128]{4,3,2,1,0:T(8,128)(2,1)S(1)}, u32[]{:S(2)}, u32[]{:S(2)}) async-start(bf16[4,5,1,256,128]{4,3,2,1,0:T(8,128)(2,1)} %shard_map.56), calls=%async_computation.1 | async-start | bytes 2621440 | tf_op jit(solution)/shard_map/all_to_all | solution.py:124
  58.5 16.4 %collective-permute-start.3 = (s32[5,2,8,2]{2,3,1,0:T(2,128)S(1)}, s32[5,2,8,2]{2,3,1,0:T(2,128)S(1)}, u32[]{:S(2)}, u32[]{:S(2)}) collective-permute-start(s32[5,2,8,2]{2,3,1,0:T(2,128)S(1)} %get-tuple-element.127), channel_id=1, source_target_pairs={{0,6},{2,4},{4,2},{6,0},{8,14},{10,12},{12,10},{14,8},{16,22},{18,... | collective-permute-start | bytes 1928 | tf_op jit(solution)/shard_map/ppermute | solution.py:120
  61.5 13.4 %collective-permute-start.4 = (s32[5,2,8,2]{2,3,1,0:T(2,128)S(1)}, s32[5,2,8,2]{2,3,1,0:T(2,128)S(1)}, u32[]{:S(2)}, u32[]{:S(2)}) collective-permute-start(s32[5,2,8,2]{2,3,1,0:T(2,128)S(1)} %get-tuple-element.126), channel_id=1, source_target_pairs={{0,4},{2,6},{4,0},{6,2},{8,12},{10,14},{12,8},{14,10},{16,20},{18,... | collective-permute-start | bytes 1928 | tf_op jit(solution)/shard_map/ppermute | solution.py:120
  62.1 12.8 %collective-permute-start.5 = (s32[5,2,8,2]{2,3,1,0:T(2,128)S(1)}, s32[5,2,8,2]{2,3,1,0:T(2,128)S(1)}, u32[]{:S(2)}, u32[]{:S(2)}) collective-permute-start(s32[5,2,8,2]{2,3,1,0:T(2,128)S(1)} %get-tuple-element.125), channel_id=1, source_target_pairs={{0,2},{2,0},{4,6},{6,4},{8,10},{10,8},{12,14},{14,12},{16,18},{18,... | collective-permute-start | bytes 1928 | tf_op jit(solution)/shard_map/ppermute | solution.py:120
  77.5 61.7 %copy-start.22 = (f32[5,4,2,2048]{3,2,1,0:T(2,128)}, f32[5,4,2,2048]{3,2,1,0:T(2,128)S(1)}, u32[]{:S(2)}) copy-start(f32[5,4,2,2048]{3,2,1,0:T(2,128)S(1)} %select_n.175.bias_ref) | copy-start | bytes 983044
  79.6 59.6 %copy-start.24 = (bf16[5,4,2,2048]{3,2,1,0:T(2,128)(2,1)}, bf16[5,4,2,2048]{3,2,1,0:T(2,128)(2,1)S(1)}, u32[]{:S(2)}) copy-start(bf16[5,4,2,2048]{3,2,1,0:T(2,128)(2,1)S(1)} %convert_element_type.30.lin_ref) | copy-start | bytes 491524
  111.1 28.1 %collective-permute-start.6 = (bf16[3,3,2,256,128]{4,3,2,1,0:T(8,128)(2,1)S(1)}, bf16[3,3,2,256,128]{4,3,2,1,0:T(8,128)(2,1)S(1)}, u32[]{:S(2)}, u32[]{:S(2)}) collective-permute-start(bf16[3,3,2,256,128]{4,3,2,1,0:T(8,128)(2,1)S(1)} %slice.19), channel_id=1, source_target_pairs={{0,8},{2,10},{4,12},{6,14},{8,16},{10,18},{12,20},{14,22},{16,24},... | collective-permute-start | bytes 3538952 | tf_op jit(solution)/shard_map/ppermute | solution.py:120
  113.9 50.6 %copy-start.27 = (bf16[320,2560]{1,0:T(8,128)(2,1)S(1)}, bf16[320,2560]{1,0:T(8,128)(2,1)}, u32[]{:S(2)}) copy-start(bf16[320,2560]{1,0:T(8,128)(2,1)} %copy-done.26) | copy-start | bytes 4915204
  139.2 23.9 %collective-permute-start.7 = (bf16[3,2,2,256,128]{4,3,2,1,0:T(8,128)(2,1)S(1)}, bf16[3,2,2,256,128]{4,3,2,1,0:T(8,128)(2,1)S(1)}, u32[]{:S(2)}, u32[]{:S(2)}) collective-permute-start(bf16[3,2,2,256,128]{4,3,2,1,0:T(8,128)(2,1)S(1)} %slice.18), channel_id=1, source_target_pairs={{0,8},{2,10},{4,12},{6,14},{8,16},{10,18},{12,20},{14,22},{16,24},... | collective-permute-start | bytes 2359304 | tf_op jit(solution)/shard_map/ppermute | solution.py:120
  163.1 24.9 %copy-start.4 = (bf16[4,3,256,128]{3,2,1,0:T(8,128)(2,1)}, bf16[4,3,256,128]{3,2,1,0:T(8,128)(2,1)S(1)}, u32[]{:S(2)}) copy-start(bf16[4,3,256,128]{3,2,1,0:T(8,128)(2,1)S(1)} %shard_map.57.refs_0_) | copy-start | bytes 2359300
  163.1 39.1 %collective-permute-start.8 = (bf16[320,2560]{1,0:T(8,128)(2,1)}, bf16[320,2560]{1,0:T(8,128)(2,1)S(1)}, u32[]{:S(2)}, u32[]{:S(2)}) collective-permute-start(bf16[320,2560]{1,0:T(8,128)(2,1)} %collective-permute-done.1.refs_6_), channel_id=1, source_target_pairs={{8,0},{10,2},{12,4},{14,6},{16,24},{18,26},{20,28},{22,30},{9,1},{... | collective-permute-start | bytes 4915208 | tf_op jit(solution)/shard_map/ppermute | solution.py:120
  164.4 37.8 %collective-permute-start.9 = (bf16[320,2560]{1,0:T(8,128)(2,1)S(1)}, bf16[320,2560]{1,0:T(8,128)(2,1)}, u32[]{:S(2)}, u32[]{:S(2)}) collective-permute-start(bf16[320,2560]{1,0:T(8,128)(2,1)S(1)} %copy-done.27), channel_id=1, source_target_pairs={{8,16},{10,18},{12,20},{14,22},{16,8},{18,10},{20,12},{22,14},{9,1... | collective-permute-start | bytes 4915208 | tf_op jit(solution)/shard_map/ppermute | solution.py:120
  166.3 21.7 %collective-permute-start.10 = (bf16[4,3,256,128]{3,2,1,0:T(8,128)(2,1)S(1)}, bf16[4,3,256,128]{3,2,1,0:T(8,128)(2,1)S(1)}, u32[]{:S(2)}, u32[]{:S(2)}) collective-permute-start(bf16[4,3,256,128]{3,2,1,0:T(8,128)(2,1)S(1)} %shard_map.57.refs_0_), channel_id=1, source_target_pairs={{0,2},{2,0},{4,6},{6,4},{8,10},{10,8},{12,14},{14,12},{16,18},{18,... | collective-permute-start | bytes 2359304 | tf_op jit(solution)/shard_map/ppermute | solution.py:120
  167.2 33.1 %collective-permute-start.11 = (bf16[4,3,256,128]{3,2,1,0:T(8,128)(2,1)S(1)}, bf16[4,3,256,128]{3,2,1,0:T(8,128)(2,1)S(1)}, u32[]{:S(2)}, u32[]{:S(2)}) collective-permute-start(bf16[4,3,256,128]{3,2,1,0:T(8,128)(2,1)S(1)} %shard_map.57.refs_0_), channel_id=1, source_target_pairs={{0,4},{2,6},{4,0},{6,2},{8,12},{10,14},{12,8},{14,10},{16,20},{18,... | collective-permute-start | bytes 2359304 | tf_op jit(solution)/shard_map/ppermute | solution.py:120
  168.7 32.5 %collective-permute-start.12 = (bf16[4,3,256,128]{3,2,1,0:T(8,128)(2,1)S(1)}, bf16[4,3,256,128]{3,2,1,0:T(8,128)(2,1)S(1)}, u32[]{:S(2)}, u32[]{:S(2)}) collective-permute-start(bf16[4,3,256,128]{3,2,1,0:T(8,128)(2,1)S(1)} %shard_map.57.refs_0_), channel_id=1, source_target_pairs={{0,6},{2,4},{4,2},{6,0},{8,14},{10,12},{12,10},{14,8},{16,22},{18,... | collective-permute-start | bytes 2359304 | tf_op jit(solution)/shard_map/ppermute | solution.py:120
  169.7 1.0 copy-start.23
  170.7 0.9 copy-start.25
  188.0 0.9 copy-start.7
  200.4 0.9 copy-start.10
  201.3 0.9 copy-start.13
  202.2 2.7 %copy-start.28 = (bf16[320,2560]{1,0:T(8,128)(2,1)}, bf16[320,2560]{1,0:T(8,128)(2,1)S(1)}, u32[]{:S(2)}) copy-start(bf16[320,2560]{1,0:T(8,128)(2,1)S(1)} %collective-permute-done.8.refs_7_) | copy-start | bytes 4915204
  202.2 36.7 %collective-permute-start.16 = (bf16[320,2560]{1,0:T(8,128)(2,1)}, bf16[320,2560]{1,0:T(8,128)(2,1)}, u32[]{:S(2)}, u32[]{:S(2)}) collective-permute-start(bf16[320,2560]{1,0:T(8,128)(2,1)} %collective-permute-done.9.refs_8_), channel_id=1, source_target_pairs={{8,0},{10,2},{12,4},{14,6},{16,24},{18,26},{20,28},{22,30},{9,1},{... | collective-permute-start | bytes 4915208 | tf_op jit(solution)/shard_map/ppermute | solution.py:120
  203.5 19.3 %collective-permute-start.13 = (bf16[4,2,256,128]{3,2,1,0:T(8,128)(2,1)S(1)}, bf16[4,2,256,128]{3,2,1,0:T(8,128)(2,1)S(1)}, u32[]{:S(2)}, u32[]{:S(2)}) collective-permute-start(bf16[4,2,256,128]{3,2,1,0:T(8,128)(2,1)S(1)} %shard_map.58.refs_0_.refs_4_), channel_id=1, source_target_pairs={{0,2},{2,0},{4,6},{6,4},{8,10},{10,8},{12,14},{14,12},{16,18},{18,... | collective-permute-start | bytes 1572872 | tf_op jit(solution)/shard_map/ppermute | solution.py:120
  204.9 20.0 %collective-permute-start.14 = (bf16[4,2,256,128]{3,2,1,0:T(8,128)(2,1)S(1)}, bf16[4,2,256,128]{3,2,1,0:T(8,128)(2,1)S(1)}, u32[]{:S(2)}, u32[]{:S(2)}) collective-permute-start(bf16[4,2,256,128]{3,2,1,0:T(8,128)(2,1)S(1)} %shard_map.58.refs_0_.refs_4_), channel_id=1, source_target_pairs={{0,4},{2,6},{4,0},{6,2},{8,12},{10,14},{12,8},{14,10},{16,20},{18,... | collective-permute-start | bytes 1572872 | tf_op jit(solution)/shard_map/ppermute | solution.py:120
  205.6 19.4 %collective-permute-start.15 = (bf16[4,2,256,128]{3,2,1,0:T(8,128)(2,1)S(1)}, bf16[4,2,256,128]{3,2,1,0:T(8,128)(2,1)}, u32[]{:S(2)}, u32[]{:S(2)}) collective-permute-start(bf16[4,2,256,128]{3,2,1,0:T(8,128)(2,1)S(1)} %shard_map.58.refs_0_.refs_4_), channel_id=1, source_target_pairs={{0,6},{2,4},{4,2},{6,0},{8,14},{10,12},{12,10},{14,8},{16,22},{18,... | collective-permute-start | bytes 1572872 | tf_op jit(solution)/shard_map/ppermute | solution.py:120
  207.1 1.1 copy-start.5
  208.3 1.1 copy-start.8
  209.4 1.1 copy-start.11
  210.5 1.1 copy-start.14
  222.8 11.3 %copy-start.18 = (bf16[4,2,256,128]{3,2,1,0:T(8,128)(2,1)}, bf16[4,2,256,128]{3,2,1,0:T(8,128)(2,1)S(1)}, u32[]{:S(2)}) copy-start(bf16[4,2,256,128]{3,2,1,0:T(8,128)(2,1)S(1)} %collective-permute-done.13.refs_1_.refs_5_) | copy-start | bytes 1572868
  225.0 9.2 %copy-start.20 = (bf16[4,2,256,128]{3,2,1,0:T(8,128)(2,1)}, bf16[4,2,256,128]{3,2,1,0:T(8,128)(2,1)S(1)}, u32[]{:S(2)}) copy-start(bf16[4,2,256,128]{3,2,1,0:T(8,128)(2,1)S(1)} %collective-permute-done.14.refs_2_.refs_6_) | copy-start | bytes 1572868
  234.2 0.8 copy-start.16
  238.9 2.6 collective-permute-start.17
  241.5 5.8 %copy-start.12 = (bf16[4,3,256,128]{3,2,1,0:T(8,128)(2,1)S(1)}, bf16[4,3,256,128]{3,2,1,0:T(8,128)(2,1)}, u32[]{:S(2)}) copy-start(bf16[4,3,256,128]{3,2,1,0:T(8,128)(2,1)} %copy-done.10) | copy-start | bytes 2359300
  241.5 5.8 %copy-start.15 = (bf16[4,3,256,128]{3,2,1,0:T(8,128)(2,1)S(1)}, bf16[4,3,256,128]{3,2,1,0:T(8,128)(2,1)}, u32[]{:S(2)}) copy-start(bf16[4,3,256,128]{3,2,1,0:T(8,128)(2,1)} %copy-done.13) | copy-start | bytes 2359300
  242.7 4.6 %copy-start.6 = (bf16[4,3,256,128]{3,2,1,0:T(8,128)(2,1)S(1)}, bf16[4,3,256,128]{3,2,1,0:T(8,128)(2,1)}, u32[]{:S(2)}) copy-start(bf16[4,3,256,128]{3,2,1,0:T(8,128)(2,1)} %copy-done.4) | copy-start | bytes 2359300
  242.7 4.6 %copy-start.9 = (bf16[4,3,256,128]{3,2,1,0:T(8,128)(2,1)S(1)}, bf16[4,3,256,128]{3,2,1,0:T(8,128)(2,1)}, u32[]{:S(2)}) copy-start(bf16[4,3,256,128]{3,2,1,0:T(8,128)(2,1)} %copy-done.7) | copy-start | bytes 2359300
  242.7 18.1 %all-to-all-start.2 = ((bf16[4,3,320,128]{3,2,1,0:T(8,128)(2,1)}), bf16[4,3,320,128]{3,2,1,0:T(8,128)(2,1)}, u32[]{:S(2)}, u32[]{:S(2)}) async-start(bf16[4,3,320,128]{3,2,1,0:T(8,128)(2,1)} %add_convert_fusion), calls=%async_computation.2 | async-start | bytes 1966080 | tf_op jit(solution)/shard_map/all_to_all | solution.py:124
  247.3 1.0 copy-start.17
  248.4 1.0 copy-start.19
  249.4 1.0 copy-start.21
  257.1 1.8 collective-permute-start.18
  260.8 6.1 %collective-permute-start.19 = (bf16[1,320,128]{2,1,0:T(8,128)(2,1)S(1)}, bf16[1,320,128]{2,1,0:T(8,128)(2,1)S(1)}, u32[]{:S(2)}, u32[]{:S(2)}) collective-permute-start(bf16[1,320,128]{2,1,0:T(8,128)(2,1)S(1)} %get-tuple-element.118), channel_id=1, source_target_pairs={{0,6},{2,4},{4,2},{6,0},{8,14},{10,12},{12,10},{14,8},{16,22},{18,... | collective-permute-start | bytes 245768 | tf_op jit(solution)/shard_map/ppermute | solution.py:120
  262.2 5.2 %collective-permute-start.20 = (bf16[1,320,128]{2,1,0:T(8,128)(2,1)S(1)}, bf16[1,320,128]{2,1,0:T(8,128)(2,1)S(1)}, u32[]{:S(2)}, u32[]{:S(2)}) collective-permute-start(bf16[1,320,128]{2,1,0:T(8,128)(2,1)S(1)} %get-tuple-element.117), channel_id=1, source_target_pairs={{0,4},{2,6},{4,0},{6,2},{8,12},{10,14},{12,8},{14,10},{16,20},{18,... | collective-permute-start | bytes 245768 | tf_op jit(solution)/shard_map/ppermute | solution.py:120
  263.8 4.4 %collective-permute-start.21 = (bf16[1,320,128]{2,1,0:T(8,128)(2,1)S(1)}, bf16[1,320,128]{2,1,0:T(8,128)(2,1)S(1)}, u32[]{:S(2)}, u32[]{:S(2)}) collective-permute-start(bf16[1,320,128]{2,1,0:T(8,128)(2,1)S(1)} %get-tuple-element.116), channel_id=1, source_target_pairs={{0,2},{2,0},{4,6},{6,4},{8,10},{10,8},{12,14},{14,12},{16,18},{18,... | collective-permute-start | bytes 245768 | tf_op jit(solution)/shard_map/ppermute | solution.py:120
  266.4 2.1 copy-start.29

commit v3 on v2

--- a/solution.py
+++ b/solution.py
@@ -185,7 +185,7 @@
                 ).astype(jnp.bfloat16)
             return carry
 
-        lax.fori_loop(0, places, body, 0)
+        lax.fori_loop(0, places, body, 0, unroll=True)
 
     fill(last2, PLANE - skipped, 0)
     fill(last, PLANE, PLANE - skipped)
@@ -207,7 +207,7 @@
         ).astype(jnp.bfloat16)
         return carry
 
-    lax.fori_loop(0, PLANE, one_shard, 0)
+    lax.fori_loop(0, PLANE, one_shard, 0, unroll=2)
 
 
 def attention(first, count, q, own, last, last2, bias, lin):

time: 270 us -> 263 us (0.974)
  Pallas kernels: 70.3 us -> 58.6 us
  waiting for transfers between devices: 128 us -> 132 us
    pallas_call x2, Pallas kernels: 40.2 us -> 28.5 us  [attention(): pl.pallas_call(functools.partial(attention_kernel, tok), grid=(count,), o...]
    ppermute x20, waiting for transfers between devices: 122 us -> 126 us  [send(): return lax.ppermute(value, 'seq', pairs)]
  transfers between devices with their start and end apart: 25 -> 25, of which waited for: 13 -> 15; matrix products, arithmetic and copies ran while one was open for 3% -> 3% of each run, Pallas kernels for 25% -> 22%
where the time goes in v3:
time: 263 us; the launch traced here: 262 us
  waiting for transfers between devices  132 us (50%)
  Pallas kernels  58.6 us (22%)
  starting transfers between devices  42.1 us (16%)
  local copies, waits for them, and re-layouts  27.2 us (10%)
    ppermute x20, waiting for transfers between devices, send(): return lax.ppermute(value, 'seq', pairs)  126 us
    pallas_call x2, Pallas kernels, attention(): pl.pallas_call(functools.partial(attention_kernel, tok), grid=(count,), o...  28.5 us
    ppermute x20, starting transfers between devices, send(): return lax.ppermute(value, 'seq', pairs)  28.3 us
    pallas_call x3, Pallas kernels, project(): pl.pallas_call(functools.partial(project_kernel, tok, group, spans, tuple...  26.9 us
    unnamed x62, local copies, waits for them, and re-layouts  17 us
    all_to_all x3, starting transfers between devices, exchange(): lax.all_to_all(value, 'seq', 0, 0, tiled=True, axis_index_groups=PLANES)  13.7 us
  transfers between devices with their start and end apart: 25, of which 15 were waited for; matrix products, arithmetic and copies ran while one was open for 3% of the time, Pallas kernels for 22%

profile of v3, /device:TPU:0, one launch (start us, length us, event | category | flops | bytes accessed | tf_op | source)
XLA Modules:
  0.0 262.1 jit_solution(13730228686457791104)
XLA Ops:
  0.0 1.3 copy-done.1
  1.3 1.3 copy-done.2
  2.6 1.9 shard_map.55
  4.6 5.4 %all-to-all-start = ((bf16[4,5,2,256,128]{4,3,2,1,0:T(8,128)(2,1)}), bf16[4,5,2,256,128]{4,3,2,1,0:T(8,128)(2,1)}, u32[]{:S(2)}, u32[]{:S(2)}) async-start(bf16[4,5,2,256,128]{4,3,2,1,0:T(8,128)(2,1)} %shard_map.55), calls=%async_computation | async-start | bytes 5242880 | tf_op jit(solution)/shard_map/all_to_all | solution.py:124
  10.0 2.5 collective-permute-start
  12.5 1.8 collective-permute-start.1
  14.3 34.0 %collective-permute-done.refs_5_ = bf16[320,2560]{1,0:T(8,128)(2,1)S(1)} collective-permute-done((bf16[320,2560]{1,0:T(8,128)(2,1)S(1)}, bf16[320,2560]{1,0:T(8,128)(2,1)S(1)}, u32[]{:S(2)}, u32[]{:S(2)}) %collective-permute-start) | collective-permute-done | bytes 1638432 | tf_op jit(solution)/shard_map/ppermute | solution.py:120
  48.3 1.3 copy-done.26
  49.6 3.6 %collective-permute-start.2 = (bf16[4,5,2,256,128]{4,3,2,1,0:T(8,128)(2,1)}, bf16[4,5,2,256,128]{4,3,2,1,0:T(8,128)(2,1)}, u32[]{:S(2)}, u32[]{:S(2)}) collective-permute-start(bf16[4,5,2,256,128]{4,3,2,1,0:T(8,128)(2,1)} %all-to-all-done.own), channel_id=1, source_target_pairs={{0,8},{2,10},{4,12},{6,14},{8,16},{10,18},{12,20},{14,22},{16,24},... | collective-permute-start | bytes 7864328 | tf_op jit(solution)/shard_map/ppermute | solution.py:120
  53.2 1.3 shard_map.56
  54.5 3.9 %all-to-all-start.1 = ((bf16[4,5,1,256,128]{4,3,2,1,0:T(8,128)(2,1)}), bf16[4,5,1,256,128]{4,3,2,1,0:T(8,128)(2,1)S(1)}, u32[]{:S(2)}, u32[]{:S(2)}) async-start(bf16[4,5,1,256,128]{4,3,2,1,0:T(8,128)(2,1)} %shard_map.56), calls=%async_computation.1 | async-start | bytes 2621440 | tf_op jit(solution)/shard_map/all_to_all | solution.py:124
  58.5 3.0 %collective-permute-start.3 = (s32[5,2,8,2]{2,3,1,0:T(2,128)S(1)}, s32[5,2,8,2]{2,3,1,0:T(2,128)S(1)}, u32[]{:S(2)}, u32[]{:S(2)}) collective-permute-start(s32[5,2,8,2]{2,3,1,0:T(2,128)S(1)} %get-tuple-element.127), channel_id=1, source_target_pairs={{0,6},{2,4},{4,2},{6,0},{8,14},{10,12},{12,10},{14,8},{16,22},{18,... | collective-permute-start | bytes 1928 | tf_op jit(solution)/shard_map/ppermute | solution.py:120
  62.2 12.8 %collective-permute-done.3 = s32[5,2,8,2]{2,3,1,0:T(2,128)S(1)} collective-permute-done((s32[5,2,8,2]{2,3,1,0:T(2,128)S(1)}, s32[5,2,8,2]{2,3,1,0:T(2,128)S(1)}, u32[]{:S(2)}, u32[]{:S(2)}) %collective-permute-start.3) | collective-permute-done | bytes 672 | tf_op jit(solution)/shard_map/ppermute | solution.py:120
  75.5 0.9 broadcast_in_dim.25
  76.4 1.1 select_n.175.bias_ref
  77.8 0.8 broadcast_in_dim.27
  78.7 1.0 convert_element_type.30.lin_ref
  79.6 30.1 %collective-permute-done.2.last = bf16[4,5,2,256,128]{4,3,2,1,0:T(8,128)(2,1)} collective-permute-done((bf16[4,5,2,256,128]{4,3,2,1,0:T(8,128)(2,1)}, bf16[4,5,2,256,128]{4,3,2,1,0:T(8,128)(2,1)}, u32[]{:S(2)}, u32[]{:S(2)}) %collective-permute-start.2) | collective-permute-done | bytes 2621472 | tf_op jit(solution)/shard_map/ppermute | solution.py:120
  109.8 1.4 slice.19
  111.1 1.5 collective-permute-start.6
  112.7 1.2 slice.18
  113.9 25.4 %collective-permute-done.6.last2 = bf16[3,3,2,256,128]{4,3,2,1,0:T(8,128)(2,1)S(1)} collective-permute-done((bf16[3,3,2,256,128]{4,3,2,1,0:T(8,128)(2,1)S(1)}, bf16[3,3,2,256,128]{4,3,2,1,0:T(8,128)(2,1)S(1)}, u32[]{:S(2)}, u32[]{:S(2)}) %collective-permute-start.6) | collective-permute-done | bytes 1179680 | tf_op jit(solution)/shard_map/ppermute | solution.py:120
  139.2 16.8 %shard_map.57.refs_0_ = bf16[4,3,256,128]{3,2,1,0:T(8,128)(2,1)S(1)} custom-call(bf16[4,5,1,256,128]{4,3,2,1,0:T(8,128)(2,1)S(1)} %all-to-all-done.1.q_ref, bf16[4,5,2,256,128]{4,3,2,1,0:T(8,128)(2,1)} %all-to-all-done.own, bf16[4,5,2,256,128]{4,3,2,1,0:T(8,128)(2,1)} %collective-permute-done.2.last, ...), custom_call_target="tpu_custom_call" | custom-call | flops 6442450944 | bytes 8650752 | tf_op jit(solution)/shard_map/pallas_call | solution.py:226
  156.1 1.8 collective-permute-done.7.last2
  157.9 1.3 collective-permute-start.8
  159.2 1.8 collective-permute-start.9
  161.0 0.7 collective-permute-start.10
  161.7 1.5 collective-permute-start.11
  163.2 1.3 collective-permute-start.12
  164.5 1.0 copy-done.23
  165.5 0.9 copy-done.25
  166.4 11.6 %shard_map.58.refs_0_.refs_4_ = bf16[4,2,256,128]{3,2,1,0:T(8,128)(2,1)S(1)} custom-call(bf16[4,5,1,256,128]{4,3,2,1,0:T(8,128)(2,1)S(1)} %all-to-all-done.1.q_ref, bf16[4,5,2,256,128]{4,3,2,1,0:T(8,128)(2,1)} %all-to-all-done.own, bf16[4,5,2,256,128]{4,3,2,1,0:T(8,128)(2,1)} %collective-permute-done.2.last, ...), custom_call_target="tpu_custom_call" | custom-call | flops 4294967296 | bytes 5767168 | tf_op jit(solution)/shard_map/pallas_call | solution.py:226
  178.1 3.5 %collective-permute-done.10.refs_1_ = bf16[4,3,256,128]{3,2,1,0:T(8,128)(2,1)S(1)} collective-permute-done((bf16[4,3,256,128]{3,2,1,0:T(8,128)(2,1)S(1)}, bf16[4,3,256,128]{3,2,1,0:T(8,128)(2,1)S(1)}, u32[]{:S(2)}, u32[]{:S(2)}) %collective-permute-start.10) | collective-permute-done | bytes 786464 | tf_op jit(solution)/shard_map/ppermute | solution.py:120
  181.5 0.9 copy-done.7
  182.4 11.5 %collective-permute-done.11.refs_2_ = bf16[4,3,256,128]{3,2,1,0:T(8,128)(2,1)S(1)} collective-permute-done((bf16[4,3,256,128]{3,2,1,0:T(8,128)(2,1)S(1)}, bf16[4,3,256,128]{3,2,1,0:T(8,128)(2,1)S(1)}, u32[]{:S(2)}, u32[]{:S(2)}) %collective-permute-start.11) | collective-permute-done | bytes 786464 | tf_op jit(solution)/shard_map/ppermute | solution.py:120
  193.9 0.9 copy-done.10
  194.8 0.9 copy-done.13
  195.7 1.5 collective-permute-start.16
  197.2 1.7 collective-permute-start.13
  199.3 1.4 collective-permute-start.15
  200.9 1.1 copy-done.5
  202.0 1.1 copy-done.8
  203.1 1.1 copy-done.11
  204.3 1.1 copy-done.14
  205.4 11.1 %shard_map.59.refs_8_ = f32[4,3,320,256]{3,2,1,0:T(8,128)} custom-call(s32[3]{0:T(128)S(1)} %pad_add_fusion.1.place, bf16[4,3,256,128]{3,2,1,0:T(8,128)(2,1)S(1)} %copy-done.5, bf16[4,3,256,128]{3,2,1,0:T(8,128)(2,1)S(1)} %copy-done.8, bf16[4,3,256,128]{3,2,1,0:T(8,128)(2,1)S(1)} %copy-done.11, bf16[4,3,256,128]{3,2,1,0:T(8,128)(2,1)S(1)} %copy-done.14, ...), custom_call_target="tpu_custom_call" | custom-call | flops 1 | bytes 1 | tf_op jit(solution)/shard_map/pallas_call | solution.py:308
  216.5 1.7 collective-permute-done.14.refs_2_.refs_6_
  218.3 9.2 %shard_map.60 = (bf16[4,3,320,128]{3,2,1,0:T(8,128)(2,1)S(1)}, bf16[4,3,320,128]{3,2,1,0:T(8,128)(2,1)S(1)}) custom-call(s32[3]{0:T(128)S(1)} %pad_add_fusion.1.place, bf16[4,2,256,128]{3,2,1,0:T(8,128)(2,1)S(1)} %shard_map.58.refs_0_.refs_4_, bf16[4,2,256,128]{3,2,1,0:T(8,128)(2,1)S(1)} %collective-permute-done.13.refs_1_.refs_5_, ...), custom_call_target="tpu_custom_call" | custom-call | flops 1 | bytes 1 | tf_op jit(solution)/shard_map/pallas_call | solution.py:308
  227.4 0.8 copy-done.16
  228.3 3.7 %collective-permute-done.16.refs_9_ = bf16[320,2560]{1,0:T(8,128)(2,1)} collective-permute-done((bf16[320,2560]{1,0:T(8,128)(2,1)}, bf16[320,2560]{1,0:T(8,128)(2,1)}, u32[]{:S(2)}, u32[]{:S(2)}) %collective-permute-start.16) | collective-permute-done | bytes 1638432 | tf_op jit(solution)/shard_map/ppermute | solution.py:120
  231.9 2.6 collective-permute-done.17
  234.5 1.2 add_convert_fusion
  235.7 4.4 %all-to-all-start.2 = ((bf16[4,3,320,128]{3,2,1,0:T(8,128)(2,1)}), bf16[4,3,320,128]{3,2,1,0:T(8,128)(2,1)}, u32[]{:S(2)}, u32[]{:S(2)}) async-start(bf16[4,3,320,128]{3,2,1,0:T(8,128)(2,1)} %add_convert_fusion), calls=%async_computation.2 | async-start | bytes 1966080 | tf_op jit(solution)/shard_map/all_to_all | solution.py:124
  240.1 1.0 copy-done.17
  241.2 1.0 copy-done.19
  242.2 1.0 copy-done.21
  243.3 6.6 %shard_map.61 = (bf16[4,1,320,128]{3,2,1,0:T(8,128)(2,1)S(1)}, bf16[4,1,320,128]{3,2,1,0:T(8,128)(2,1)}) custom-call(s32[3]{0:T(128)S(1)} %pad_add_fusion.1.place, bf16[4,3,256,128]{3,2,1,0:T(8,128)(2,1)S(1)} %copy-done.6, bf16[4,3,256,128]{3,2,1,0:T(8,128)(2,1)S(1)} %copy-done.9, bf16[4,3,256,128]{3,2,1,0:T(8,128)(2,1)S(1)} %copy-done.12, ...), custom_call_target="tpu_custom_call" | custom-call | flops 10000000000 | bytes 16777216 | tf_op jit(solution)/shard_map/pallas_call | solution.py:308
  250.1 1.7 collective-permute-done.18
  251.8 1.8 all-to-all-done.2
  253.7 1.5 collective-permute-start.19
  255.2 1.5 collective-permute-start.20
  256.6 0.6 collective-permute-start.21
  257.2 1.2 fusion.1
  260.1 1.0 collective-permute-done.21
  261.4 0.8 constant_dynamic-update-slice_fusion
  (87 shorter events, 4.2 us)
Async XLA Ops:
  0.0 1.3 copy-start.1
  1.3 1.3 copy-start.2
  4.6 5.4 %copy-start = (bf16[320,2560]{1,0:T(8,128)(2,1)S(1)}, bf16[320,2560]{1,0:T(8,128)(2,1)}, u32[]{:S(2)}) copy-start(bf16[320,2560]{1,0:T(8,128)(2,1)} %refs_4_.3) | copy-start | bytes 4915204
  4.6 48.6 %copy-start.3 = (bf16[256,2560]{1,0:T(8,128)(2,1)S(1)}, bf16[256,2560]{1,0:T(8,128)(2,1)}, u32[]{:S(2)}) copy-start(bf16[256,2560]{1,0:T(8,128)(2,1)} %refs_0_.2) | copy-start | bytes 3932164
  4.6 45.0 %all-to-all-start = ((bf16[4,5,2,256,128]{4,3,2,1,0:T(8,128)(2,1)}), bf16[4,5,2,256,128]{4,3,2,1,0:T(8,128)(2,1)}, u32[]{:S(2)}, u32[]{:S(2)}) async-start(bf16[4,5,2,256,128]{4,3,2,1,0:T(8,128)(2,1)} %shard_map.55), calls=%async_computation | async-start | bytes 5242880 | tf_op jit(solution)/shard_map/all_to_all | solution.py:124
  10.0 38.3 %collective-permute-start = (bf16[320,2560]{1,0:T(8,128)(2,1)S(1)}, bf16[320,2560]{1,0:T(8,128)(2,1)S(1)}, u32[]{:S(2)}, u32[]{:S(2)}) collective-permute-start(bf16[320,2560]{1,0:T(8,128)(2,1)S(1)} %copy-done), channel_id=1, source_target_pairs={{0,8},{2,10},{4,12},{6,14},{8,0},{10,2},{12,4},{14,6},{16,24},{18,... | collective-permute-start | bytes 4915208 | tf_op jit(solution)/shard_map/ppermute | solution.py:120
  12.5 37.1 %collective-permute-start.1 = (bf16[320,2560]{1,0:T(8,128)(2,1)S(1)}, bf16[320,2560]{1,0:T(8,128)(2,1)}, u32[]{:S(2)}, u32[]{:S(2)}) collective-permute-start(bf16[320,2560]{1,0:T(8,128)(2,1)S(1)} %copy-done), channel_id=1, source_target_pairs={{8,16},{10,18},{12,20},{14,22},{16,8},{18,10},{20,12},{22,14},{9,1... | collective-permute-start | bytes 4915208 | tf_op jit(solution)/shard_map/ppermute | solution.py:120
  48.3 1.3 copy-start.26
  49.6 60.2 %collective-permute-start.2 = (bf16[4,5,2,256,128]{4,3,2,1,0:T(8,128)(2,1)}, bf16[4,5,2,256,128]{4,3,2,1,0:T(8,128)(2,1)}, u32[]{:S(2)}, u32[]{:S(2)}) collective-permute-start(bf16[4,5,2,256,128]{4,3,2,1,0:T(8,128)(2,1)} %all-to-all-done.own), channel_id=1, source_target_pairs={{0,8},{2,10},{4,12},{6,14},{8,16},{10,18},{12,20},{14,22},{16,24},... | collective-permute-start | bytes 7864328 | tf_op jit(solution)/shard_map/ppermute | solution.py:120
  54.5 3.9 %copy-start.30 = (s32[20,2,8,2]{0,3,2,1:T(2,128)S(1)}, s32[20,2,8,2]{0,3,2,1:T(2,128)}, u32[]{:S(2)}) copy-start(s32[20,2,8,2]{0,3,2,1:T(2,128)} %param.8) | copy-start | bytes 7684
  54.5 25.2 %all-to-all-start.1 = ((bf16[4,5,1,256,128]{4,3,2,1,0:T(8,128)(2,1)}), bf16[4,5,1,256,128]{4,3,2,1,0:T(8,128)(2,1)S(1)}, u32[]{:S(2)}, u32[]{:S(2)}) async-start(bf16[4,5,1,256,128]{4,3,2,1,0:T(8,128)(2,1)} %shard_map.56), calls=%async_computation.1 | async-start | bytes 2621440 | tf_op jit(solution)/shard_map/all_to_all | solution.py:124
  58.5 16.4 %collective-permute-start.3 = (s32[5,2,8,2]{2,3,1,0:T(2,128)S(1)}, s32[5,2,8,2]{2,3,1,0:T(2,128)S(1)}, u32[]{:S(2)}, u32[]{:S(2)}) collective-permute-start(s32[5,2,8,2]{2,3,1,0:T(2,128)S(1)} %get-tuple-element.127), channel_id=1, source_target_pairs={{0,6},{2,4},{4,2},{6,0},{8,14},{10,12},{12,10},{14,8},{16,22},{18,... | collective-permute-start | bytes 1928 | tf_op jit(solution)/shard_map/ppermute | solution.py:120
  61.5 13.4 %collective-permute-start.4 = (s32[5,2,8,2]{2,3,1,0:T(2,128)S(1)}, s32[5,2,8,2]{2,3,1,0:T(2,128)S(1)}, u32[]{:S(2)}, u32[]{:S(2)}) collective-permute-start(s32[5,2,8,2]{2,3,1,0:T(2,128)S(1)} %get-tuple-element.126), channel_id=1, source_target_pairs={{0,4},{2,6},{4,0},{6,2},{8,12},{10,14},{12,8},{14,10},{16,20},{18,... | collective-permute-start | bytes 1928 | tf_op jit(solution)/shard_map/ppermute | solution.py:120
  62.1 12.8 %collective-permute-start.5 = (s32[5,2,8,2]{2,3,1,0:T(2,128)S(1)}, s32[5,2,8,2]{2,3,1,0:T(2,128)S(1)}, u32[]{:S(2)}, u32[]{:S(2)}) collective-permute-start(s32[5,2,8,2]{2,3,1,0:T(2,128)S(1)} %get-tuple-element.125), channel_id=1, source_target_pairs={{0,2},{2,0},{4,6},{6,4},{8,10},{10,8},{12,14},{14,12},{16,18},{18,... | collective-permute-start | bytes 1928 | tf_op jit(solution)/shard_map/ppermute | solution.py:120
  77.5 61.7 %copy-start.22 = (f32[5,4,2,2048]{3,2,1,0:T(2,128)}, f32[5,4,2,2048]{3,2,1,0:T(2,128)S(1)}, u32[]{:S(2)}) copy-start(f32[5,4,2,2048]{3,2,1,0:T(2,128)S(1)} %select_n.175.bias_ref) | copy-start | bytes 983044
  79.6 59.6 %copy-start.24 = (bf16[5,4,2,2048]{3,2,1,0:T(2,128)(2,1)}, bf16[5,4,2,2048]{3,2,1,0:T(2,128)(2,1)S(1)}, u32[]{:S(2)}) copy-start(bf16[5,4,2,2048]{3,2,1,0:T(2,128)(2,1)S(1)} %convert_element_type.30.lin_ref) | copy-start | bytes 491524
  111.1 28.1 %collective-permute-start.6 = (bf16[3,3,2,256,128]{4,3,2,1,0:T(8,128)(2,1)S(1)}, bf16[3,3,2,256,128]{4,3,2,1,0:T(8,128)(2,1)S(1)}, u32[]{:S(2)}, u32[]{:S(2)}) collective-permute-start(bf16[3,3,2,256,128]{4,3,2,1,0:T(8,128)(2,1)S(1)} %slice.19), channel_id=1, source_target_pairs={{0,8},{2,10},{4,12},{6,14},{8,16},{10,18},{12,20},{14,22},{16,24},... | collective-permute-start | bytes 3538952 | tf_op jit(solution)/shard_map/ppermute | solution.py:120
  113.9 45.3 %copy-start.27 = (bf16[320,2560]{1,0:T(8,128)(2,1)S(1)}, bf16[320,2560]{1,0:T(8,128)(2,1)}, u32[]{:S(2)}) copy-start(bf16[320,2560]{1,0:T(8,128)(2,1)} %copy-done.26) | copy-start | bytes 4915204
  139.2 18.7 %collective-permute-start.7 = (bf16[3,2,2,256,128]{4,3,2,1,0:T(8,128)(2,1)S(1)}, bf16[3,2,2,256,128]{4,3,2,1,0:T(8,128)(2,1)S(1)}, u32[]{:S(2)}, u32[]{:S(2)}) collective-permute-start(bf16[3,2,2,256,128]{4,3,2,1,0:T(8,128)(2,1)S(1)} %slice.18), channel_id=1, source_target_pairs={{0,8},{2,10},{4,12},{6,14},{8,16},{10,18},{12,20},{14,22},{16,24},... | collective-permute-start | bytes 2359304 | tf_op jit(solution)/shard_map/ppermute | solution.py:120
  156.1 22.0 %copy-start.4 = (bf16[4,3,256,128]{3,2,1,0:T(8,128)(2,1)}, bf16[4,3,256,128]{3,2,1,0:T(8,128)(2,1)S(1)}, u32[]{:S(2)}) copy-start(bf16[4,3,256,128]{3,2,1,0:T(8,128)(2,1)S(1)} %shard_map.57.refs_0_) | copy-start | bytes 2359300
  157.9 37.8 %collective-permute-start.8 = (bf16[320,2560]{1,0:T(8,128)(2,1)}, bf16[320,2560]{1,0:T(8,128)(2,1)S(1)}, u32[]{:S(2)}, u32[]{:S(2)}) collective-permute-start(bf16[320,2560]{1,0:T(8,128)(2,1)} %collective-permute-done.1.refs_6_), channel_id=1, source_target_pairs={{8,0},{10,2},{12,4},{14,6},{16,24},{18,26},{20,28},{22,30},{9,1},{... | collective-permute-start | bytes 4915208 | tf_op jit(solution)/shard_map/ppermute | solution.py:120
  159.2 36.5 %collective-permute-start.9 = (bf16[320,2560]{1,0:T(8,128)(2,1)S(1)}, bf16[320,2560]{1,0:T(8,128)(2,1)}, u32[]{:S(2)}, u32[]{:S(2)}) collective-permute-start(bf16[320,2560]{1,0:T(8,128)(2,1)S(1)} %copy-done.27), channel_id=1, source_target_pairs={{8,16},{10,18},{12,20},{14,22},{16,8},{18,10},{20,12},{22,14},{9,1... | collective-permute-start | bytes 4915208 | tf_op jit(solution)/shard_map/ppermute | solution.py:120
  161.0 20.5 %collective-permute-start.10 = (bf16[4,3,256,128]{3,2,1,0:T(8,128)(2,1)S(1)}, bf16[4,3,256,128]{3,2,1,0:T(8,128)(2,1)S(1)}, u32[]{:S(2)}, u32[]{:S(2)}) collective-permute-start(bf16[4,3,256,128]{3,2,1,0:T(8,128)(2,1)S(1)} %shard_map.57.refs_0_), channel_id=1, source_target_pairs={{0,2},{2,0},{4,6},{6,4},{8,10},{10,8},{12,14},{14,12},{16,18},{18,... | collective-permute-start | bytes 2359304 | tf_op jit(solution)/shard_map/ppermute | solution.py:120
  161.7 32.2 %collective-permute-start.11 = (bf16[4,3,256,128]{3,2,1,0:T(8,128)(2,1)S(1)}, bf16[4,3,256,128]{3,2,1,0:T(8,128)(2,1)S(1)}, u32[]{:S(2)}, u32[]{:S(2)}) collective-permute-start(bf16[4,3,256,128]{3,2,1,0:T(8,128)(2,1)S(1)} %shard_map.57.refs_0_), channel_id=1, source_target_pairs={{0,4},{2,6},{4,0},{6,2},{8,12},{10,14},{12,8},{14,10},{16,20},{18,... | collective-permute-start | bytes 2359304 | tf_op jit(solution)/shard_map/ppermute | solution.py:120
  163.2 31.6 %collective-permute-start.12 = (bf16[4,3,256,128]{3,2,1,0:T(8,128)(2,1)S(1)}, bf16[4,3,256,128]{3,2,1,0:T(8,128)(2,1)S(1)}, u32[]{:S(2)}, u32[]{:S(2)}) collective-permute-start(bf16[4,3,256,128]{3,2,1,0:T(8,128)(2,1)S(1)} %shard_map.57.refs_0_), channel_id=1, source_target_pairs={{0,6},{2,4},{4,2},{6,0},{8,14},{10,12},{12,10},{14,8},{16,22},{18,... | collective-permute-start | bytes 2359304 | tf_op jit(solution)/shard_map/ppermute | solution.py:120
  164.5 1.0 copy-start.23
  165.5 0.9 copy-start.25
  181.5 0.9 copy-start.7
  193.9 0.9 copy-start.10
  194.8 0.9 copy-start.13
  195.7 3.2 %copy-start.28 = (bf16[320,2560]{1,0:T(8,128)(2,1)}, bf16[320,2560]{1,0:T(8,128)(2,1)S(1)}, u32[]{:S(2)}) copy-start(bf16[320,2560]{1,0:T(8,128)(2,1)S(1)} %collective-permute-done.8.refs_7_) | copy-start | bytes 4915204
  195.7 36.2 %collective-permute-start.16 = (bf16[320,2560]{1,0:T(8,128)(2,1)}, bf16[320,2560]{1,0:T(8,128)(2,1)}, u32[]{:S(2)}, u32[]{:S(2)}) collective-permute-start(bf16[320,2560]{1,0:T(8,128)(2,1)} %collective-permute-done.9.refs_8_), channel_id=1, source_target_pairs={{8,0},{10,2},{12,4},{14,6},{16,24},{18,26},{20,28},{22,30},{9,1},{... | collective-permute-start | bytes 4915208 | tf_op jit(solution)/shard_map/ppermute | solution.py:120
  197.2 19.3 %collective-permute-start.13 = (bf16[4,2,256,128]{3,2,1,0:T(8,128)(2,1)S(1)}, bf16[4,2,256,128]{3,2,1,0:T(8,128)(2,1)S(1)}, u32[]{:S(2)}, u32[]{:S(2)}) collective-permute-start(bf16[4,2,256,128]{3,2,1,0:T(8,128)(2,1)S(1)} %shard_map.58.refs_0_.refs_4_), channel_id=1, source_target_pairs={{0,2},{2,0},{4,6},{6,4},{8,10},{10,8},{12,14},{14,12},{16,18},{18,... | collective-permute-start | bytes 1572872 | tf_op jit(solution)/shard_map/ppermute | solution.py:120
  199.0 19.3 %collective-permute-start.14 = (bf16[4,2,256,128]{3,2,1,0:T(8,128)(2,1)S(1)}, bf16[4,2,256,128]{3,2,1,0:T(8,128)(2,1)S(1)}, u32[]{:S(2)}, u32[]{:S(2)}) collective-permute-start(bf16[4,2,256,128]{3,2,1,0:T(8,128)(2,1)S(1)} %shard_map.58.refs_0_.refs_4_), channel_id=1, source_target_pairs={{0,4},{2,6},{4,0},{6,2},{8,12},{10,14},{12,8},{14,10},{16,20},{18,... | collective-permute-start | bytes 1572872 | tf_op jit(solution)/shard_map/ppermute | solution.py:120
  199.3 18.9 %collective-permute-start.15 = (bf16[4,2,256,128]{3,2,1,0:T(8,128)(2,1)S(1)}, bf16[4,2,256,128]{3,2,1,0:T(8,128)(2,1)}, u32[]{:S(2)}, u32[]{:S(2)}) collective-permute-start(bf16[4,2,256,128]{3,2,1,0:T(8,128)(2,1)S(1)} %shard_map.58.refs_0_.refs_4_), channel_id=1, source_target_pairs={{0,6},{2,4},{4,2},{6,0},{8,14},{10,12},{12,10},{14,8},{16,22},{18,... | collective-permute-start | bytes 1572872 | tf_op jit(solution)/shard_map/ppermute | solution.py:120
  200.9 1.1 copy-start.5
  202.0 1.1 copy-start.8
  203.1 1.1 copy-start.11
  204.3 1.1 copy-start.14
  216.5 10.9 %copy-start.18 = (bf16[4,2,256,128]{3,2,1,0:T(8,128)(2,1)}, bf16[4,2,256,128]{3,2,1,0:T(8,128)(2,1)S(1)}, u32[]{:S(2)}) copy-start(bf16[4,2,256,128]{3,2,1,0:T(8,128)(2,1)S(1)} %collective-permute-done.13.refs_1_.refs_5_) | copy-start | bytes 1572868
  218.2 9.2 %copy-start.20 = (bf16[4,2,256,128]{3,2,1,0:T(8,128)(2,1)}, bf16[4,2,256,128]{3,2,1,0:T(8,128)(2,1)S(1)}, u32[]{:S(2)}) copy-start(bf16[4,2,256,128]{3,2,1,0:T(8,128)(2,1)S(1)} %collective-permute-done.14.refs_2_.refs_6_) | copy-start | bytes 1572868
  227.4 0.8 copy-start.16
  231.9 2.6 collective-permute-start.17
  234.5 5.6 %copy-start.12 = (bf16[4,3,256,128]{3,2,1,0:T(8,128)(2,1)S(1)}, bf16[4,3,256,128]{3,2,1,0:T(8,128)(2,1)}, u32[]{:S(2)}) copy-start(bf16[4,3,256,128]{3,2,1,0:T(8,128)(2,1)} %copy-done.10) | copy-start | bytes 2359300
  234.5 5.6 %copy-start.15 = (bf16[4,3,256,128]{3,2,1,0:T(8,128)(2,1)S(1)}, bf16[4,3,256,128]{3,2,1,0:T(8,128)(2,1)}, u32[]{:S(2)}) copy-start(bf16[4,3,256,128]{3,2,1,0:T(8,128)(2,1)} %copy-done.13) | copy-start | bytes 2359300
  235.7 4.4 %copy-start.6 = (bf16[4,3,256,128]{3,2,1,0:T(8,128)(2,1)S(1)}, bf16[4,3,256,128]{3,2,1,0:T(8,128)(2,1)}, u32[]{:S(2)}) copy-start(bf16[4,3,256,128]{3,2,1,0:T(8,128)(2,1)} %copy-done.4) | copy-start | bytes 2359300
  235.7 4.4 %copy-start.9 = (bf16[4,3,256,128]{3,2,1,0:T(8,128)(2,1)S(1)}, bf16[4,3,256,128]{3,2,1,0:T(8,128)(2,1)}, u32[]{:S(2)}) copy-start(bf16[4,3,256,128]{3,2,1,0:T(8,128)(2,1)} %copy-done.7) | copy-start | bytes 2359300
  235.7 17.9 %all-to-all-start.2 = ((bf16[4,3,320,128]{3,2,1,0:T(8,128)(2,1)}), bf16[4,3,320,128]{3,2,1,0:T(8,128)(2,1)}, u32[]{:S(2)}, u32[]{:S(2)}) async-start(bf16[4,3,320,128]{3,2,1,0:T(8,128)(2,1)} %add_convert_fusion), calls=%async_computation.2 | async-start | bytes 1966080 | tf_op jit(solution)/shard_map/all_to_all | solution.py:124
  240.1 1.0 copy-start.17
  241.2 1.0 copy-start.19
  242.2 1.0 copy-start.21
  249.9 1.8 collective-permute-start.18
  253.7 6.1 %collective-permute-start.19 = (bf16[1,320,128]{2,1,0:T(8,128)(2,1)S(1)}, bf16[1,320,128]{2,1,0:T(8,128)(2,1)S(1)}, u32[]{:S(2)}, u32[]{:S(2)}) collective-permute-start(bf16[1,320,128]{2,1,0:T(8,128)(2,1)S(1)} %get-tuple-element.118), channel_id=1, source_target_pairs={{0,6},{2,4},{4,2},{6,0},{8,14},{10,12},{12,10},{14,8},{16,22},{18,... | collective-permute-start | bytes 245768 | tf_op jit(solution)/shard_map/ppermute | solution.py:120
  255.2 4.9 %collective-permute-start.20 = (bf16[1,320,128]{2,1,0:T(8,128)(2,1)S(1)}, bf16[1,320,128]{2,1,0:T(8,128)(2,1)S(1)}, u32[]{:S(2)}, u32[]{:S(2)}) collective-permute-start(bf16[1,320,128]{2,1,0:T(8,128)(2,1)S(1)} %get-tuple-element.117), channel_id=1, source_target_pairs={{0,4},{2,6},{4,0},{6,2},{8,12},{10,14},{12,8},{14,10},{16,20},{18,... | collective-permute-start | bytes 245768 | tf_op jit(solution)/shard_map/ppermute | solution.py:120
  256.6 4.4 %collective-permute-start.21 = (bf16[1,320,128]{2,1,0:T(8,128)(2,1)S(1)}, bf16[1,320,128]{2,1,0:T(8,128)(2,1)S(1)}, u32[]{:S(2)}, u32[]{:S(2)}) collective-permute-start(bf16[1,320,128]{2,1,0:T(8,128)(2,1)S(1)} %get-tuple-element.116), channel_id=1, source_target_pairs={{0,2},{2,0},{4,6},{6,4},{8,10},{10,8},{12,14},{14,12},{16,18},{18,... | collective-permute-start | bytes 245768 | tf_op jit(solution)/shard_map/ppermute | solution.py:120
  259.3 2.1 copy-start.29

commit v4 on v3

--- a/solution.py
+++ b/solution.py
@@ -291,7 +291,7 @@
             outs[1][i, p] = jnp.where(core == 0, high, low)
             return carry
 
-        lax.fori_loop(0, PLANE, one_shard, 0)
+        lax.fori_loop(0, PLANE, one_shard, 0, unroll=2)
 
 
 def project(place, group, spans, gathered, pieces, so_far=None, ends=True, cost=LIGHT):
@@ -402,9 +402,7 @@
     pieces = [(out_weight,), (weight_pair,), (weight_mid, weight_end)]
     (so_far,) = project(place, group, spans[:1], gathered[:PLANE], pieces, ends=False)
     mine, theirs = project(place, group, spans[1:], gathered[PLANE:], pieces, so_far)
-    mine, theirs, weight_mid2, weight_end2, *gathered = together(
-        mine, theirs, weight_mid2, weight_end2, *gathered
-    )
+    mine, theirs, *gathered = together(mine, theirs, *gathered)
 
     both, weight_mid2, weight_end2 = together(summed(mine, theirs), weight_mid2, weight_end2)
     arrived = exchange(both)

time: 263 us -> 261 us (level)
  Pallas kernels: 58.6 us -> 55.9 us
    pallas_call x3, Pallas kernels: 26.9 us -> 24.3 us  [project(): pl.pallas_call(functools.partial(project_kernel, tok, group, spans, tuple...]
  transfers between devices with their start and end apart: 25 -> 25, of which waited for: 15 -> 15; matrix products, arithmetic and copies ran while one was open for 3% -> 4% of each run, Pallas kernels for 22% -> 21%
where the time goes in v4:
time: 261 us; the launch traced here: 260 us
  waiting for transfers between devices  133 us (51%)
  Pallas kernels  55.9 us (21%)
  starting transfers between devices  42.2 us (16%)
  local copies, waits for them, and re-layouts  27.2 us (10%)
    ppermute x20, waiting for transfers between devices, send(): return lax.ppermute(value, 'seq', pairs)  128 us
    ppermute x20, starting transfers between devices, send(): return lax.ppermute(value, 'seq', pairs)  28.6 us
    pallas_call x2, Pallas kernels, attention(): pl.pallas_call(functools.partial(attention_kernel, tok), grid=(count,), o...  28.5 us
    pallas_call x3, Pallas kernels, project(): pl.pallas_call(functools.partial(project_kernel, tok, group, spans, tuple...  24.3 us
    unnamed x62, local copies, waits for them, and re-layouts  17 us
    all_to_all x3, starting transfers between devices, exchange(): lax.all_to_all(value, 'seq', 0, 0, tiled=True, axis_index_groups=PLANES)  13.6 us
  transfers between devices with their start and end apart: 25, of which 15 were waited for; matrix products, arithmetic and copies ran while one was open for 4% of the time, Pallas kernels for 21%

profile of v4, /device:TPU:0, one launch (start us, length us, event | category | flops | bytes accessed | tf_op | source)
XLA Modules:
  0.0 260.2 jit_solution(806974969320648754)
XLA Ops:
  0.0 1.3 copy-done.1
  1.3 1.3 copy-done.2
  2.6 1.9 shard_map.55
  4.6 5.4 %all-to-all-start = ((bf16[4,5,2,256,128]{4,3,2,1,0:T(8,128)(2,1)}), bf16[4,5,2,256,128]{4,3,2,1,0:T(8,128)(2,1)}, u32[]{:S(2)}, u32[]{:S(2)}) async-start(bf16[4,5,2,256,128]{4,3,2,1,0:T(8,128)(2,1)} %shard_map.55), calls=%async_computation | async-start | bytes 5242880 | tf_op jit(solution)/shard_map/all_to_all | solution.py:124
  10.0 2.5 collective-permute-start
  12.5 1.8 collective-permute-start.1
  14.3 34.0 %collective-permute-done.refs_5_ = bf16[320,2560]{1,0:T(8,128)(2,1)S(1)} collective-permute-done((bf16[320,2560]{1,0:T(8,128)(2,1)S(1)}, bf16[320,2560]{1,0:T(8,128)(2,1)S(1)}, u32[]{:S(2)}, u32[]{:S(2)}) %collective-permute-start) | collective-permute-done | bytes 1638432 | tf_op jit(solution)/shard_map/ppermute | solution.py:120
  48.3 1.3 copy-done.26
  49.6 3.6 %collective-permute-start.2 = (bf16[4,5,2,256,128]{4,3,2,1,0:T(8,128)(2,1)}, bf16[4,5,2,256,128]{4,3,2,1,0:T(8,128)(2,1)}, u32[]{:S(2)}, u32[]{:S(2)}) collective-permute-start(bf16[4,5,2,256,128]{4,3,2,1,0:T(8,128)(2,1)} %all-to-all-done.own), channel_id=1, source_target_pairs={{0,8},{2,10},{4,12},{6,14},{8,16},{10,18},{12,20},{14,22},{16,24},... | collective-permute-start | bytes 7864328 | tf_op jit(solution)/shard_map/ppermute | solution.py:120
  53.2 1.3 shard_map.56
  54.5 3.9 %all-to-all-start.1 = ((bf16[4,5,1,256,128]{4,3,2,1,0:T(8,128)(2,1)}), bf16[4,5,1,256,128]{4,3,2,1,0:T(8,128)(2,1)S(1)}, u32[]{:S(2)}, u32[]{:S(2)}) async-start(bf16[4,5,1,256,128]{4,3,2,1,0:T(8,128)(2,1)} %shard_map.56), calls=%async_computation.1 | async-start | bytes 2621440 | tf_op jit(solution)/shard_map/all_to_all | solution.py:124
  58.5 3.0 %collective-permute-start.3 = (s32[5,2,8,2]{2,3,1,0:T(2,128)S(1)}, s32[5,2,8,2]{2,3,1,0:T(2,128)S(1)}, u32[]{:S(2)}, u32[]{:S(2)}) collective-permute-start(s32[5,2,8,2]{2,3,1,0:T(2,128)S(1)} %get-tuple-element.123), channel_id=1, source_target_pairs={{0,6},{2,4},{4,2},{6,0},{8,14},{10,12},{12,10},{14,8},{16,22},{18,... | collective-permute-start | bytes 1928 | tf_op jit(solution)/shard_map/ppermute | solution.py:120
  61.5 0.6 collective-permute-start.4
  62.2 12.8 %collective-permute-done.3 = s32[5,2,8,2]{2,3,1,0:T(2,128)S(1)} collective-permute-done((s32[5,2,8,2]{2,3,1,0:T(2,128)S(1)}, s32[5,2,8,2]{2,3,1,0:T(2,128)S(1)}, u32[]{:S(2)}, u32[]{:S(2)}) %collective-permute-start.3) | collective-permute-done | bytes 672 | tf_op jit(solution)/shard_map/ppermute | solution.py:120
  75.5 0.9 broadcast_in_dim.25
  76.4 1.1 select_n.175.bias_ref
  77.8 0.8 broadcast_in_dim.27
  78.7 1.0 convert_element_type.30.lin_ref
  79.6 30.1 %collective-permute-done.2.last = bf16[4,5,2,256,128]{4,3,2,1,0:T(8,128)(2,1)} collective-permute-done((bf16[4,5,2,256,128]{4,3,2,1,0:T(8,128)(2,1)}, bf16[4,5,2,256,128]{4,3,2,1,0:T(8,128)(2,1)}, u32[]{:S(2)}, u32[]{:S(2)}) %collective-permute-start.2) | collective-permute-done | bytes 2621472 | tf_op jit(solution)/shard_map/ppermute | solution.py:120
  109.8 1.4 slice.19
  111.1 1.5 collective-permute-start.6
  112.7 1.2 slice.18
  113.9 25.4 %collective-permute-done.6.last2 = bf16[3,3,2,256,128]{4,3,2,1,0:T(8,128)(2,1)S(1)} collective-permute-done((bf16[3,3,2,256,128]{4,3,2,1,0:T(8,128)(2,1)S(1)}, bf16[3,3,2,256,128]{4,3,2,1,0:T(8,128)(2,1)S(1)}, u32[]{:S(2)}, u32[]{:S(2)}) %collective-permute-start.6) | collective-permute-done | bytes 1179680 | tf_op jit(solution)/shard_map/ppermute | solution.py:120
  139.2 16.8 %shard_map.57.refs_0_ = bf16[4,3,256,128]{3,2,1,0:T(8,128)(2,1)S(1)} custom-call(bf16[4,5,1,256,128]{4,3,2,1,0:T(8,128)(2,1)S(1)} %all-to-all-done.1.q_ref, bf16[4,5,2,256,128]{4,3,2,1,0:T(8,128)(2,1)} %all-to-all-done.own, bf16[4,5,2,256,128]{4,3,2,1,0:T(8,128)(2,1)} %collective-permute-done.2.last, ...), custom_call_target="tpu_custom_call" | custom-call | flops 6442450944 | bytes 8650752 | tf_op jit(solution)/shard_map/pallas_call | solution.py:226
  156.1 1.8 collective-permute-done.7.last2
  157.9 1.3 collective-permute-start.8
  159.2 1.8 collective-permute-start.9
  161.0 0.7 collective-permute-start.10
  161.7 1.5 collective-permute-start.11
  163.2 1.3 collective-permute-start.12
  164.5 1.0 copy-done.23
  165.5 0.9 copy-done.25
  166.4 11.6 %shard_map.58.refs_0_.refs_4_ = bf16[4,2,256,128]{3,2,1,0:T(8,128)(2,1)S(1)} custom-call(bf16[4,5,1,256,128]{4,3,2,1,0:T(8,128)(2,1)S(1)} %all-to-all-done.1.q_ref, bf16[4,5,2,256,128]{4,3,2,1,0:T(8,128)(2,1)} %all-to-all-done.own, bf16[4,5,2,256,128]{4,3,2,1,0:T(8,128)(2,1)} %collective-permute-done.2.last, ...), custom_call_target="tpu_custom_call" | custom-call | flops 4294967296 | bytes 5767168 | tf_op jit(solution)/shard_map/pallas_call | solution.py:226
  178.1 3.5 %collective-permute-done.10.refs_1_ = bf16[4,3,256,128]{3,2,1,0:T(8,128)(2,1)S(1)} collective-permute-done((bf16[4,3,256,128]{3,2,1,0:T(8,128)(2,1)S(1)}, bf16[4,3,256,128]{3,2,1,0:T(8,128)(2,1)S(1)}, u32[]{:S(2)}, u32[]{:S(2)}) %collective-permute-start.10) | collective-permute-done | bytes 786464 | tf_op jit(solution)/shard_map/ppermute | solution.py:120
  181.5 0.9 copy-done.7
  182.4 11.5 %collective-permute-done.11.refs_2_ = bf16[4,3,256,128]{3,2,1,0:T(8,128)(2,1)S(1)} collective-permute-done((bf16[4,3,256,128]{3,2,1,0:T(8,128)(2,1)S(1)}, bf16[4,3,256,128]{3,2,1,0:T(8,128)(2,1)S(1)}, u32[]{:S(2)}, u32[]{:S(2)}) %collective-permute-start.11) | collective-permute-done | bytes 786464 | tf_op jit(solution)/shard_map/ppermute | solution.py:120
  193.9 0.9 copy-done.10
  194.8 0.9 copy-done.13
  195.7 1.3 collective-permute-start.13
  197.0 1.7 collective-permute-start.14
  198.8 0.9 collective-permute-start.15
  199.6 1.5 collective-permute-start.17
  201.2 1.1 copy-done.5
  202.3 1.1 copy-done.8
  203.5 1.1 copy-done.11
  204.6 1.1 copy-done.14
  205.7 10.2 %shard_map.59.refs_8_ = f32[4,3,320,256]{3,2,1,0:T(8,128)} custom-call(s32[3]{0:T(128)S(1)} %pad_add_fusion.1.place, bf16[4,3,256,128]{3,2,1,0:T(8,128)(2,1)S(1)} %copy-done.5, bf16[4,3,256,128]{3,2,1,0:T(8,128)(2,1)S(1)} %copy-done.8, bf16[4,3,256,128]{3,2,1,0:T(8,128)(2,1)S(1)} %copy-done.11, bf16[4,3,256,128]{3,2,1,0:T(8,128)(2,1)S(1)} %copy-done.14, ...), custom_call_target="tpu_custom_call" | custom-call | flops 1 | bytes 1 | tf_op jit(solution)/shard_map/pallas_call | solution.py:308
  216.5 7.7 %shard_map.60 = (bf16[4,3,320,128]{3,2,1,0:T(8,128)(2,1)S(1)}, bf16[4,3,320,128]{3,2,1,0:T(8,128)(2,1)S(1)}) custom-call(s32[3]{0:T(128)S(1)} %pad_add_fusion.1.place, bf16[4,2,256,128]{3,2,1,0:T(8,128)(2,1)S(1)} %shard_map.58.refs_0_.refs_4_, bf16[4,2,256,128]{3,2,1,0:T(8,128)(2,1)S(1)} %collective-permute-done.13.refs_1_.refs_5_, ...), custom_call_target="tpu_custom_call" | custom-call | flops 1 | bytes 1 | tf_op jit(solution)/shard_map/pallas_call | solution.py:308
  224.3 0.8 copy-done.16
  225.1 2.6 collective-permute-done.16
  227.7 1.2 add_convert_fusion
  228.9 6.6 %collective-permute-done.17.refs_9_ = bf16[320,2560]{1,0:T(8,128)(2,1)} collective-permute-done((bf16[320,2560]{1,0:T(8,128)(2,1)}, bf16[320,2560]{1,0:T(8,128)(2,1)}, u32[]{:S(2)}, u32[]{:S(2)}) %collective-permute-start.17) | collective-permute-done | bytes 1638432 | tf_op jit(solution)/shard_map/ppermute | solution.py:120
  235.5 4.2 %all-to-all-start.2 = ((bf16[4,3,320,128]{3,2,1,0:T(8,128)(2,1)}), bf16[4,3,320,128]{3,2,1,0:T(8,128)(2,1)}, u32[]{:S(2)}, u32[]{:S(2)}) async-start(bf16[4,3,320,128]{3,2,1,0:T(8,128)(2,1)} %add_convert_fusion), calls=%async_computation.2 | async-start | bytes 1966080 | tf_op jit(solution)/shard_map/all_to_all | solution.py:124
  239.8 1.0 copy-done.17
  240.8 1.0 copy-done.19
  241.9 1.0 copy-done.21
  242.9 6.3 %shard_map.61 = (bf16[4,1,320,128]{3,2,1,0:T(8,128)(2,1)S(1)}, bf16[4,1,320,128]{3,2,1,0:T(8,128)(2,1)}) custom-call(s32[3]{0:T(128)S(1)} %pad_add_fusion.1.place, bf16[4,3,256,128]{3,2,1,0:T(8,128)(2,1)S(1)} %copy-done.6, bf16[4,3,256,128]{3,2,1,0:T(8,128)(2,1)S(1)} %copy-done.9, bf16[4,3,256,128]{3,2,1,0:T(8,128)(2,1)S(1)} %copy-done.12, ...), custom_call_target="tpu_custom_call" | custom-call | flops 10000000000 | bytes 16777216 | tf_op jit(solution)/shard_map/pallas_call | solution.py:308
  249.3 1.8 collective-permute-done.18
  251.2 2.9 %collective-permute-start.19 = (bf16[1,320,128]{2,1,0:T(8,128)(2,1)S(1)}, bf16[1,320,128]{2,1,0:T(8,128)(2,1)S(1)}, u32[]{:S(2)}, u32[]{:S(2)}) collective-permute-start(bf16[1,320,128]{2,1,0:T(8,128)(2,1)S(1)} %get-tuple-element.114), channel_id=1, source_target_pairs={{0,6},{2,4},{4,2},{6,0},{8,14},{10,12},{12,10},{14,8},{16,22},{18,... | collective-permute-start | bytes 245768 | tf_op jit(solution)/shard_map/ppermute | solution.py:120
  254.2 0.6 collective-permute-start.20
  254.8 1.2 fusion.1
  257.0 1.7 collective-permute-done.20
  258.7 0.5 collective-permute-done.21
  259.4 0.8 constant_dynamic-update-slice_fusion
  (87 shorter events, 3.2 us)
Async XLA Ops:
  0.0 1.3 copy-start.1
  1.3 1.3 copy-start.2
  4.6 5.4 %copy-start = (bf16[320,2560]{1,0:T(8,128)(2,1)S(1)}, bf16[320,2560]{1,0:T(8,128)(2,1)}, u32[]{:S(2)}) copy-start(bf16[320,2560]{1,0:T(8,128)(2,1)} %refs_4_.3) | copy-start | bytes 4915204
  4.6 48.6 %copy-start.3 = (bf16[256,2560]{1,0:T(8,128)(2,1)S(1)}, bf16[256,2560]{1,0:T(8,128)(2,1)}, u32[]{:S(2)}) copy-start(bf16[256,2560]{1,0:T(8,128)(2,1)} %refs_0_.2) | copy-start | bytes 3932164
  4.6 45.0 %all-to-all-start = ((bf16[4,5,2,256,128]{4,3,2,1,0:T(8,128)(2,1)}), bf16[4,5,2,256,128]{4,3,2,1,0:T(8,128)(2,1)}, u32[]{:S(2)}, u32[]{:S(2)}) async-start(bf16[4,5,2,256,128]{4,3,2,1,0:T(8,128)(2,1)} %shard_map.55), calls=%async_computation | async-start | bytes 5242880 | tf_op jit(solution)/shard_map/all_to_all | solution.py:124
  10.0 38.3 %collective-permute-start = (bf16[320,2560]{1,0:T(8,128)(2,1)S(1)}, bf16[320,2560]{1,0:T(8,128)(2,1)S(1)}, u32[]{:S(2)}, u32[]{:S(2)}) collective-permute-start(bf16[320,2560]{1,0:T(8,128)(2,1)S(1)} %copy-done), channel_id=1, source_target_pairs={{0,8},{2,10},{4,12},{6,14},{8,0},{10,2},{12,4},{14,6},{16,24},{18,... | collective-permute-start | bytes 4915208 | tf_op jit(solution)/shard_map/ppermute | solution.py:120
  12.5 37.1 %collective-permute-start.1 = (bf16[320,2560]{1,0:T(8,128)(2,1)S(1)}, bf16[320,2560]{1,0:T(8,128)(2,1)}, u32[]{:S(2)}, u32[]{:S(2)}) collective-permute-start(bf16[320,2560]{1,0:T(8,128)(2,1)S(1)} %copy-done), channel_id=1, source_target_pairs={{8,16},{10,18},{12,20},{14,22},{16,8},{18,10},{20,12},{22,14},{9,1... | collective-permute-start | bytes 4915208 | tf_op jit(solution)/shard_map/ppermute | solution.py:120
  48.3 1.3 copy-start.26
  49.6 60.2 %collective-permute-start.2 = (bf16[4,5,2,256,128]{4,3,2,1,0:T(8,128)(2,1)}, bf16[4,5,2,256,128]{4,3,2,1,0:T(8,128)(2,1)}, u32[]{:S(2)}, u32[]{:S(2)}) collective-permute-start(bf16[4,5,2,256,128]{4,3,2,1,0:T(8,128)(2,1)} %all-to-all-done.own), channel_id=1, source_target_pairs={{0,8},{2,10},{4,12},{6,14},{8,16},{10,18},{12,20},{14,22},{16,24},... | collective-permute-start | bytes 7864328 | tf_op jit(solution)/shard_map/ppermute | solution.py:120
  54.5 3.9 %copy-start.30 = (s32[20,2,8,2]{0,3,2,1:T(2,128)S(1)}, s32[20,2,8,2]{0,3,2,1:T(2,128)}, u32[]{:S(2)}) copy-start(s32[20,2,8,2]{0,3,2,1:T(2,128)} %param.8) | copy-start | bytes 7684
  54.5 25.2 %all-to-all-start.1 = ((bf16[4,5,1,256,128]{4,3,2,1,0:T(8,128)(2,1)}), bf16[4,5,1,256,128]{4,3,2,1,0:T(8,128)(2,1)S(1)}, u32[]{:S(2)}, u32[]{:S(2)}) async-start(bf16[4,5,1,256,128]{4,3,2,1,0:T(8,128)(2,1)} %shard_map.56), calls=%async_computation.1 | async-start | bytes 2621440 | tf_op jit(solution)/shard_map/all_to_all | solution.py:124
  58.5 16.4 %collective-permute-start.3 = (s32[5,2,8,2]{2,3,1,0:T(2,128)S(1)}, s32[5,2,8,2]{2,3,1,0:T(2,128)S(1)}, u32[]{:S(2)}, u32[]{:S(2)}) collective-permute-start(s32[5,2,8,2]{2,3,1,0:T(2,128)S(1)} %get-tuple-element.123), channel_id=1, source_target_pairs={{0,6},{2,4},{4,2},{6,0},{8,14},{10,12},{12,10},{14,8},{16,22},{18,... | collective-permute-start | bytes 1928 | tf_op jit(solution)/shard_map/ppermute | solution.py:120
  61.5 13.4 %collective-permute-start.4 = (s32[5,2,8,2]{2,3,1,0:T(2,128)S(1)}, s32[5,2,8,2]{2,3,1,0:T(2,128)S(1)}, u32[]{:S(2)}, u32[]{:S(2)}) collective-permute-start(s32[5,2,8,2]{2,3,1,0:T(2,128)S(1)} %get-tuple-element.122), channel_id=1, source_target_pairs={{0,4},{2,6},{4,0},{6,2},{8,12},{10,14},{12,8},{14,10},{16,20},{18,... | collective-permute-start | bytes 1928 | tf_op jit(solution)/shard_map/ppermute | solution.py:120
  62.1 12.8 %collective-permute-start.5 = (s32[5,2,8,2]{2,3,1,0:T(2,128)S(1)}, s32[5,2,8,2]{2,3,1,0:T(2,128)S(1)}, u32[]{:S(2)}, u32[]{:S(2)}) collective-permute-start(s32[5,2,8,2]{2,3,1,0:T(2,128)S(1)} %get-tuple-element.121), channel_id=1, source_target_pairs={{0,2},{2,0},{4,6},{6,4},{8,10},{10,8},{12,14},{14,12},{16,18},{18,... | collective-permute-start | bytes 1928 | tf_op jit(solution)/shard_map/ppermute | solution.py:120
  77.5 61.7 %copy-start.22 = (f32[5,4,2,2048]{3,2,1,0:T(2,128)}, f32[5,4,2,2048]{3,2,1,0:T(2,128)S(1)}, u32[]{:S(2)}) copy-start(f32[5,4,2,2048]{3,2,1,0:T(2,128)S(1)} %select_n.175.bias_ref) | copy-start | bytes 983044
  79.6 59.6 %copy-start.24 = (bf16[5,4,2,2048]{3,2,1,0:T(2,128)(2,1)}, bf16[5,4,2,2048]{3,2,1,0:T(2,128)(2,1)S(1)}, u32[]{:S(2)}) copy-start(bf16[5,4,2,2048]{3,2,1,0:T(2,128)(2,1)S(1)} %convert_element_type.30.lin_ref) | copy-start | bytes 491524
  111.1 28.1 %collective-permute-start.6 = (bf16[3,3,2,256,128]{4,3,2,1,0:T(8,128)(2,1)S(1)}, bf16[3,3,2,256,128]{4,3,2,1,0:T(8,128)(2,1)S(1)}, u32[]{:S(2)}, u32[]{:S(2)}) collective-permute-start(bf16[3,3,2,256,128]{4,3,2,1,0:T(8,128)(2,1)S(1)} %slice.19), channel_id=1, source_target_pairs={{0,8},{2,10},{4,12},{6,14},{8,16},{10,18},{12,20},{14,22},{16,24},... | collective-permute-start | bytes 3538952 | tf_op jit(solution)/shard_map/ppermute | solution.py:120
  113.9 45.3 %copy-start.27 = (bf16[320,2560]{1,0:T(8,128)(2,1)S(1)}, bf16[320,2560]{1,0:T(8,128)(2,1)}, u32[]{:S(2)}) copy-start(bf16[320,2560]{1,0:T(8,128)(2,1)} %copy-done.26) | copy-start | bytes 4915204
  139.2 18.7 %collective-permute-start.7 = (bf16[3,2,2,256,128]{4,3,2,1,0:T(8,128)(2,1)S(1)}, bf16[3,2,2,256,128]{4,3,2,1,0:T(8,128)(2,1)S(1)}, u32[]{:S(2)}, u32[]{:S(2)}) collective-permute-start(bf16[3,2,2,256,128]{4,3,2,1,0:T(8,128)(2,1)S(1)} %slice.18), channel_id=1, source_target_pairs={{0,8},{2,10},{4,12},{6,14},{8,16},{10,18},{12,20},{14,22},{16,24},... | collective-permute-start | bytes 2359304 | tf_op jit(solution)/shard_map/ppermute | solution.py:120
  156.1 22.0 %copy-start.4 = (bf16[4,3,256,128]{3,2,1,0:T(8,128)(2,1)}, bf16[4,3,256,128]{3,2,1,0:T(8,128)(2,1)S(1)}, u32[]{:S(2)}) copy-start(bf16[4,3,256,128]{3,2,1,0:T(8,128)(2,1)S(1)} %shard_map.57.refs_0_) | copy-start | bytes 2359300
  157.9 37.8 %collective-permute-start.8 = (bf16[320,2560]{1,0:T(8,128)(2,1)}, bf16[320,2560]{1,0:T(8,128)(2,1)S(1)}, u32[]{:S(2)}, u32[]{:S(2)}) collective-permute-start(bf16[320,2560]{1,0:T(8,128)(2,1)} %collective-permute-done.1.refs_6_), channel_id=1, source_target_pairs={{8,0},{10,2},{12,4},{14,6},{16,24},{18,26},{20,28},{22,30},{9,1},{... | collective-permute-start | bytes 4915208 | tf_op jit(solution)/shard_map/ppermute | solution.py:120
  159.2 36.5 %collective-permute-start.9 = (bf16[320,2560]{1,0:T(8,128)(2,1)S(1)}, bf16[320,2560]{1,0:T(8,128)(2,1)}, u32[]{:S(2)}, u32[]{:S(2)}) collective-permute-start(bf16[320,2560]{1,0:T(8,128)(2,1)S(1)} %copy-done.27), channel_id=1, source_target_pairs={{8,16},{10,18},{12,20},{14,22},{16,8},{18,10},{20,12},{22,14},{9,1... | collective-permute-start | bytes 4915208 | tf_op jit(solution)/shard_map/ppermute | solution.py:120
  161.0 20.5 %collective-permute-start.10 = (bf16[4,3,256,128]{3,2,1,0:T(8,128)(2,1)S(1)}, bf16[4,3,256,128]{3,2,1,0:T(8,128)(2,1)S(1)}, u32[]{:S(2)}, u32[]{:S(2)}) collective-permute-start(bf16[4,3,256,128]{3,2,1,0:T(8,128)(2,1)S(1)} %shard_map.57.refs_0_), channel_id=1, source_target_pairs={{0,2},{2,0},{4,6},{6,4},{8,10},{10,8},{12,14},{14,12},{16,18},{18,... | collective-permute-start | bytes 2359304 | tf_op jit(solution)/shard_map/ppermute | solution.py:120
  161.7 32.2 %collective-permute-start.11 = (bf16[4,3,256,128]{3,2,1,0:T(8,128)(2,1)S(1)}, bf16[4,3,256,128]{3,2,1,0:T(8,128)(2,1)S(1)}, u32[]{:S(2)}, u32[]{:S(2)}) collective-permute-start(bf16[4,3,256,128]{3,2,1,0:T(8,128)(2,1)S(1)} %shard_map.57.refs_0_), channel_id=1, source_target_pairs={{0,4},{2,6},{4,0},{6,2},{8,12},{10,14},{12,8},{14,10},{16,20},{18,... | collective-permute-start | bytes 2359304 | tf_op jit(solution)/shard_map/ppermute | solution.py:120
  163.2 31.6 %collective-permute-start.12 = (bf16[4,3,256,128]{3,2,1,0:T(8,128)(2,1)S(1)}, bf16[4,3,256,128]{3,2,1,0:T(8,128)(2,1)S(1)}, u32[]{:S(2)}, u32[]{:S(2)}) collective-permute-start(bf16[4,3,256,128]{3,2,1,0:T(8,128)(2,1)S(1)} %shard_map.57.refs_0_), channel_id=1, source_target_pairs={{0,6},{2,4},{4,2},{6,0},{8,14},{10,12},{12,10},{14,8},{16,22},{18,... | collective-permute-start | bytes 2359304 | tf_op jit(solution)/shard_map/ppermute | solution.py:120
  164.5 1.0 copy-start.23
  165.5 0.9 copy-start.25
  181.5 0.9 copy-start.7
  193.9 0.9 copy-start.10
  194.8 0.9 copy-start.13
  195.7 1.3 copy-start.28
  195.7 20.2 %collective-permute-start.13 = (bf16[4,2,256,128]{3,2,1,0:T(8,128)(2,1)S(1)}, bf16[4,2,256,128]{3,2,1,0:T(8,128)(2,1)S(1)}, u32[]{:S(2)}, u32[]{:S(2)}) collective-permute-start(bf16[4,2,256,128]{3,2,1,0:T(8,128)(2,1)S(1)} %shard_map.58.refs_0_.refs_4_), channel_id=1, source_target_pairs={{0,2},{2,0},{4,6},{6,4},{8,10},{10,8},{12,14},{14,12},{16,18},{18,... | collective-permute-start | bytes 1572872 | tf_op jit(solution)/shard_map/ppermute | solution.py:120
  197.0 19.1 %collective-permute-start.14 = (bf16[4,2,256,128]{3,2,1,0:T(8,128)(2,1)S(1)}, bf16[4,2,256,128]{3,2,1,0:T(8,128)(2,1)S(1)}, u32[]{:S(2)}, u32[]{:S(2)}) collective-permute-start(bf16[4,2,256,128]{3,2,1,0:T(8,128)(2,1)S(1)} %shard_map.58.refs_0_.refs_4_), channel_id=1, source_target_pairs={{0,4},{2,6},{4,0},{6,2},{8,12},{10,14},{12,8},{14,10},{16,20},{18,... | collective-permute-start | bytes 1572872 | tf_op jit(solution)/shard_map/ppermute | solution.py:120
  198.8 17.8 %collective-permute-start.15 = (bf16[4,2,256,128]{3,2,1,0:T(8,128)(2,1)S(1)}, bf16[4,2,256,128]{3,2,1,0:T(8,128)(2,1)}, u32[]{:S(2)}, u32[]{:S(2)}) collective-permute-start(bf16[4,2,256,128]{3,2,1,0:T(8,128)(2,1)S(1)} %shard_map.58.refs_0_.refs_4_), channel_id=1, source_target_pairs={{0,6},{2,4},{4,2},{6,0},{8,14},{10,12},{12,10},{14,8},{16,22},{18,... | collective-permute-start | bytes 1572872 | tf_op jit(solution)/shard_map/ppermute | solution.py:120
  199.6 35.9 %collective-permute-start.17 = (bf16[320,2560]{1,0:T(8,128)(2,1)}, bf16[320,2560]{1,0:T(8,128)(2,1)}, u32[]{:S(2)}, u32[]{:S(2)}) collective-permute-start(bf16[320,2560]{1,0:T(8,128)(2,1)} %collective-permute-done.9.refs_8_), channel_id=1, source_target_pairs={{8,0},{10,2},{12,4},{14,6},{16,24},{18,26},{20,28},{22,30},{9,1},{... | collective-permute-start | bytes 4915208 | tf_op jit(solution)/shard_map/ppermute | solution.py:120
  201.2 1.1 copy-start.5
  202.3 1.1 copy-start.8
  203.5 1.1 copy-start.11
  204.6 1.1 copy-start.14
  215.9 8.3 %copy-start.18 = (bf16[4,2,256,128]{3,2,1,0:T(8,128)(2,1)}, bf16[4,2,256,128]{3,2,1,0:T(8,128)(2,1)S(1)}, u32[]{:S(2)}) copy-start(bf16[4,2,256,128]{3,2,1,0:T(8,128)(2,1)S(1)} %collective-permute-done.13.refs_1_.refs_5_) | copy-start | bytes 1572868
  216.1 8.2 %copy-start.20 = (bf16[4,2,256,128]{3,2,1,0:T(8,128)(2,1)}, bf16[4,2,256,128]{3,2,1,0:T(8,128)(2,1)S(1)}, u32[]{:S(2)}) copy-start(bf16[4,2,256,128]{3,2,1,0:T(8,128)(2,1)S(1)} %collective-permute-done.14.refs_2_.refs_6_) | copy-start | bytes 1572868
  224.3 0.8 copy-start.16
  225.1 2.6 collective-permute-start.16
  227.7 12.1 %copy-start.12 = (bf16[4,3,256,128]{3,2,1,0:T(8,128)(2,1)S(1)}, bf16[4,3,256,128]{3,2,1,0:T(8,128)(2,1)}, u32[]{:S(2)}) copy-start(bf16[4,3,256,128]{3,2,1,0:T(8,128)(2,1)} %copy-done.10) | copy-start | bytes 2359300
  227.7 12.1 %copy-start.15 = (bf16[4,3,256,128]{3,2,1,0:T(8,128)(2,1)S(1)}, bf16[4,3,256,128]{3,2,1,0:T(8,128)(2,1)}, u32[]{:S(2)}) copy-start(bf16[4,3,256,128]{3,2,1,0:T(8,128)(2,1)} %copy-done.13) | copy-start | bytes 2359300
  228.9 10.8 %copy-start.6 = (bf16[4,3,256,128]{3,2,1,0:T(8,128)(2,1)S(1)}, bf16[4,3,256,128]{3,2,1,0:T(8,128)(2,1)}, u32[]{:S(2)}) copy-start(bf16[4,3,256,128]{3,2,1,0:T(8,128)(2,1)} %copy-done.4) | copy-start | bytes 2359300
  228.9 10.9 %copy-start.9 = (bf16[4,3,256,128]{3,2,1,0:T(8,128)(2,1)S(1)}, bf16[4,3,256,128]{3,2,1,0:T(8,128)(2,1)}, u32[]{:S(2)}) copy-start(bf16[4,3,256,128]{3,2,1,0:T(8,128)(2,1)} %copy-done.7) | copy-start | bytes 2359300
  235.5 15.7 %all-to-all-start.2 = ((bf16[4,3,320,128]{3,2,1,0:T(8,128)(2,1)}), bf16[4,3,320,128]{3,2,1,0:T(8,128)(2,1)}, u32[]{:S(2)}, u32[]{:S(2)}) async-start(bf16[4,3,320,128]{3,2,1,0:T(8,128)(2,1)} %add_convert_fusion), calls=%async_computation.2 | async-start | bytes 1966080 | tf_op jit(solution)/shard_map/all_to_all | solution.py:124
  239.8 1.0 copy-start.17
  240.8 1.0 copy-start.19
  241.9 1.0 copy-start.21
  249.3 1.8 collective-permute-start.18
  251.2 5.8 %collective-permute-start.19 = (bf16[1,320,128]{2,1,0:T(8,128)(2,1)S(1)}, bf16[1,320,128]{2,1,0:T(8,128)(2,1)S(1)}, u32[]{:S(2)}, u32[]{:S(2)}) collective-permute-start(bf16[1,320,128]{2,1,0:T(8,128)(2,1)S(1)} %get-tuple-element.114), channel_id=1, source_target_pairs={{0,6},{2,4},{4,2},{6,0},{8,14},{10,12},{12,10},{14,8},{16,22},{18,... | collective-permute-start | bytes 245768 | tf_op jit(solution)/shard_map/ppermute | solution.py:120
  254.2 4.5 %collective-permute-start.20 = (bf16[1,320,128]{2,1,0:T(8,128)(2,1)S(1)}, bf16[1,320,128]{2,1,0:T(8,128)(2,1)S(1)}, u32[]{:S(2)}, u32[]{:S(2)}) collective-permute-start(bf16[1,320,128]{2,1,0:T(8,128)(2,1)S(1)} %get-tuple-element.113), channel_id=1, source_target_pairs={{0,4},{2,6},{4,0},{6,2},{8,12},{10,14},{12,8},{14,10},{16,20},{18,... | collective-permute-start | bytes 245768 | tf_op jit(solution)/shard_map/ppermute | solution.py:120
  254.7 4.4 %collective-permute-start.21 = (bf16[1,320,128]{2,1,0:T(8,128)(2,1)S(1)}, bf16[1,320,128]{2,1,0:T(8,128)(2,1)S(1)}, u32[]{:S(2)}, u32[]{:S(2)}) collective-permute-start(bf16[1,320,128]{2,1,0:T(8,128)(2,1)S(1)} %get-tuple-element.112), channel_id=1, source_target_pairs={{0,2},{2,0},{4,6},{6,4},{8,10},{10,8},{12,14},{14,12},{16,18},{18,... | collective-permute-start | bytes 245768 | tf_op jit(solution)/shard_map/ppermute | solution.py:120
  256.8 2.6 copy-start.29

commit v5 on v4

--- a/solution.py
+++ b/solution.py
@@ -402,7 +402,6 @@
     pieces = [(out_weight,), (weight_pair,), (weight_mid, weight_end)]
     (so_far,) = project(place, group, spans[:1], gathered[:PLANE], pieces, ends=False)
     mine, theirs = project(place, group, spans[1:], gathered[PLANE:], pieces, so_far)
-    mine, theirs, *gathered = together(mine, theirs, *gathered)
 
     both, weight_mid2, weight_end2 = together(summed(mine, theirs), weight_mid2, weight_end2)
     arrived = exchange(both)

time: 261 us -> 261 us (level)
  no operation moved by 1% of the time
where the time goes in v5:
time: 261 us; the launch traced here: 260 us
  waiting for transfers between devices  133 us (51%)
  Pallas kernels  55.9 us (21%)
  starting transfers between devices  42.2 us (16%)
  local copies, waits for them, and re-layouts  27.2 us (10%)
    ppermute x20, waiting for transfers between devices, send(): return lax.ppermute(value, 'seq', pairs)  128 us
    ppermute x20, starting transfers between devices, send(): return lax.ppermute(value, 'seq', pairs)  28.6 us
    pallas_call x2, Pallas kernels, attention(): pl.pallas_call(functools.partial(attention_kernel, tok), grid=(count,), o...  28.5 us
    pallas_call x3, Pallas kernels, project(): pl.pallas_call(functools.partial(project_kernel, tok, group, spans, tuple...  24.3 us
    unnamed x62, local copies, waits for them, and re-layouts  17 us
    all_to_all x3, starting transfers between devices, exchange(): lax.all_to_all(value, 'seq', 0, 0, tiled=True, axis_index_groups=PLANES)  13.6 us
  transfers between devices with their start and end apart: 25, of which 15 were waited for; matrix products, arithmetic and copies ran while one was open for 4% of the time, Pallas kernels for 21%

profile of v5, /device:TPU:0, one launch (start us, length us, event | category | flops | bytes accessed | tf_op | source)
XLA Modules:
  0.0 260.2 jit_solution(806974969320648754)
XLA Ops:
  0.0 1.3 copy-done.1
  1.3 1.3 copy-done.2
  2.6 1.9 shard_map.55
  4.6 5.4 %all-to-all-start = ((bf16[4,5,2,256,128]{4,3,2,1,0:T(8,128)(2,1)}), bf16[4,5,2,256,128]{4,3,2,1,0:T(8,128)(2,1)}, u32[]{:S(2)}, u32[]{:S(2)}) async-start(bf16[4,5,2,256,128]{4,3,2,1,0:T(8,128)(2,1)} %shard_map.55), calls=%async_computation | async-start | bytes 5242880 | tf_op jit(solution)/shard_map/all_to_all | solution.py:124
  10.0 2.5 collective-permute-start
  12.5 1.8 collective-permute-start.1
  14.3 34.0 %collective-permute-done.refs_5_ = bf16[320,2560]{1,0:T(8,128)(2,1)S(1)} collective-permute-done((bf16[320,2560]{1,0:T(8,128)(2,1)S(1)}, bf16[320,2560]{1,0:T(8,128)(2,1)S(1)}, u32[]{:S(2)}, u32[]{:S(2)}) %collective-permute-start) | collective-permute-done | bytes 1638432 | tf_op jit(solution)/shard_map/ppermute | solution.py:120
  48.3 1.3 copy-done.26
  49.6 3.6 %collective-permute-start.2 = (bf16[4,5,2,256,128]{4,3,2,1,0:T(8,128)(2,1)}, bf16[4,5,2,256,128]{4,3,2,1,0:T(8,128)(2,1)}, u32[]{:S(2)}, u32[]{:S(2)}) collective-permute-start(bf16[4,5,2,256,128]{4,3,2,1,0:T(8,128)(2,1)} %all-to-all-done.own), channel_id=1, source_target_pairs={{0,8},{2,10},{4,12},{6,14},{8,16},{10,18},{12,20},{14,22},{16,24},... | collective-permute-start | bytes 7864328 | tf_op jit(solution)/shard_map/ppermute | solution.py:120
  53.2 1.3 shard_map.56
  54.5 3.9 %all-to-all-start.1 = ((bf16[4,5,1,256,128]{4,3,2,1,0:T(8,128)(2,1)}), bf16[4,5,1,256,128]{4,3,2,1,0:T(8,128)(2,1)S(1)}, u32[]{:S(2)}, u32[]{:S(2)}) async-start(bf16[4,5,1,256,128]{4,3,2,1,0:T(8,128)(2,1)} %shard_map.56), calls=%async_computation.1 | async-start | bytes 2621440 | tf_op jit(solution)/shard_map/all_to_all | solution.py:124
  58.5 3.0 %collective-permute-start.3 = (s32[5,2,8,2]{2,3,1,0:T(2,128)S(1)}, s32[5,2,8,2]{2,3,1,0:T(2,128)S(1)}, u32[]{:S(2)}, u32[]{:S(2)}) collective-permute-start(s32[5,2,8,2]{2,3,1,0:T(2,128)S(1)} %get-tuple-element.103), channel_id=1, source_target_pairs={{0,6},{2,4},{4,2},{6,0},{8,14},{10,12},{12,10},{14,8},{16,22},{18,... | collective-permute-start | bytes 1928 | tf_op jit(solution)/shard_map/ppermute | solution.py:120
  61.5 0.6 collective-permute-start.4
  62.2 12.8 %collective-permute-done.3 = s32[5,2,8,2]{2,3,1,0:T(2,128)S(1)} collective-permute-done((s32[5,2,8,2]{2,3,1,0:T(2,128)S(1)}, s32[5,2,8,2]{2,3,1,0:T(2,128)S(1)}, u32[]{:S(2)}, u32[]{:S(2)}) %collective-permute-start.3) | collective-permute-done | bytes 672 | tf_op jit(solution)/shard_map/ppermute | solution.py:120
  75.5 0.9 broadcast_in_dim.25
  76.4 1.1 select_n.175.bias_ref
  77.8 0.8 broadcast_in_dim.27
  78.7 1.0 convert_element_type.30.lin_ref
  79.6 30.1 %collective-permute-done.2.last = bf16[4,5,2,256,128]{4,3,2,1,0:T(8,128)(2,1)} collective-permute-done((bf16[4,5,2,256,128]{4,3,2,1,0:T(8,128)(2,1)}, bf16[4,5,2,256,128]{4,3,2,1,0:T(8,128)(2,1)}, u32[]{:S(2)}, u32[]{:S(2)}) %collective-permute-start.2) | collective-permute-done | bytes 2621472 | tf_op jit(solution)/shard_map/ppermute | solution.py:120
  109.8 1.4 slice.19
  111.1 1.5 collective-permute-start.6
  112.7 1.2 slice.18
  113.9 25.4 %collective-permute-done.6.last2 = bf16[3,3,2,256,128]{4,3,2,1,0:T(8,128)(2,1)S(1)} collective-permute-done((bf16[3,3,2,256,128]{4,3,2,1,0:T(8,128)(2,1)S(1)}, bf16[3,3,2,256,128]{4,3,2,1,0:T(8,128)(2,1)S(1)}, u32[]{:S(2)}, u32[]{:S(2)}) %collective-permute-start.6) | collective-permute-done | bytes 1179680 | tf_op jit(solution)/shard_map/ppermute | solution.py:120
  139.2 16.8 %shard_map.57.refs_0_ = bf16[4,3,256,128]{3,2,1,0:T(8,128)(2,1)S(1)} custom-call(bf16[4,5,1,256,128]{4,3,2,1,0:T(8,128)(2,1)S(1)} %all-to-all-done.1.q_ref, bf16[4,5,2,256,128]{4,3,2,1,0:T(8,128)(2,1)} %all-to-all-done.own, bf16[4,5,2,256,128]{4,3,2,1,0:T(8,128)(2,1)} %collective-permute-done.2.last, ...), custom_call_target="tpu_custom_call" | custom-call | flops 6442450944 | bytes 8650752 | tf_op jit(solution)/shard_map/pallas_call | solution.py:226
  156.1 1.8 collective-permute-done.7.last2
  157.9 1.3 collective-permute-start.8
  159.2 1.8 collective-permute-start.9
  161.0 0.7 collective-permute-start.10
  161.7 1.5 collective-permute-start.11
  163.2 1.3 collective-permute-start.12
  164.5 1.0 copy-done.23
  165.5 0.9 copy-done.25
  166.4 11.6 %shard_map.58.refs_0_.refs_4_ = bf16[4,2,256,128]{3,2,1,0:T(8,128)(2,1)S(1)} custom-call(bf16[4,5,1,256,128]{4,3,2,1,0:T(8,128)(2,1)S(1)} %all-to-all-done.1.q_ref, bf16[4,5,2,256,128]{4,3,2,1,0:T(8,128)(2,1)} %all-to-all-done.own, bf16[4,5,2,256,128]{4,3,2,1,0:T(8,128)(2,1)} %collective-permute-done.2.last, ...), custom_call_target="tpu_custom_call" | custom-call | flops 4294967296 | bytes 5767168 | tf_op jit(solution)/shard_map/pallas_call | solution.py:226
  178.1 3.5 %collective-permute-done.10.refs_1_ = bf16[4,3,256,128]{3,2,1,0:T(8,128)(2,1)S(1)} collective-permute-done((bf16[4,3,256,128]{3,2,1,0:T(8,128)(2,1)S(1)}, bf16[4,3,256,128]{3,2,1,0:T(8,128)(2,1)S(1)}, u32[]{:S(2)}, u32[]{:S(2)}) %collective-permute-start.10) | collective-permute-done | bytes 786464 | tf_op jit(solution)/shard_map/ppermute | solution.py:120
  181.5 0.9 copy-done.7
  182.4 11.5 %collective-permute-done.11.refs_2_ = bf16[4,3,256,128]{3,2,1,0:T(8,128)(2,1)S(1)} collective-permute-done((bf16[4,3,256,128]{3,2,1,0:T(8,128)(2,1)S(1)}, bf16[4,3,256,128]{3,2,1,0:T(8,128)(2,1)S(1)}, u32[]{:S(2)}, u32[]{:S(2)}) %collective-permute-start.11) | collective-permute-done | bytes 786464 | tf_op jit(solution)/shard_map/ppermute | solution.py:120
  193.9 0.9 copy-done.10
  194.8 0.9 copy-done.13
  195.7 1.3 collective-permute-start.13
  197.0 1.7 collective-permute-start.14
  198.8 0.9 collective-permute-start.15
  199.6 1.5 collective-permute-start.17
  201.2 1.1 copy-done.5
  202.3 1.1 copy-done.8
  203.5 1.1 copy-done.11
  204.6 1.1 copy-done.14
  205.7 10.2 %shard_map.59.refs_8_ = f32[4,3,320,256]{3,2,1,0:T(8,128)} custom-call(s32[3]{0:T(128)S(1)} %pad_add_fusion.1.place, bf16[4,3,256,128]{3,2,1,0:T(8,128)(2,1)S(1)} %copy-done.5, bf16[4,3,256,128]{3,2,1,0:T(8,128)(2,1)S(1)} %copy-done.8, bf16[4,3,256,128]{3,2,1,0:T(8,128)(2,1)S(1)} %copy-done.11, bf16[4,3,256,128]{3,2,1,0:T(8,128)(2,1)S(1)} %copy-done.14, ...), custom_call_target="tpu_custom_call" | custom-call | flops 1 | bytes 1 | tf_op jit(solution)/shard_map/pallas_call | solution.py:308
  216.5 7.7 %shard_map.60 = (bf16[4,3,320,128]{3,2,1,0:T(8,128)(2,1)S(1)}, bf16[4,3,320,128]{3,2,1,0:T(8,128)(2,1)S(1)}) custom-call(s32[3]{0:T(128)S(1)} %pad_add_fusion.1.place, bf16[4,2,256,128]{3,2,1,0:T(8,128)(2,1)S(1)} %shard_map.58.refs_0_.refs_4_, bf16[4,2,256,128]{3,2,1,0:T(8,128)(2,1)S(1)} %collective-permute-done.13.refs_1_.refs_5_, ...), custom_call_target="tpu_custom_call" | custom-call | flops 1 | bytes 1 | tf_op jit(solution)/shard_map/pallas_call | solution.py:308
  224.3 0.8 copy-done.16
  225.1 2.6 collective-permute-done.16
  227.7 1.2 add_convert_fusion
  228.9 6.6 %collective-permute-done.17.refs_9_ = bf16[320,2560]{1,0:T(8,128)(2,1)} collective-permute-done((bf16[320,2560]{1,0:T(8,128)(2,1)}, bf16[320,2560]{1,0:T(8,128)(2,1)}, u32[]{:S(2)}, u32[]{:S(2)}) %collective-permute-start.17) | collective-permute-done | bytes 1638432 | tf_op jit(solution)/shard_map/ppermute | solution.py:120
  235.5 4.2 %all-to-all-start.2 = ((bf16[4,3,320,128]{3,2,1,0:T(8,128)(2,1)}), bf16[4,3,320,128]{3,2,1,0:T(8,128)(2,1)}, u32[]{:S(2)}, u32[]{:S(2)}) async-start(bf16[4,3,320,128]{3,2,1,0:T(8,128)(2,1)} %add_convert_fusion), calls=%async_computation.2 | async-start | bytes 1966080 | tf_op jit(solution)/shard_map/all_to_all | solution.py:124
  239.8 1.0 copy-done.17
  240.8 1.0 copy-done.19
  241.9 1.0 copy-done.21
  242.9 6.3 %shard_map.61 = (bf16[4,1,320,128]{3,2,1,0:T(8,128)(2,1)S(1)}, bf16[4,1,320,128]{3,2,1,0:T(8,128)(2,1)}) custom-call(s32[3]{0:T(128)S(1)} %pad_add_fusion.1.place, bf16[4,3,256,128]{3,2,1,0:T(8,128)(2,1)S(1)} %copy-done.6, bf16[4,3,256,128]{3,2,1,0:T(8,128)(2,1)S(1)} %copy-done.9, bf16[4,3,256,128]{3,2,1,0:T(8,128)(2,1)S(1)} %copy-done.12, ...), custom_call_target="tpu_custom_call" | custom-call | flops 10000000000 | bytes 16777216 | tf_op jit(solution)/shard_map/pallas_call | solution.py:308
  249.3 1.8 collective-permute-done.18
  251.2 2.9 %collective-permute-start.19 = (bf16[1,320,128]{2,1,0:T(8,128)(2,1)S(1)}, bf16[1,320,128]{2,1,0:T(8,128)(2,1)S(1)}, u32[]{:S(2)}, u32[]{:S(2)}) collective-permute-start(bf16[1,320,128]{2,1,0:T(8,128)(2,1)S(1)} %get-tuple-element.94), channel_id=1, source_target_pairs={{0,6},{2,4},{4,2},{6,0},{8,14},{10,12},{12,10},{14,8},{16,22},{18,... | collective-permute-start | bytes 245768 | tf_op jit(solution)/shard_map/ppermute | solution.py:120
  254.2 0.6 collective-permute-start.20
  254.8 1.2 fusion.1
  257.0 1.7 collective-permute-done.20
  258.7 0.5 collective-permute-done.21
  259.4 0.8 constant_dynamic-update-slice_fusion
  (87 shorter events, 3.2 us)
Async XLA Ops:
  0.0 1.3 copy-start.1
  1.3 1.3 copy-start.2
  4.6 5.4 %copy-start = (bf16[320,2560]{1,0:T(8,128)(2,1)S(1)}, bf16[320,2560]{1,0:T(8,128)(2,1)}, u32[]{:S(2)}) copy-start(bf16[320,2560]{1,0:T(8,128)(2,1)} %refs_4_.3) | copy-start | bytes 4915204
  4.6 48.6 %copy-start.3 = (bf16[256,2560]{1,0:T(8,128)(2,1)S(1)}, bf16[256,2560]{1,0:T(8,128)(2,1)}, u32[]{:S(2)}) copy-start(bf16[256,2560]{1,0:T(8,128)(2,1)} %refs_0_.2) | copy-start | bytes 3932164
  4.6 45.0 %all-to-all-start = ((bf16[4,5,2,256,128]{4,3,2,1,0:T(8,128)(2,1)}), bf16[4,5,2,256,128]{4,3,2,1,0:T(8,128)(2,1)}, u32[]{:S(2)}, u32[]{:S(2)}) async-start(bf16[4,5,2,256,128]{4,3,2,1,0:T(8,128)(2,1)} %shard_map.55), calls=%async_computation | async-start | bytes 5242880 | tf_op jit(solution)/shard_map/all_to_all | solution.py:124
  10.0 38.3 %collective-permute-start = (bf16[320,2560]{1,0:T(8,128)(2,1)S(1)}, bf16[320,2560]{1,0:T(8,128)(2,1)S(1)}, u32[]{:S(2)}, u32[]{:S(2)}) collective-permute-start(bf16[320,2560]{1,0:T(8,128)(2,1)S(1)} %copy-done), channel_id=1, source_target_pairs={{0,8},{2,10},{4,12},{6,14},{8,0},{10,2},{12,4},{14,6},{16,24},{18,... | collective-permute-start | bytes 4915208 | tf_op jit(solution)/shard_map/ppermute | solution.py:120
  12.5 37.1 %collective-permute-start.1 = (bf16[320,2560]{1,0:T(8,128)(2,1)S(1)}, bf16[320,2560]{1,0:T(8,128)(2,1)}, u32[]{:S(2)}, u32[]{:S(2)}) collective-permute-start(bf16[320,2560]{1,0:T(8,128)(2,1)S(1)} %copy-done), channel_id=1, source_target_pairs={{8,16},{10,18},{12,20},{14,22},{16,8},{18,10},{20,12},{22,14},{9,1... | collective-permute-start | bytes 4915208 | tf_op jit(solution)/shard_map/ppermute | solution.py:120
  48.3 1.3 copy-start.26
  49.6 60.2 %collective-permute-start.2 = (bf16[4,5,2,256,128]{4,3,2,1,0:T(8,128)(2,1)}, bf16[4,5,2,256,128]{4,3,2,1,0:T(8,128)(2,1)}, u32[]{:S(2)}, u32[]{:S(2)}) collective-permute-start(bf16[4,5,2,256,128]{4,3,2,1,0:T(8,128)(2,1)} %all-to-all-done.own), channel_id=1, source_target_pairs={{0,8},{2,10},{4,12},{6,14},{8,16},{10,18},{12,20},{14,22},{16,24},... | collective-permute-start | bytes 7864328 | tf_op jit(solution)/shard_map/ppermute | solution.py:120
  54.5 3.9 %copy-start.30 = (s32[20,2,8,2]{0,3,2,1:T(2,128)S(1)}, s32[20,2,8,2]{0,3,2,1:T(2,128)}, u32[]{:S(2)}) copy-start(s32[20,2,8,2]{0,3,2,1:T(2,128)} %param.8) | copy-start | bytes 7684
  54.5 25.2 %all-to-all-start.1 = ((bf16[4,5,1,256,128]{4,3,2,1,0:T(8,128)(2,1)}), bf16[4,5,1,256,128]{4,3,2,1,0:T(8,128)(2,1)S(1)}, u32[]{:S(2)}, u32[]{:S(2)}) async-start(bf16[4,5,1,256,128]{4,3,2,1,0:T(8,128)(2,1)} %shard_map.56), calls=%async_computation.1 | async-start | bytes 2621440 | tf_op jit(solution)/shard_map/all_to_all | solution.py:124
  58.5 16.4 %collective-permute-start.3 = (s32[5,2,8,2]{2,3,1,0:T(2,128)S(1)}, s32[5,2,8,2]{2,3,1,0:T(2,128)S(1)}, u32[]{:S(2)}, u32[]{:S(2)}) collective-permute-start(s32[5,2,8,2]{2,3,1,0:T(2,128)S(1)} %get-tuple-element.103), channel_id=1, source_target_pairs={{0,6},{2,4},{4,2},{6,0},{8,14},{10,12},{12,10},{14,8},{16,22},{18,... | collective-permute-start | bytes 1928 | tf_op jit(solution)/shard_map/ppermute | solution.py:120
  61.5 13.4 %collective-permute-start.4 = (s32[5,2,8,2]{2,3,1,0:T(2,128)S(1)}, s32[5,2,8,2]{2,3,1,0:T(2,128)S(1)}, u32[]{:S(2)}, u32[]{:S(2)}) collective-permute-start(s32[5,2,8,2]{2,3,1,0:T(2,128)S(1)} %get-tuple-element.102), channel_id=1, source_target_pairs={{0,4},{2,6},{4,0},{6,2},{8,12},{10,14},{12,8},{14,10},{16,20},{18,... | collective-permute-start | bytes 1928 | tf_op jit(solution)/shard_map/ppermute | solution.py:120
  62.1 12.8 %collective-permute-start.5 = (s32[5,2,8,2]{2,3,1,0:T(2,128)S(1)}, s32[5,2,8,2]{2,3,1,0:T(2,128)S(1)}, u32[]{:S(2)}, u32[]{:S(2)}) collective-permute-start(s32[5,2,8,2]{2,3,1,0:T(2,128)S(1)} %get-tuple-element.101), channel_id=1, source_target_pairs={{0,2},{2,0},{4,6},{6,4},{8,10},{10,8},{12,14},{14,12},{16,18},{18,... | collective-permute-start | bytes 1928 | tf_op jit(solution)/shard_map/ppermute | solution.py:120
  77.5 61.7 %copy-start.22 = (f32[5,4,2,2048]{3,2,1,0:T(2,128)}, f32[5,4,2,2048]{3,2,1,0:T(2,128)S(1)}, u32[]{:S(2)}) copy-start(f32[5,4,2,2048]{3,2,1,0:T(2,128)S(1)} %select_n.175.bias_ref) | copy-start | bytes 983044
  79.6 59.6 %copy-start.24 = (bf16[5,4,2,2048]{3,2,1,0:T(2,128)(2,1)}, bf16[5,4,2,2048]{3,2,1,0:T(2,128)(2,1)S(1)}, u32[]{:S(2)}) copy-start(bf16[5,4,2,2048]{3,2,1,0:T(2,128)(2,1)S(1)} %convert_element_type.30.lin_ref) | copy-start | bytes 491524
  111.1 28.1 %collective-permute-start.6 = (bf16[3,3,2,256,128]{4,3,2,1,0:T(8,128)(2,1)S(1)}, bf16[3,3,2,256,128]{4,3,2,1,0:T(8,128)(2,1)S(1)}, u32[]{:S(2)}, u32[]{:S(2)}) collective-permute-start(bf16[3,3,2,256,128]{4,3,2,1,0:T(8,128)(2,1)S(1)} %slice.19), channel_id=1, source_target_pairs={{0,8},{2,10},{4,12},{6,14},{8,16},{10,18},{12,20},{14,22},{16,24},... | collective-permute-start | bytes 3538952 | tf_op jit(solution)/shard_map/ppermute | solution.py:120
  113.9 45.3 %copy-start.27 = (bf16[320,2560]{1,0:T(8,128)(2,1)S(1)}, bf16[320,2560]{1,0:T(8,128)(2,1)}, u32[]{:S(2)}) copy-start(bf16[320,2560]{1,0:T(8,128)(2,1)} %copy-done.26) | copy-start | bytes 4915204
  139.2 18.7 %collective-permute-start.7 = (bf16[3,2,2,256,128]{4,3,2,1,0:T(8,128)(2,1)S(1)}, bf16[3,2,2,256,128]{4,3,2,1,0:T(8,128)(2,1)S(1)}, u32[]{:S(2)}, u32[]{:S(2)}) collective-permute-start(bf16[3,2,2,256,128]{4,3,2,1,0:T(8,128)(2,1)S(1)} %slice.18), channel_id=1, source_target_pairs={{0,8},{2,10},{4,12},{6,14},{8,16},{10,18},{12,20},{14,22},{16,24},... | collective-permute-start | bytes 2359304 | tf_op jit(solution)/shard_map/ppermute | solution.py:120
  156.1 22.0 %copy-start.4 = (bf16[4,3,256,128]{3,2,1,0:T(8,128)(2,1)}, bf16[4,3,256,128]{3,2,1,0:T(8,128)(2,1)S(1)}, u32[]{:S(2)}) copy-start(bf16[4,3,256,128]{3,2,1,0:T(8,128)(2,1)S(1)} %shard_map.57.refs_0_) | copy-start | bytes 2359300
  157.9 37.8 %collective-permute-start.8 = (bf16[320,2560]{1,0:T(8,128)(2,1)}, bf16[320,2560]{1,0:T(8,128)(2,1)S(1)}, u32[]{:S(2)}, u32[]{:S(2)}) collective-permute-start(bf16[320,2560]{1,0:T(8,128)(2,1)} %collective-permute-done.1.refs_6_), channel_id=1, source_target_pairs={{8,0},{10,2},{12,4},{14,6},{16,24},{18,26},{20,28},{22,30},{9,1},{... | collective-permute-start | bytes 4915208 | tf_op jit(solution)/shard_map/ppermute | solution.py:120
  159.2 36.5 %collective-permute-start.9 = (bf16[320,2560]{1,0:T(8,128)(2,1)S(1)}, bf16[320,2560]{1,0:T(8,128)(2,1)}, u32[]{:S(2)}, u32[]{:S(2)}) collective-permute-start(bf16[320,2560]{1,0:T(8,128)(2,1)S(1)} %copy-done.27), channel_id=1, source_target_pairs={{8,16},{10,18},{12,20},{14,22},{16,8},{18,10},{20,12},{22,14},{9,1... | collective-permute-start | bytes 4915208 | tf_op jit(solution)/shard_map/ppermute | solution.py:120
  161.0 20.5 %collective-permute-start.10 = (bf16[4,3,256,128]{3,2,1,0:T(8,128)(2,1)S(1)}, bf16[4,3,256,128]{3,2,1,0:T(8,128)(2,1)S(1)}, u32[]{:S(2)}, u32[]{:S(2)}) collective-permute-start(bf16[4,3,256,128]{3,2,1,0:T(8,128)(2,1)S(1)} %shard_map.57.refs_0_), channel_id=1, source_target_pairs={{0,2},{2,0},{4,6},{6,4},{8,10},{10,8},{12,14},{14,12},{16,18},{18,... | collective-permute-start | bytes 2359304 | tf_op jit(solution)/shard_map/ppermute | solution.py:120
  161.7 32.2 %collective-permute-start.11 = (bf16[4,3,256,128]{3,2,1,0:T(8,128)(2,1)S(1)}, bf16[4,3,256,128]{3,2,1,0:T(8,128)(2,1)S(1)}, u32[]{:S(2)}, u32[]{:S(2)}) collective-permute-start(bf16[4,3,256,128]{3,2,1,0:T(8,128)(2,1)S(1)} %shard_map.57.refs_0_), channel_id=1, source_target_pairs={{0,4},{2,6},{4,0},{6,2},{8,12},{10,14},{12,8},{14,10},{16,20},{18,... | collective-permute-start | bytes 2359304 | tf_op jit(solution)/shard_map/ppermute | solution.py:120
  163.2 31.6 %collective-permute-start.12 = (bf16[4,3,256,128]{3,2,1,0:T(8,128)(2,1)S(1)}, bf16[4,3,256,128]{3,2,1,0:T(8,128)(2,1)S(1)}, u32[]{:S(2)}, u32[]{:S(2)}) collective-permute-start(bf16[4,3,256,128]{3,2,1,0:T(8,128)(2,1)S(1)} %shard_map.57.refs_0_), channel_id=1, source_target_pairs={{0,6},{2,4},{4,2},{6,0},{8,14},{10,12},{12,10},{14,8},{16,22},{18,... | collective-permute-start | bytes 2359304 | tf_op jit(solution)/shard_map/ppermute | solution.py:120
  164.5 1.0 copy-start.23
  165.5 0.9 copy-start.25
  181.5 0.9 copy-start.7
  193.9 0.9 copy-start.10
  194.8 0.9 copy-start.13
  195.7 1.3 copy-start.28
  195.7 20.2 %collective-permute-start.13 = (bf16[4,2,256,128]{3,2,1,0:T(8,128)(2,1)S(1)}, bf16[4,2,256,128]{3,2,1,0:T(8,128)(2,1)S(1)}, u32[]{:S(2)}, u32[]{:S(2)}) collective-permute-start(bf16[4,2,256,128]{3,2,1,0:T(8,128)(2,1)S(1)} %shard_map.58.refs_0_.refs_4_), channel_id=1, source_target_pairs={{0,2},{2,0},{4,6},{6,4},{8,10},{10,8},{12,14},{14,12},{16,18},{18,... | collective-permute-start | bytes 1572872 | tf_op jit(solution)/shard_map/ppermute | solution.py:120
  197.0 19.1 %collective-permute-start.14 = (bf16[4,2,256,128]{3,2,1,0:T(8,128)(2,1)S(1)}, bf16[4,2,256,128]{3,2,1,0:T(8,128)(2,1)S(1)}, u32[]{:S(2)}, u32[]{:S(2)}) collective-permute-start(bf16[4,2,256,128]{3,2,1,0:T(8,128)(2,1)S(1)} %shard_map.58.refs_0_.refs_4_), channel_id=1, source_target_pairs={{0,4},{2,6},{4,0},{6,2},{8,12},{10,14},{12,8},{14,10},{16,20},{18,... | collective-permute-start | bytes 1572872 | tf_op jit(solution)/shard_map/ppermute | solution.py:120
  198.8 17.8 %collective-permute-start.15 = (bf16[4,2,256,128]{3,2,1,0:T(8,128)(2,1)S(1)}, bf16[4,2,256,128]{3,2,1,0:T(8,128)(2,1)}, u32[]{:S(2)}, u32[]{:S(2)}) collective-permute-start(bf16[4,2,256,128]{3,2,1,0:T(8,128)(2,1)S(1)} %shard_map.58.refs_0_.refs_4_), channel_id=1, source_target_pairs={{0,6},{2,4},{4,2},{6,0},{8,14},{10,12},{12,10},{14,8},{16,22},{18,... | collective-permute-start | bytes 1572872 | tf_op jit(solution)/shard_map/ppermute | solution.py:120
  199.6 35.9 %collective-permute-start.17 = (bf16[320,2560]{1,0:T(8,128)(2,1)}, bf16[320,2560]{1,0:T(8,128)(2,1)}, u32[]{:S(2)}, u32[]{:S(2)}) collective-permute-start(bf16[320,2560]{1,0:T(8,128)(2,1)} %collective-permute-done.9.refs_8_), channel_id=1, source_target_pairs={{8,0},{10,2},{12,4},{14,6},{16,24},{18,26},{20,28},{22,30},{9,1},{... | collective-permute-start | bytes 4915208 | tf_op jit(solution)/shard_map/ppermute | solution.py:120
  201.2 1.1 copy-start.5
  202.3 1.1 copy-start.8
  203.5 1.1 copy-start.11
  204.6 1.1 copy-start.14
  215.9 8.3 %copy-start.18 = (bf16[4,2,256,128]{3,2,1,0:T(8,128)(2,1)}, bf16[4,2,256,128]{3,2,1,0:T(8,128)(2,1)S(1)}, u32[]{:S(2)}) copy-start(bf16[4,2,256,128]{3,2,1,0:T(8,128)(2,1)S(1)} %collective-permute-done.13.refs_1_.refs_5_) | copy-start | bytes 1572868
  216.1 8.2 %copy-start.20 = (bf16[4,2,256,128]{3,2,1,0:T(8,128)(2,1)}, bf16[4,2,256,128]{3,2,1,0:T(8,128)(2,1)S(1)}, u32[]{:S(2)}) copy-start(bf16[4,2,256,128]{3,2,1,0:T(8,128)(2,1)S(1)} %collective-permute-done.14.refs_2_.refs_6_) | copy-start | bytes 1572868
  224.3 0.8 copy-start.16
  225.1 2.6 collective-permute-start.16
  227.7 12.1 %copy-start.12 = (bf16[4,3,256,128]{3,2,1,0:T(8,128)(2,1)S(1)}, bf16[4,3,256,128]{3,2,1,0:T(8,128)(2,1)}, u32[]{:S(2)}) copy-start(bf16[4,3,256,128]{3,2,1,0:T(8,128)(2,1)} %copy-done.10) | copy-start | bytes 2359300
  227.7 12.1 %copy-start.15 = (bf16[4,3,256,128]{3,2,1,0:T(8,128)(2,1)S(1)}, bf16[4,3,256,128]{3,2,1,0:T(8,128)(2,1)}, u32[]{:S(2)}) copy-start(bf16[4,3,256,128]{3,2,1,0:T(8,128)(2,1)} %copy-done.13) | copy-start | bytes 2359300
  228.9 10.8 %copy-start.6 = (bf16[4,3,256,128]{3,2,1,0:T(8,128)(2,1)S(1)}, bf16[4,3,256,128]{3,2,1,0:T(8,128)(2,1)}, u32[]{:S(2)}) copy-start(bf16[4,3,256,128]{3,2,1,0:T(8,128)(2,1)} %copy-done.4) | copy-start | bytes 2359300
  228.9 10.9 %copy-start.9 = (bf16[4,3,256,128]{3,2,1,0:T(8,128)(2,1)S(1)}, bf16[4,3,256,128]{3,2,1,0:T(8,128)(2,1)}, u32[]{:S(2)}) copy-start(bf16[4,3,256,128]{3,2,1,0:T(8,128)(2,1)} %copy-done.7) | copy-start | bytes 2359300
  235.5 15.7 %all-to-all-start.2 = ((bf16[4,3,320,128]{3,2,1,0:T(8,128)(2,1)}), bf16[4,3,320,128]{3,2,1,0:T(8,128)(2,1)}, u32[]{:S(2)}, u32[]{:S(2)}) async-start(bf16[4,3,320,128]{3,2,1,0:T(8,128)(2,1)} %add_convert_fusion), calls=%async_computation.2 | async-start | bytes 1966080 | tf_op jit(solution)/shard_map/all_to_all | solution.py:124
  239.8 1.0 copy-start.17
  240.8 1.0 copy-start.19
  241.9 1.0 copy-start.21
  249.3 1.8 collective-permute-start.18
  251.2 5.8 %collective-permute-start.19 = (bf16[1,320,128]{2,1,0:T(8,128)(2,1)S(1)}, bf16[1,320,128]{2,1,0:T(8,128)(2,1)S(1)}, u32[]{:S(2)}, u32[]{:S(2)}) collective-permute-start(bf16[1,320,128]{2,1,0:T(8,128)(2,1)S(1)} %get-tuple-element.94), channel_id=1, source_target_pairs={{0,6},{2,4},{4,2},{6,0},{8,14},{10,12},{12,10},{14,8},{16,22},{18,... | collective-permute-start | bytes 245768 | tf_op jit(solution)/shard_map/ppermute | solution.py:120
  254.2 4.5 %collective-permute-start.20 = (bf16[1,320,128]{2,1,0:T(8,128)(2,1)S(1)}, bf16[1,320,128]{2,1,0:T(8,128)(2,1)S(1)}, u32[]{:S(2)}, u32[]{:S(2)}) collective-permute-start(bf16[1,320,128]{2,1,0:T(8,128)(2,1)S(1)} %get-tuple-element.93), channel_id=1, source_target_pairs={{0,4},{2,6},{4,0},{6,2},{8,12},{10,14},{12,8},{14,10},{16,20},{18,... | collective-permute-start | bytes 245768 | tf_op jit(solution)/shard_map/ppermute | solution.py:120
  254.7 4.4 %collective-permute-start.21 = (bf16[1,320,128]{2,1,0:T(8,128)(2,1)S(1)}, bf16[1,320,128]{2,1,0:T(8,128)(2,1)S(1)}, u32[]{:S(2)}, u32[]{:S(2)}) collective-permute-start(bf16[1,320,128]{2,1,0:T(8,128)(2,1)S(1)} %get-tuple-element.92), channel_id=1, source_target_pairs={{0,2},{2,0},{4,6},{6,4},{8,10},{10,8},{12,14},{14,12},{16,18},{18,... | collective-permute-start | bytes 245768 | tf_op jit(solution)/shard_map/ppermute | solution.py:120
  256.8 2.6 copy-start.29
